TPU v7x, 32 devices: a whole 2x2x4 slice. The times are simulated.
32 devices in a mesh: blk: 8 (over z, y), sec: 4 (over x, core).
Axes of the slice: x: 2, y: 2, z: 4, core: 2. Of those that a mesh axis runs over, the one named last changes fastest.
Arguments:
- factors: bfloat16 [8, 512, 1024], P('blk', None, 'sec'), may hold values from -0.5 to 0.5
- occ_energy: float32 [8], replicated, may hold values from -2 to -0.5
- vir_energy: float32 [512], replicated, may hold values from 0.2 to 3
- metric: float32 [1024, 1024], replicated, may hold values from -0.1875 to 0.1875
Outputs:
- gamma: float32 [1024, 8, 512], P('sec', 'blk')
- density: float32 [512, 512], P('blk')
All inputs are finite; a program needn't handle non-finite values.
Results may differ from a plain program's by a relative error of at most 0.00077.
Values may be sent and summed in bfloat16 or wider, within the bound.
No kernel may reach another device: no remote copies, remote signals or barrier semaphores. Data moves between devices by JAX's collectives and lax.ppermute only.
A program may use at most 64 MiB of HBM per device.

v0:
```python
import jax
import jax.numpy as jnp
from jax import lax
from jax.sharding import PartitionSpec as P

CYCLE_STEPS = 4


def from_behind(shard, axis, by):
    devices = lax.axis_size(axis)
    return lax.ppermute(shard, axis, [(i, (i + by) % devices) for i in range(devices)])


def batch_energy(occ_energy, batch_index, per_batch):
    return lax.dynamic_slice_in_dim(occ_energy, batch_index * per_batch, per_batch, 0)


def pair_block(
    own_full, own_energy, partner, part_energy, vir_energy, acc_own, acc_part, density, weight
):
    per_batch = own_full.shape[0]

    def one_pair(pair_index, loop_state):
        acc_own, acc_part, density = loop_state
        first_pos = pair_index // per_batch
        second = pair_index % per_batch
        left_block = lax.dynamic_index_in_dim(own_full, first_pos, 0, keepdims=False)
        right_block = lax.dynamic_index_in_dim(partner, second, 0, keepdims=False)
        intersection = lax.dot_general(
            left_block, right_block, (((1,), (1,)), ((), ())), preferred_element_type=jnp.float32
        )
        energy_sum = lax.dynamic_index_in_dim(
            own_energy, first_pos, 0, keepdims=False
        ) + lax.dynamic_index_in_dim(part_energy, second, 0, keepdims=False)
        denominator = energy_sum - vir_energy[:, None] - vir_energy[None, :]
        amplitude = intersection / denominator
        mixed_amp = 2.0 * amplitude - amplitude.T
        amp_half = amplitude.astype(jnp.bfloat16)
        mixed_half = mixed_amp.astype(jnp.bfloat16)
        own_term = jnp.einsum(
            "bp,ab->pa", right_block, mixed_half, preferred_element_type=jnp.float32
        )
        acc_own = acc_own.at[first_pos].add(weight * own_term)
        dens_term = lax.dot_general(
            mixed_half, amp_half, (((1,), (1,)), ((), ())), preferred_element_type=jnp.float32
        )
        part_term = jnp.einsum(
            "ap,ab->pb", left_block, mixed_half, preferred_element_type=jnp.float32
        )
        acc_part = acc_part.at[second].add(weight * part_term)
        dens_term = dens_term + lax.dot_general(
            mixed_half, amp_half, (((0,), (0,)), ((), ())), preferred_element_type=jnp.float32
        )
        density = density + weight * dens_term
        return (acc_own, acc_part, density)

    return lax.fori_loop(0, per_batch * per_batch, one_pair, (acc_own, acc_part, density))


def per_device(factors, occ_energy, vir_energy, metric):
    n_blk = lax.axis_size("blk")
    n_sec = lax.axis_size("sec")
    blk_pos = lax.axis_index("blk")
    sec_pos = lax.axis_index("sec")
    per_batch = factors.shape[0]
    virtuals = factors.shape[1]
    aux_part = factors.shape[2]
    aux_total = aux_part * n_sec
    cycle_turns = min(CYCLE_STEPS, n_blk // (2 * n_sec))
    own_full = lax.all_gather(factors, "sec", axis=2, tiled=True)
    own_energy = batch_energy(occ_energy, blk_pos, per_batch)
    acc_own = jnp.zeros((per_batch, aux_total, virtuals), jnp.float32)
    density = jnp.zeros((virtuals, virtuals), jnp.float32)
    segmented = [factors]
    moving = factors
    for shift_turn in range(n_sec - 1):
        moving = from_behind(moving, "blk", 1)
        segmented.append(moving)
    partner = lax.all_to_all(
        jnp.stack(segmented, 0), "sec", split_axis=0, concat_axis=3, tiled=True
    )[0]
    acc_part = jnp.zeros((per_batch, aux_total, virtuals), jnp.float32)
    for cycle_step in range(cycle_turns):
        if cycle_step > 0:
            partner = from_behind(partner, "blk", n_sec)
            acc_part = from_behind(acc_part, "blk", n_sec)
        offset = sec_pos + n_sec * cycle_step
        weight = jnp.where(offset == 0, jnp.float32(0.5), jnp.float32(1.0))
        part_energy = batch_energy(occ_energy, (blk_pos - offset) % n_blk, per_batch)
        acc_own, acc_part, density = pair_block(
            own_full,
            own_energy,
            partner,
            part_energy,
            vir_energy,
            acc_own,
            acc_part,
            density,
            weight,
        )
    if cycle_turns > 1:
        acc_part = from_behind(acc_part, "blk", -n_sec * (cycle_turns - 1))
    regrouped = lax.all_to_all(acc_part[None], "sec", split_axis=2, concat_axis=0, tiled=True)
    carried = regrouped[n_sec - 1]
    for shift_turn in range(n_sec - 2, -1, -1):
        carried = from_behind(carried, "blk", -1) + regrouped[shift_turn]
    metric_rows = lax.dynamic_slice_in_dim(metric, sec_pos * aux_part, aux_part, 0)
    own_term = jnp.einsum("pq,ipa->qia", metric, acc_own, precision=lax.Precision.HIGHEST)
    gamma_part = lax.psum_scatter(
        own_term + jnp.einsum("pq,ipa->qia", metric_rows, carried, precision=lax.Precision.HIGHEST),
        "sec",
        scatter_dimension=0,
        tiled=True,
    )
    density_rows = lax.psum_scatter(density, "blk", scatter_dimension=0, tiled=True)
    density_out = lax.psum(density_rows, "sec")
    return (gamma_part, density_out)


def solution(mesh):
    return jax.shard_map(
        per_device,
        mesh=mesh,
        in_specs=(P("blk", None, "sec"), P(), P(), P()),
        out_specs=(P("sec", "blk", None), P("blk", None)),
        check_vma=False,
    )
```

profile of v0, /device:TPU:1, one launch (start us, length us, event | category | flops | bytes accessed | tf_op | source)
XLA Modules:
  0.0 248.1 jit_solution(9871074045163659175)
XLA Ops:
  8.3 2.1 collective-permute-start
  10.5 9.0 %collective-permute-done = bf16[1,512,256]{1,2,0:T(8,128)(2,1)S(1)} collective-permute-done((bf16[1,512,256]{1,2,0:T(8,128)(2,1)S(1)}, bf16[1,512,256]{1,2,0:T(8,128)(2,1)S(1)}, u32[]{:S(2)}, u32[]{:S(2)}) %collective-permute-start) | collective-permute-done | bytes 262176 | tf_op jit(solution)/shard_map/ppermute | solution.py:11
  19.5 9.3 %collective-permute-done.1 = bf16[1,512,256]{1,2,0:T(8,128)(2,1)S(1)} collective-permute-done((bf16[1,512,256]{1,2,0:T(8,128)(2,1)S(1)}, bf16[1,512,256]{1,2,0:T(8,128)(2,1)S(1)}, u32[]{:S(2)}, u32[]{:S(2)}) %collective-permute-start.1) | collective-permute-done | bytes 262176 | tf_op jit(solution)/shard_map/ppermute | solution.py:11
  28.8 8.3 %collective-permute-done.2 = bf16[1,512,256]{1,2,0:T(8,128)(2,1)S(1)} collective-permute-done((bf16[1,512,256]{1,2,0:T(8,128)(2,1)S(1)}, bf16[1,512,256]{1,2,0:T(8,128)(2,1)S(1)}, u32[]{:S(2)}, u32[]{:S(2)}) %collective-permute-start.2) | collective-permute-done | bytes 262176 | tf_op jit(solution)/shard_map/ppermute | solution.py:11
  38.2 6.6 %all-to-all-start = ((bf16[4,1,512,256]{2,3,1,0:T(8,128)(2,1)}), bf16[4,1,512,256]{2,3,1,0:T(8,128)(2,1)S(1)}, u32[]{:S(2)}, u32[]{:S(2)}) async-start(bf16[4,1,512,256]{2,3,1,0:T(8,128)(2,1)} %pad_maximum_fusion), calls=%async_computation | async-start | bytes 2097152 | tf_op jit(solution)/shard_map/all_to_all | solution.py:79
  46.7 11.7 %all-to-all-done = bf16[4,1,512,256]{2,3,1,0:T(8,128)(2,1)S(1)} async-done(((bf16[4,1,512,256]{2,3,1,0:T(8,128)(2,1)}), bf16[4,1,512,256]{2,3,1,0:T(8,128)(2,1)S(1)}, u32[]{:S(2)}, u32[]{:S(2)}) %all-to-all-start) | async-done | bytes 1048608 | tf_op jit(solution)/shard_map/all_to_all | solution.py:79
  58.4 2.4 fusion.5
  62.1 1.7 subtract_convert_fusion
  64.5 3.7 %copy.21 = f32[1,1,1024,512]{3,1,0,2:T(1,128)} copy(f32[1,1,1024,512]{2,3,1,0:T(8,128)S(1)} %multiply_bitcast_fusion) | data formatting | bytes 4194304 | tf_op jit(solution)/shard_map/broadcast_in_dim | solution.py:103
  68.2 4.4 %all-to-all-start.1 = ((f32[1,1,1024,512]{3,1,0,2:T(1,128)}), f32[1,1,1024,512]{3,1,0,2:T(1,128)S(1)}, u32[]{:S(2)}, u32[]{:S(2)}) async-start(f32[1,1,1024,512]{3,1,0,2:T(1,128)} %copy.21), calls=%async_computation.1 | async-start | bytes 4194304 | tf_op jit(solution)/shard_map/all_to_all | solution.py:103
  72.7 2.8 %fusion.15 = f32[512,512]{1,0:T(8,128)} fusion(bf16[512,512]{1,0:T(8,128)(2,1)S(1)} %subtract_convert_fusion, f32[512,512]{0,1:T(8,128)} %copy.20, f32[512]{0:T(512)S(1)} %copy-done.4, f32[512]{0:T(512)S(1)} %broadcast_subtract_fusion), kind=kOutput, calls=%fused_computation.24 | convolution fusion | flops 269221888 | bytes 2625536 | tf_op jit(solution)/shard_map/while/body/eval_jaxpr/dot_general | solution.py:44
  75.5 22.0 %all-to-all-done.1 = f32[1,1,1024,512]{3,1,0,2:T(1,128)S(1)} async-done(((f32[1,1,1024,512]{3,1,0,2:T(1,128)}), f32[1,1,1024,512]{3,1,0,2:T(1,128)S(1)}, u32[]{:S(2)}, u32[]{:S(2)}) %all-to-all-start.1) | async-done | bytes 2097184 | tf_op jit(solution)/shard_map/all_to_all | solution.py:103
  98.9 2.8 %fusion.3 = f32[512,512]{1,0:T(8,128)} fusion(f32[512,512]{1,0:T(8,128)S(1)} %copy-done.6, bf16[512,512]{1,0:T(8,128)(2,1)S(1)} %subtract_convert_fusion, f32[]{:T(128)S(6)} %select_n.41, f32[512,512]{0,1:T(8,128)} %copy.20, f32[512]{0:T(512)S(1)} %copy-done.4, f32[512]{0:T(512)S(1)} %broadcast_subtract_fusion), kind=kOutput, calls=%fused_computation.6 | convolution fusion | flops 269746176 | bytes 3674116 | tf_op jit(solution)/shard_map/while/body/eval_jaxpr/dot_general | solution.py:51
  101.7 1.9 fusion.18
  103.6 9.2 %collective-permute-done.3 = f32[1,256,512]{2,1,0:T(8,128)} collective-permute-done((f32[1,256,512]{2,1,0:T(8,128)}, f32[1,256,512]{2,1,0:T(8,128)}, u32[]{:S(2)}, u32[]{:S(2)}) %collective-permute-start.3) | collective-permute-done | bytes 524320 | tf_op jit(solution)/shard_map/ppermute | solution.py:11
  113.9 3.2 %collective-permute-start.4 = (f32[1,256,512]{2,1,0:T(8,128)S(1)}, f32[1,256,512]{2,1,0:T(8,128)S(1)}, u32[]{:S(2)}, u32[]{:S(2)}) collective-permute-start(f32[1,256,512]{2,1,0:T(8,128)S(1)} %fusion.13), channel_id=1, source_target_pairs={{0,28},{4,0},{8,4},{12,8},{16,12},{20,16},{24,20},{28,24},{1,29},{... | collective-permute-start | bytes 1572872 | tf_op jit(solution)/shard_map/ppermute | solution.py:11
  117.1 13.6 %collective-permute-done.4 = f32[1,256,512]{2,1,0:T(8,128)S(1)} collective-permute-done((f32[1,256,512]{2,1,0:T(8,128)S(1)}, f32[1,256,512]{2,1,0:T(8,128)S(1)}, u32[]{:S(2)}, u32[]{:S(2)}) %collective-permute-start.4) | collective-permute-done | bytes 524320 | tf_op jit(solution)/shard_map/ppermute | solution.py:11
  132.0 5.1 %collective-permute-start.5 = (f32[1,256,512]{2,1,0:T(8,128)S(1)}, f32[1,256,512]{2,1,0:T(8,128)S(1)}, u32[]{:S(2)}, u32[]{:S(2)}) collective-permute-start(f32[1,256,512]{2,1,0:T(8,128)S(1)} %fusion.12), channel_id=1, source_target_pairs={{0,28},{4,0},{8,4},{12,8},{16,12},{20,16},{24,20},{28,24},{1,29},{... | collective-permute-start | bytes 1572872 | tf_op jit(solution)/shard_map/ppermute | solution.py:11
  137.9 6.8 %fusion.1 = f32[512,1024]{1,0:T(8,128)S(1)} fusion(f32[1024,1024]{1,0:T(8,128)S(1)} %copy-done, f32[1024,512]{1,0:T(8,128)S(1)} %fusion.20, f32[]{:T(128)S(6)} %select_n.41), kind=kOutput, calls=%fused_computation.3 | convolution fusion | flops 6442975232 | bytes 8388612 | tf_op jit(solution)/shard_map/pq,ipa->qia/dot_general | solution.py:108
  145.8 3.3 %fusion = f32[1024,1,512]{0,2,1:T(8,128)} fusion(f32[512,1024]{1,0:T(8,128)S(1)} %fusion.1, f32[1024,1024]{1,0:T(8,128)S(1)} %copy-done, s32[]{:T(128)S(6)} %select_n.45, f32[1,256,512]{2,1,0:T(8,128)S(1)} %collective-permute-done.5, f32[1,1,256,512]{3,1,0,2:T(1,128)S(1)} %get-tuple-element.75), kind=kOutput, calls=%fused_computation.1 | convolution fusion | flops 1611268096 | bytes 6291460 | tf_op jit(solution)/shard_map/pq,ipa->qia/dot_general | solution.py:110
  149.2 23.9 %reduce-scatter.5.cloned.1.call-done = f32[64,512]{1,0:T(8,128)} async-done(((f32[512,512]{1,0:T(8,128)}), f32[64,512]{1,0:T(8,128)}) %reduce-scatter.5.cloned.1.call-update) | async-done | bytes 131088 | tf_op jit(solution)/shard_map/reduce_scatter | solution.py:115
  173.1 34.7 %reduce-scatter.3.cloned.1.call-done = f32[256,1,512]{0,2,1:T(8,128)} async-done(((f32[1024,1,512]{0,2,1:T(8,128)}), f32[256,1,512]{0,2,1:T(8,128)}) %reduce-scatter.3.cloned.1.call-update) | async-done | bytes 524304 | tf_op jit(solution)/shard_map/reduce_scatter | solution.py:109
  207.8 1.9 copy.26
  209.8 30.2 %all-reduce.2.cloned.1.call-done = f32[64,512]{1,0:T(8,128)} async-done(((f32[64,512]{1,0:T(8,128)}), f32[64,512]{1,0:T(8,128)}) %all-reduce.2.cloned.1.call-update) | async-done | bytes 131088 | tf_op jit(solution)/shard_map/psum | solution.py:116
  (39 shorter events, 12.3 us)
Async XLA Ops:
  7.2 51.2 %all-gather.2.cloned.1.call-start = ((), (), s32[]{:S(2)}) async-start(), calls=%async_computation.4 | async-start | bytes 1310720 | tf_op jit(solution)/shard_map/all_gather | solution.py:70
  8.3 11.2 %collective-permute-start = (bf16[1,512,256]{1,2,0:T(8,128)(2,1)S(1)}, bf16[1,512,256]{1,2,0:T(8,128)(2,1)S(1)}, u32[]{:S(2)}, u32[]{:S(2)}) collective-permute-start(bf16[1,512,256]{1,2,0:T(8,128)(2,1)S(1)} %copy.18), channel_id=1, source_target_pairs={{0,4},{4,8},{8,12},{12,16},{16,20},{20,24},{24,28},{28,0},{1,5},{5... | collective-permute-start | bytes 786440 | tf_op jit(solution)/shard_map/ppermute | solution.py:11
  19.5 9.3 %collective-permute-start.1 = (bf16[1,512,256]{1,2,0:T(8,128)(2,1)S(1)}, bf16[1,512,256]{1,2,0:T(8,128)(2,1)S(1)}, u32[]{:S(2)}, u32[]{:S(2)}) collective-permute-start(bf16[1,512,256]{1,2,0:T(8,128)(2,1)S(1)} %collective-permute-done), channel_id=1, source_target_pairs={{0,4},{4,8},{8,12},{12,16},{16,20},{20,24},{24,28},{28,0},{1,5},{5... | collective-permute-start | bytes 786440 | tf_op jit(solution)/shard_map/ppermute | solution.py:11
  28.8 8.3 %collective-permute-start.2 = (bf16[1,512,256]{1,2,0:T(8,128)(2,1)S(1)}, bf16[1,512,256]{1,2,0:T(8,128)(2,1)S(1)}, u32[]{:S(2)}, u32[]{:S(2)}) collective-permute-start(bf16[1,512,256]{1,2,0:T(8,128)(2,1)S(1)} %collective-permute-done.1), channel_id=1, source_target_pairs={{0,4},{4,8},{8,12},{12,16},{16,20},{20,24},{24,28},{28,0},{1,5},{5... | collective-permute-start | bytes 786440 | tf_op jit(solution)/shard_map/ppermute | solution.py:11
  37.1 7.7 %copy-start.5 = (f32[8]{0:T(128)S(1)}, f32[8]{0:T(128)}, u32[]{:S(2)}) copy-start(f32[8]{0:T(128)} %param.9) | copy-start | bytes 100
  37.1 9.6 %copy-start.4 = (f32[512]{0:T(512)S(1)}, f32[512]{0:T(512)}, u32[]{:S(2)}) copy-start(f32[512]{0:T(512)} %param.10) | copy-start | bytes 6148
  38.2 20.2 %all-to-all-start = ((bf16[4,1,512,256]{2,3,1,0:T(8,128)(2,1)}), bf16[4,1,512,256]{2,3,1,0:T(8,128)(2,1)S(1)}, u32[]{:S(2)}, u32[]{:S(2)}) async-start(bf16[4,1,512,256]{2,3,1,0:T(8,128)(2,1)} %pad_maximum_fusion), calls=%async_computation | async-start | bytes 2097152 | tf_op jit(solution)/shard_map/all_to_all | solution.py:79
  58.4 3.7 %copy-start.1 = (bf16[4,1,512,256]{2,3,1,0:T(8,128)(2,1)}, bf16[4,1,512,256]{2,3,1,0:T(8,128)(2,1)S(1)}, u32[]{:S(2)}) copy-start(bf16[4,1,512,256]{2,3,1,0:T(8,128)(2,1)S(1)} %all-to-all-done) | copy-start | bytes 3145732
  62.1 1.7 copy-start.3
  68.2 29.3 %all-to-all-start.1 = ((f32[1,1,1024,512]{3,1,0,2:T(1,128)}), f32[1,1,1024,512]{3,1,0,2:T(1,128)S(1)}, u32[]{:S(2)}, u32[]{:S(2)}) async-start(f32[1,1,1024,512]{3,1,0,2:T(1,128)} %copy.21), calls=%async_computation.1 | async-start | bytes 4194304 | tf_op jit(solution)/shard_map/all_to_all | solution.py:103
  72.7 100.4 %reduce-scatter.5.cloned.1.call-start = ((), (), s32[]{:S(2)}) async-start(), calls=%async_computation.6 | async-start | bytes 1179648 | tf_op jit(solution)/shard_map/reduce_scatter | solution.py:115
  97.5 1.4 copy-start.6
  98.5 14.3 %collective-permute-start.3 = (f32[1,256,512]{2,1,0:T(8,128)}, f32[1,256,512]{2,1,0:T(8,128)}, u32[]{:S(2)}, u32[]{:S(2)}) collective-permute-start(f32[1,256,512]{2,1,0:T(8,128)} %slice_bitcast_fusion), channel_id=1, source_target_pairs={{0,28},{4,0},{8,4},{12,8},{16,12},{20,16},{24,20},{28,24},{1,29},{... | collective-permute-start | bytes 1572872 | tf_op jit(solution)/shard_map/ppermute | solution.py:11
  101.7 106.1 %reduce-scatter.3.cloned.1.call-start = ((), (), s32[]{:S(2)}) async-start(), calls=%async_computation.5 | async-start | bytes 2621440 | tf_op jit(solution)/shard_map/reduce_scatter | solution.py:109
  103.6 33.5 %copy-start.2 = (bf16[4,1,512,256]{2,3,1,0:T(8,128)(2,1)S(1)}, bf16[4,1,512,256]{2,3,1,0:T(8,128)(2,1)}, u32[]{:S(2)}) copy-start(bf16[4,1,512,256]{2,3,1,0:T(8,128)(2,1)} %copy-done.1) | copy-start | bytes 3145732
  113.9 16.8 %collective-permute-start.4 = (f32[1,256,512]{2,1,0:T(8,128)S(1)}, f32[1,256,512]{2,1,0:T(8,128)S(1)}, u32[]{:S(2)}, u32[]{:S(2)}) collective-permute-start(f32[1,256,512]{2,1,0:T(8,128)S(1)} %fusion.13), channel_id=1, source_target_pairs={{0,28},{4,0},{8,4},{12,8},{16,12},{20,16},{24,20},{28,24},{1,29},{... | collective-permute-start | bytes 1572872 | tf_op jit(solution)/shard_map/ppermute | solution.py:11
  130.7 7.2 %copy-start = (f32[1024,1024]{1,0:T(8,128)S(1)}, f32[1024,1024]{1,0:T(8,128)}, u32[]{:S(2)}) copy-start(f32[1024,1024]{1,0:T(8,128)} %param.11) | copy-start | bytes 12582916
  132.0 13.8 %collective-permute-start.5 = (f32[1,256,512]{2,1,0:T(8,128)S(1)}, f32[1,256,512]{2,1,0:T(8,128)S(1)}, u32[]{:S(2)}, u32[]{:S(2)}) collective-permute-start(f32[1,256,512]{2,1,0:T(8,128)S(1)} %fusion.12), channel_id=1, source_target_pairs={{0,28},{4,0},{8,4},{12,8},{16,12},{20,16},{24,20},{28,24},{1,29},{... | collective-permute-start | bytes 1572872 | tf_op jit(solution)/shard_map/ppermute | solution.py:11
  149.1 90.9 %all-reduce.2.cloned.1.call-start = ((), (), s32[]{:S(2)}) async-start(), calls=%async_computation.7 | async-start | bytes 262144 | tf_op jit(solution)/shard_map/psum | solution.py:116
Sparse Core Ops, SparseCore 0:
  10.6 18.2 all-gather.1
  101.8 71.2 reduce-scatter.4
  175.8 32.0 reduce-scatter.2
  210.0 29.9 all-reduce.1
where the time goes:
time: 251 us; the launch traced here: 248 us
  waiting for transfers between devices  173 us (69%)
  starting transfers between devices  21.5 us (9%)
  matrix products  19.6 us (8%)
  between operations  15.2 us (6%)
  local copies, waits for them, and re-layouts  13.5 us (5%)
  other arithmetic  5.21 us (2%)
    ppermute x6, waiting for transfers between devices, from_behind(): lax.ppermute(shard, axis, [(i, (i + by) % devices) for i in range(devices)])  50.5 us
    reduce_scatter x1, waiting for transfers between devices, per_device(): lax.psum_scatter(own_term + jnp.einsum('pq,ipa->qia', metric_rows, carrie...  34.7 us
    psum x1, waiting for transfers between devices, per_device(): density_out = lax.psum(density_rows, 'sec')  30.2 us
    reduce_scatter x1, waiting for transfers between devices, per_device(): lax.psum_scatter(density, 'blk', scatter_dimension=0, tiled=True)  23.9 us
    all_to_all x1, waiting for transfers between devices, per_device(): lax.all_to_all(acc_part[None], 'sec', split_axis=2, concat_axis=0, tiled=...  22 us
    all_to_all x1, waiting for transfers between devices, per_device(): lax.all_to_all(jnp.stack(segmented, 0), 'sec', split_axis=0, concat_axis=...  11.7 us
    ppermute x6, starting transfers between devices, from_behind(): lax.ppermute(shard, axis, [(i, (i + by) % devices) for i in range(devices)])  10.4 us
    dot_general x1, matrix products, per_device(): jnp.einsum('pq,ipa->qia', metric, acc_own, precision=lax.Precision.HIGHEST)  6.83 us
  transfers between devices with their start and end apart: 12, of which 11 were waited for; matrix products, arithmetic and copies ran while one was open for 10% of the time, Pallas kernels for 0%

commit v1 on v0

--- a/solution.py
+++ b/solution.py
@@ -1,6 +1,8 @@
 import jax
 import jax.numpy as jnp
 from jax import lax
+from jax.experimental import pallas as pl
+from jax.experimental.pallas import tpu as pltpu
 from jax.sharding import PartitionSpec as P
 
 CYCLE_STEPS = 4
@@ -57,7 +59,7 @@
     return lax.fori_loop(0, per_batch * per_batch, one_pair, (acc_own, acc_part, density))
 
 
-def per_device(factors, occ_energy, vir_energy, metric):
+def general_device(factors, occ_energy, vir_energy, metric):
     n_blk = lax.axis_size("blk")
     n_sec = lax.axis_size("sec")
     blk_pos = lax.axis_index("blk")
@@ -117,7 +119,308 @@
     return (gamma_part, density_out)
 
 
+AXES = ("blk", "sec")
+NT = (((1,), (1,)), ((), ()))
+NN = (((1,), (0,)), ((), ()))
+TAIL_ROWS = 16
+VMEM_LIMIT = 48 * 1024 * 1024
+
+
+def dot(left, right, dims):
+    return lax.dot_general(left, right, dims, preferred_element_type=jnp.float32)
+
+
+def split_bits(device, n_sec):
+    blk, sec = device // n_sec, device % n_sec
+    return blk // 2, blk % 2, sec // 2, sec % 2
+
+
+def join_bits(z, y, x, c, n_sec):
+    return (2 * z + y) * n_sec + 2 * x + c
+
+
+def send(value, target, n_blk, n_sec):
+    pairs = []
+    for device in range(n_blk * n_sec):
+        pairs.append((device, join_bits(*target(*split_bits(device, n_sec)), n_sec)))
+    return lax.ppermute(value, AXES, pairs)
+
+
+def pair_terms(sum_energy, weight, row_energy, col_energy, left, right):
+    straight = dot(left[0], right[0], NT)
+    turned = dot(right[0], left[0], NT)
+    for part in range(1, len(left)):
+        straight += dot(left[part], right[part], NT)
+        turned += dot(right[part], left[part], NT)
+    amplitude = straight / (sum_energy - col_energy - row_energy)
+    amplitude_t = turned / (sum_energy - row_energy - col_energy)
+    mixed = (2.0 * amplitude - amplitude_t) * weight
+    return amplitude.astype(jnp.bfloat16), mixed.astype(jnp.bfloat16)
+
+
+def first_pair_kernel(scalars, row_energy, col_energy, *refs):
+    left = [ref[...] for ref in refs[:4]]
+    right = [ref[...] for ref in refs[4:8]]
+    grad_out, dens_out = refs[8:]
+    amp_half, mixed_half = pair_terms(
+        scalars[0], scalars[1], row_energy[...], col_energy[...], left, right
+    )
+    width = right[0].shape[1]
+    for part in range(4):
+        grad_out[:, part * width : (part + 1) * width] = dot(mixed_half, right[part], NN)
+    dens_out[...] = dot(mixed_half, amp_half, NT)
+
+
+def last_pair_kernel(scalars, row_energy, col_energy, *refs):
+    left = [ref[...] for ref in refs[:4]]
+    right = [ref[...] for ref in refs[4:8]]
+    grad_in, dens_in, high_out, low_out, dens_out = refs[8:]
+    amp_half, mixed_half = pair_terms(
+        scalars[0], scalars[1], row_energy[...], col_energy[...], left, right
+    )
+    width = right[0].shape[1]
+    for part in range(4):
+        cols = slice(part * width, (part + 1) * width)
+        grad = grad_in[:, cols] + dot(mixed_half, right[part], NN)
+        high = grad.astype(jnp.bfloat16)
+        high_out[:, cols] = high
+        low_out[:, cols] = (grad - high.astype(jnp.float32)).astype(jnp.bfloat16)
+    dens_out[...] = dens_in[...] + dot(mixed_half, amp_half, NT)
+
+
+def metric_kernel(metric_high, metric_low, high, low, out, peak):
+    metric_top = metric_high[0]
+    block = dot(metric_top, high[...], NT)
+    block += dot(metric_top, low[...], NT)
+    block += dot(metric_low[0], high[...], NT)
+    out[...] = block
+    peak[...] = jnp.max(jnp.abs(block), keepdims=True)
+
+
+def turn_metric_kernel(order, metric, high, low):
+    turned = metric[...].T
+    top = turned.astype(jnp.bfloat16)
+    high[0] = top
+    low[0] = (turned - top.astype(jnp.float32)).astype(jnp.bfloat16)
+
+
+def pack16(value, peak):
+    power = jnp.clip(jnp.floor(14.0 - jnp.log2(jnp.maximum(peak, 1e-30))), -110.0, 110.0)
+    scaled = (value * jnp.exp2(power)).astype(jnp.float16)
+    tail = jnp.broadcast_to(power.astype(jnp.float16), (TAIL_ROWS, value.shape[1]))
+    return jnp.concatenate([scaled, tail], 0)
+
+
+def unpack16(packed):
+    rows = packed.shape[0] - TAIL_ROWS
+    power = packed[rows, 0].astype(jnp.float32)
+    return packed[:rows].astype(jnp.float32) * jnp.exp2(-power)
+
+
+def fast_device(factors, occ_energy, vir_energy, metric):
+    n_blk = lax.axis_size("blk")
+    n_sec = lax.axis_size("sec")
+    blk_pos = lax.axis_index("blk")
+    sec_pos = lax.axis_index("sec")
+    z, y = blk_pos // 2, blk_pos % 2
+    x, c = sec_pos // 2, sec_pos % 2
+    n_lay = n_blk // 2
+    half_lay = n_lay // 2
+    own = factors[0]
+    virtuals, width = own.shape
+    aux_total = width * n_sec
+
+    def move(value, target):
+        return send(value, target, n_blk, n_sec)
+
+    def core_swap(value):
+        return move(value, lambda z, y, x, c: (z, y, x, 1 - c))
+
+    def x_swap(value):
+        return move(value, lambda z, y, x, c: (z, y, 1 - x, c))
+
+    def y_swap(value):
+        return move(value, lambda z, y, x, c: (z, 1 - y, x, c))
+
+    def first_partner(value):
+        return move(value, lambda z, y, x, c: (z if x else z ^ 1, y, x, c))
+
+    def last_partner(value):
+        return move(value, lambda z, y, x, c: (z ^ 3 if x else z ^ 2, y, x, c))
+
+    with jax.named_scope("gather"):
+        swapped = x_swap(own)
+        last_own = last_partner(own)
+        first_own = first_partner(own)
+        other_own = y_swap(own)
+        last_swapped = last_partner(swapped)
+        first_swapped = first_partner(swapped)
+        other_swapped = y_swap(swapped)
+        at_home = c == y
+        left_mine = [
+            jnp.where(at_home, own, other_own),
+            jnp.where(at_home, swapped, other_swapped),
+        ]
+        left_sent = jnp.stack(
+            [
+                jnp.where(at_home, other_own, own),
+                jnp.where(at_home, other_swapped, swapped),
+            ],
+            0,
+        )
+        left_got = core_swap(left_sent)
+        left = left_mine + [left_got[0], left_got[1]]
+        first = [first_own, first_swapped, core_swap(first_own), core_swap(first_swapped)]
+        last = [last_own, last_swapped, core_swap(last_own), core_swap(last_swapped)]
+
+    home_energy = lax.dynamic_index_in_dim(occ_energy, 2 * z + c, 0, keepdims=False)
+
+    def energy_of(layer):
+        return lax.dynamic_index_in_dim(occ_energy, 2 * layer + y, 0, keepdims=False)
+
+    first_layer = jnp.where(x == 1, z, z ^ 1)
+    last_layer = jnp.where(x == 1, z ^ 3, z ^ 2)
+    first_scalars = jnp.stack([home_energy + energy_of(first_layer), jnp.float32(1.0)])
+    last_weight = jnp.where((x == 0) & (c == y), jnp.float32(0.0), jnp.float32(1.0))
+    last_scalars = jnp.stack([home_energy + energy_of(last_layer), last_weight])
+    row_energy, col_energy = vir_energy[None, :], vir_energy[:, None]
+
+    smem = pl.BlockSpec(memory_space=pltpu.SMEM)
+    vmem = pl.BlockSpec(memory_space=pltpu.VMEM)
+    params = pltpu.CompilerParams(vmem_limit_bytes=VMEM_LIMIT)
+    square = 2 * virtuals * virtuals
+    grad_shape = (virtuals, aux_total)
+
+    def blocks_of_round(step):
+        return 2 * (x ^ (step >> 1)) + (y ^ (step & 1))
+
+    with jax.named_scope("metric_turn"):
+        order = jnp.stack(
+            [sec_pos, sec_pos ^ 2, sec_pos ^ 1, sec_pos ^ 3]
+            + [blocks_of_round(step) for step in range(4)]
+        ).astype(jnp.int32)
+        turned = jax.ShapeDtypeStruct((4, width, aux_total), jnp.bfloat16)
+        turned_spec = pl.BlockSpec((1, width, width), lambda r, k, order: (r, 0, k))
+        metric_high, metric_low = pl.pallas_call(
+            turn_metric_kernel,
+            grid_spec=pltpu.PrefetchScalarGridSpec(
+                num_scalar_prefetch=1,
+                grid=(4, 4),
+                in_specs=[
+                    pl.BlockSpec((width, width), lambda r, k, order: (order[k], order[4 + r]))
+                ],
+                out_specs=[turned_spec, turned_spec],
+            ),
+            out_shape=[turned, turned],
+        )(order, metric)
+
+    with jax.named_scope("first_pair"):
+        grad, dens = pl.pallas_call(
+            first_pair_kernel,
+            in_specs=[smem] + [vmem] * 10,
+            out_specs=[vmem, vmem],
+            out_shape=[
+                jax.ShapeDtypeStruct(grad_shape, jnp.float32),
+                jax.ShapeDtypeStruct((virtuals, virtuals), jnp.float32),
+            ],
+            compiler_params=params,
+            cost_estimate=pl.CostEstimate(
+                flops=square * (3 * aux_total + virtuals),
+                bytes_accessed=10 * virtuals * aux_total,
+                transcendentals=0,
+            ),
+        )(first_scalars, row_energy, col_energy, *left, *first)
+
+    with jax.named_scope("last_pair"):
+        high, low, dens = pl.pallas_call(
+            last_pair_kernel,
+            in_specs=[smem] + [vmem] * 12,
+            out_specs=[vmem] * 3,
+            out_shape=[
+                jax.ShapeDtypeStruct(grad_shape, jnp.bfloat16),
+                jax.ShapeDtypeStruct(grad_shape, jnp.bfloat16),
+                jax.ShapeDtypeStruct((virtuals, virtuals), jnp.float32),
+            ],
+            compiler_params=params,
+            cost_estimate=pl.CostEstimate(
+                flops=square * (3 * aux_total + virtuals),
+                bytes_accessed=16 * virtuals * aux_total,
+                transcendentals=0,
+            ),
+        )(last_scalars, row_energy, col_energy, *left, *last, grad, dens)
+
+    with jax.named_scope("gamma"):
+        got = []
+        for step in range(4):
+            metric_spec = pl.BlockSpec((1, width, aux_total), lambda i, step=step: (step, 0, 0))
+            whole = pl.BlockSpec(grad_shape, lambda i: (0, 0))
+            block, peak = pl.pallas_call(
+                metric_kernel,
+                grid=(1,),
+                in_specs=[metric_spec, metric_spec, whole, whole],
+                out_specs=[
+                    pl.BlockSpec((width, virtuals), lambda i: (0, 0)),
+                    pl.BlockSpec((1, 1), lambda i: (0, 0)),
+                ],
+                out_shape=[
+                    jax.ShapeDtypeStruct((width, virtuals), jnp.float32),
+                    jax.ShapeDtypeStruct((1, 1), jnp.float32),
+                ],
+                compiler_params=params,
+                cost_estimate=pl.CostEstimate(
+                    flops=6 * width * virtuals * aux_total,
+                    bytes_accessed=4 * (width + virtuals) * aux_total,
+                    transcendentals=0,
+                ),
+            )(metric_high, metric_low, high, low)
+            packed = pack16(block, peak)
+            got.append(
+                move(
+                    packed,
+                    lambda z, y, x, c, step=step: (z, c, x ^ (step >> 1), y ^ (step & 1)),
+                )
+            )
+        total = unpack16(got[0])
+        for packed in got[1:]:
+            total = total + unpack16(packed)
+        gamma = total[:, None, :]
+
+    with jax.named_scope("density"):
+        half = virtuals // 2
+        layer_rows = virtuals // n_lay
+        rows = virtuals // n_blk
+        got_half = core_swap(lax.dynamic_slice_in_dim(dens, (1 - c) * half, half, 1))
+        dens = lax.dynamic_slice_in_dim(dens, c * half, half, 1) + got_half
+        dens = dens.reshape(n_lay, layer_rows, half)
+        peak = jnp.max(jnp.abs(dens))
+        layer = lax.dynamic_index_in_dim(dens, z, 0, keepdims=False)
+        for step in range(1, n_lay):
+            packed = pack16(lax.dynamic_index_in_dim(dens, z ^ step, 0, keepdims=False), peak)
+            layer = layer + unpack16(
+                move(packed, lambda z, y, x, c, step=step: (z ^ step, y, x, c))
+            )
+        mine = lax.dynamic_slice_in_dim(layer, y * rows, rows, 0)
+        theirs = lax.dynamic_slice_in_dim(layer, (1 - y) * rows, rows, 0)
+        from_y = y_swap(theirs)
+        from_xy = move(theirs, lambda z, y, x, c: (z, 1 - y, 1 - x, c))
+        block = (mine + x_swap(mine)) + (from_y + from_xy)
+        other = core_swap(block)
+        density = jnp.where(
+            c == 0,
+            jnp.concatenate([block, other], 1),
+            jnp.concatenate([other, block], 1),
+        )
+    return gamma, density
+
+
 def solution(mesh):
+    n_blk, n_sec = mesh.shape["blk"], mesh.shape["sec"]
+
+    def per_device(factors, occ_energy, vir_energy, metric):
+        two_rows_of_layers = n_sec == 4 and n_blk == 2 * n_sec and factors.shape[0] == 1
+        step = fast_device if two_rows_of_layers else general_device
+        return step(factors, occ_energy, vir_energy, metric)
+
     return jax.shard_map(
         per_device,
         mesh=mesh,

time: 251 us -> 113 us (0.45)
  waiting for transfers between devices: 173 us -> 25.9 us
  Pallas kernels: 0 us -> 29.6 us
  matrix products: 19.6 us -> 0 us
  starting transfers between devices: 21.5 us -> 30.9 us
  local copies, waits for them, and re-layouts: 13.5 us -> 9.11 us
  between operations: 15.2 us -> 12.1 us
    reduce_scatter x2 -> x0, waiting for transfers between devices: 58.6 us -> none  [the longest x1 34.7 us: per_device(): lax.psum_scatter(own_term + jnp.einsum('pq,ipa->qia', metric_rows, carrie...]
    all_to_all x2 -> x0, waiting for transfers between devices: 33.7 us -> none  [the longest x1 22 us: per_device(): lax.all_to_all(acc_part[None], 'sec', split_axis=2, concat_axis=0, tiled=...]
    psum x1 -> x0, waiting for transfers between devices: 30.2 us -> none  [per_device(): density_out = lax.psum(density_rows, 'sec')]
    pallas_call x0 -> x7, Pallas kernels: none -> 29.6 us  [the longest x1 11.7 us: fast_device(): pl.pallas_call(turn_metric_kernel, grid_spec=pltpu.PrefetchScalarGridSpec...]
    ppermute x6 -> x24, waiting for transfers between devices: 50.5 us -> 25.9 us  [send(): return lax.ppermute(value, AXES, pairs)]
    ppermute x6 -> x24, starting transfers between devices: 10.4 us -> 30.9 us  [send(): return lax.ppermute(value, AXES, pairs)]
    dot_general x7 -> x0, matrix products: 19.6 us -> none  [the longest x1 6.83 us: per_device(): jnp.einsum('pq,ipa->qia', metric, acc_own, precision=lax.Precision.HIGHEST)]
    all_to_all x2 -> x0, starting transfers between devices: 11 us -> none  [the longest x1 6.55 us: per_device(): lax.all_to_all(jnp.stack(segmented, 0), 'sec', split_axis=0, concat_axis=...]
  transfers between devices with their start and end apart: 12 -> 24, of which waited for: 11 -> 6; matrix products, arithmetic and copies ran while one was open for 10% -> 8% of each run, Pallas kernels for 0% -> 15%
where the time goes in v1:
time: 113 us; the launch traced here: 112 us
  starting transfers between devices  30.9 us (27%)
  Pallas kernels  29.6 us (26%)
  waiting for transfers between devices  25.9 us (23%)
  between operations  12.1 us (11%)
  local copies, waits for them, and re-layouts  9.11 us (8%)
  other arithmetic  4.12 us (4%)
    ppermute x24, starting transfers between devices, send(): return lax.ppermute(value, AXES, pairs)  30.9 us
    ppermute x24, waiting for transfers between devices, send(): return lax.ppermute(value, AXES, pairs)  25.9 us
    pallas_call x1, Pallas kernels, fast_device(): pl.pallas_call(turn_metric_kernel, grid_spec=pltpu.PrefetchScalarGridSpec...  11.7 us
    pallas_call x4, Pallas kernels, fast_device(): pl.pallas_call(metric_kernel, grid=(1,), in_specs=[metric_spec, metric_sp...  10.7 us
    pallas_call x1, Pallas kernels, fast_device(): pl.pallas_call(last_pair_kernel, in_specs=[smem] + [vmem] * 12, out_specs...  4.33 us
    unnamed x11, local copies, waits for them, and re-layouts  3.7 us
    slice x7, local copies, waits for them, and re-layouts, unpack16(): power = packed[rows, 0].astype(jnp.float32)  3.61 us
    pallas_call x1, Pallas kernels, fast_device(): pl.pallas_call(first_pair_kernel, in_specs=[smem] + [vmem] * 10, out_spec...  2.81 us
  transfers between devices with their start and end apart: 24, of which 6 were waited for; matrix products, arithmetic and copies ran while one was open for 8% of the time, Pallas kernels for 15%

profile of v1, /device:TPU:1, one launch (start us, length us, event | category | flops | bytes accessed | tf_op | source)
XLA Modules:
  0.0 111.8 jit_solution(7141356083339415400)
XLA Ops:
  0.6 2.1 %collective-permute-start.1 = (bf16[512,256]{1,0:T(8,128)(2,1)}, bf16[512,256]{1,0:T(8,128)(2,1)}, u32[]{:S(2)}, u32[]{:S(2)}) collective-permute-start(bf16[512,256]{1,0:T(8,128)(2,1)} %bitcast.11), channel_id=1, source_target_pairs={{0,2},{1,3},{2,0},{3,1},{4,6},{5,7},{6,4},{7,5},{8,10},{9,11},{10,... | collective-permute-start | bytes 786440 | tf_op jit(solution)/shard_map/gather/ppermute | solution.py:146
  4.0 5.1 %collective-permute-done.1 = bf16[512,256]{1,0:T(8,128)(2,1)} collective-permute-done((bf16[512,256]{1,0:T(8,128)(2,1)}, bf16[512,256]{1,0:T(8,128)(2,1)}, u32[]{:S(2)}, u32[]{:S(2)}) %collective-permute-start.1) | collective-permute-done | bytes 262176 | tf_op jit(solution)/shard_map/gather/ppermute | solution.py:146
  11.3 4.6 %collective-permute-done.2 = bf16[512,256]{1,0:T(8,128)(2,1)S(1)} collective-permute-done((bf16[512,256]{1,0:T(8,128)(2,1)}, bf16[512,256]{1,0:T(8,128)(2,1)S(1)}, u32[]{:S(2)}, u32[]{:S(2)}) %collective-permute-start.2) | collective-permute-done | bytes 262176 | tf_op jit(solution)/shard_map/gather/ppermute | solution.py:146
  16.9 2.2 %collective-permute-start.3 = (bf16[2,512,256]{2,1,0:T(8,128)(2,1)S(1)}, bf16[2,512,256]{2,1,0:T(8,128)(2,1)S(1)}, u32[]{:S(2)}, u32[]{:S(2)}) collective-permute-start(bf16[2,512,256]{2,1,0:T(8,128)(2,1)S(1)} %pad_maximum_fusion), channel_id=1, source_target_pairs={{0,1},{1,0},{2,3},{3,2},{4,5},{5,4},{6,7},{7,6},{8,9},{9,8},{10,11... | collective-permute-start | bytes 1572872 | tf_op jit(solution)/shard_map/gather/ppermute | solution.py:146
  19.2 3.1 %collective-permute-start.8 = (bf16[512,256]{1,0:T(8,128)(2,1)}, bf16[512,256]{1,0:T(8,128)(2,1)S(1)}, u32[]{:S(2)}, u32[]{:S(2)}) collective-permute-start(bf16[512,256]{1,0:T(8,128)(2,1)} %bitcast.11), channel_id=1, source_target_pairs={{0,8},{1,9},{2,2},{3,3},{4,12},{5,13},{6,6},{7,7},{8,0},{9,1},{10,... | collective-permute-start | bytes 786440 | tf_op jit(solution)/shard_map/gather/ppermute | solution.py:146
  22.3 2.1 %collective-permute-start.9 = (bf16[512,256]{1,0:T(8,128)(2,1)}, bf16[512,256]{1,0:T(8,128)(2,1)S(1)}, u32[]{:S(2)}, u32[]{:S(2)}) collective-permute-start(bf16[512,256]{1,0:T(8,128)(2,1)} %collective-permute-done.1), channel_id=1, source_target_pairs={{0,8},{1,9},{2,2},{3,3},{4,12},{5,13},{6,6},{7,7},{8,0},{9,1},{10,... | collective-permute-start | bytes 786440 | tf_op jit(solution)/shard_map/gather/ppermute | solution.py:146
  24.4 2.3 %collective-permute-start.4 = (bf16[512,256]{1,0:T(8,128)(2,1)}, bf16[512,256]{1,0:T(8,128)(2,1)S(1)}, u32[]{:S(2)}, u32[]{:S(2)}) collective-permute-start(bf16[512,256]{1,0:T(8,128)(2,1)} %bitcast.11), channel_id=1, source_target_pairs={{0,16},{1,17},{2,26},{3,27},{4,20},{5,21},{6,30},{7,31},{8,24},{9,... | collective-permute-start | bytes 786440 | tf_op jit(solution)/shard_map/gather/ppermute | solution.py:146
  30.1 7.9 %collective-permute-done.8.refs_4_ = bf16[512,256]{1,0:T(8,128)(2,1)S(1)} collective-permute-done((bf16[512,256]{1,0:T(8,128)(2,1)}, bf16[512,256]{1,0:T(8,128)(2,1)S(1)}, u32[]{:S(2)}, u32[]{:S(2)}) %collective-permute-start.8) | collective-permute-done | bytes 262176 | tf_op jit(solution)/shard_map/gather/ppermute | solution.py:146
  39.3 4.4 %collective-permute-done.9.refs_5_ = bf16[512,256]{1,0:T(8,128)(2,1)S(1)} collective-permute-done((bf16[512,256]{1,0:T(8,128)(2,1)}, bf16[512,256]{1,0:T(8,128)(2,1)S(1)}, u32[]{:S(2)}, u32[]{:S(2)}) %collective-permute-start.9) | collective-permute-done | bytes 262176 | tf_op jit(solution)/shard_map/gather/ppermute | solution.py:146
  45.4 11.7 %metric_turn.1 = (bf16[4,256,1024]{2,1,0:T(8,128)(2,1)}, bf16[4,256,1024]{2,1,0:T(8,128)(2,1)}) custom-call(s32[8]{0:T(128)} %stack.55.order, f32[1024,1024]{1,0:T(8,128)} %metric.1), custom_call_target="tpu_custom_call" | custom-call | tf_op jit(solution)/shard_map/metric_turn/pallas_call | solution.py:304
  57.7 2.8 %first_pair.1 = (f32[512,1024]{1,0:T(8,128)S(1)}, f32[512,512]{1,0:T(8,128)S(1)}) custom-call(f32[2]{0:T(128)S(1)} %pad_maximum_fusion.2.scalars, f32[1,512]{1,0:T(1,128)S(1)} %bitcast.53, f32[512,1]{1,0:T(8,128)S(1)} %copy.8.col_energy, bf16[512,256]{1,0:T(8,128)(2,1)S(1)} %get-tuple-element.44.refs_0_, bf16[512,256]{1,0:T(8,128)(2,1)S(1)} %get-tuple-element.46.refs_1_, ...), custom_call_target="tpu_custom_call" | custom-call | flops 1879048192 | bytes 5242880 | tf_op jit(solution)/shard_map/first_pair/pallas_call | solution.py:318
  60.5 1.4 %copy-done.2 = f32[512,1024]{1,0:T(8,128)} copy-done((f32[512,1024]{1,0:T(8,128)}, f32[512,1024]{1,0:T(8,128)S(1)}, u32[]{:S(2)}) %copy-start.2) | copy-done | bytes 2097176
  62.9 4.3 %last_pair.1 = (bf16[512,1024]{1,0:T(8,128)(2,1)S(1)}, bf16[512,1024]{1,0:T(8,128)(2,1)S(1)}, f32[512,512]{1,0:T(8,128)S(1)}) custom-call(f32[2]{0:T(128)S(1)} %pad_maximum_fusion.1.scalars, f32[1,512]{1,0:T(1,128)S(1)} %bitcast.54, f32[512,1]{1,0:T(8,128)S(1)} %copy.8.col_energy, bf16[512,256]{1,0:T(8,128)(2,1)S(1)} %get-tuple-element.44.refs_0_, ...), custom_call_target="tpu_custom_call" | custom-call | flops 1879048192 | bytes 8388608 | tf_op jit(solution)/shard_map/last_pair/pallas_call | solution.py:335
  67.2 2.7 %gamma.4 = (f32[256,512]{1,0:T(8,128)S(1)}, f32[1,1]{1,0:T(1,128)}) custom-call(bf16[4,256,1024]{2,1,0:T(8,128)(2,1)S(1)} %copy-done, bf16[4,256,1024]{2,1,0:T(8,128)(2,1)} %get-tuple-element.18.metric_low, bf16[512,1024]{1,0:T(8,128)(2,1)S(1)} %get-tuple-element.21.high, bf16[512,1024]{1,0:T(8,128)(2,1)S(1)} %get-tuple-element.22.low), custom_call_target="tpu_custom_call" | custom-call | flops 805306368 | bytes 3145728 | tf_op jit(solution)/shard_map/gamma/pallas_call | solution.py:357
  69.9 2.7 %gamma.5 = (f32[256,512]{1,0:T(8,128)S(1)}, f32[1,1]{1,0:T(1,128)}) custom-call(bf16[4,256,1024]{2,1,0:T(8,128)(2,1)S(1)} %copy-done, bf16[4,256,1024]{2,1,0:T(8,128)(2,1)} %get-tuple-element.18.metric_low, bf16[512,1024]{1,0:T(8,128)(2,1)S(1)} %get-tuple-element.21.high, bf16[512,1024]{1,0:T(8,128)(2,1)S(1)} %get-tuple-element.22.low), custom_call_target="tpu_custom_call" | custom-call | flops 805306368 | bytes 3145728 | tf_op jit(solution)/shard_map/gamma/pallas_call | solution.py:357
  74.0 2.7 %gamma.7 = (f32[256,512]{1,0:T(8,128)S(1)}, f32[1,1]{1,0:T(1,128)}) custom-call(bf16[4,256,1024]{2,1,0:T(8,128)(2,1)S(1)} %copy-done, bf16[4,256,1024]{2,1,0:T(8,128)(2,1)} %get-tuple-element.18.metric_low, bf16[512,1024]{1,0:T(8,128)(2,1)S(1)} %get-tuple-element.21.high, bf16[512,1024]{1,0:T(8,128)(2,1)S(1)} %get-tuple-element.22.low), custom_call_target="tpu_custom_call" | custom-call | flops 805306368 | bytes 3145728 | tf_op jit(solution)/shard_map/gamma/pallas_call | solution.py:357
  77.7 3.5 %collective-permute-start.12 = (f16[272,512]{1,0:T(8,128)(2,1)S(1)}, f16[272,512]{1,0:T(8,128)(2,1)S(1)}, u32[]{:S(2)}, u32[]{:S(2)}) collective-permute-start(f16[272,512]{1,0:T(8,128)(2,1)S(1)} %concatenate.27), channel_id=1, source_target_pairs={{0,0},{1,4},{2,2},{3,6},{4,1},{5,5},{6,3},{7,7},{8,8},{9,12},{10,1... | collective-permute-start | bytes 835592 | tf_op jit(solution)/shard_map/gamma/ppermute | solution.py:146
  81.4 2.7 %gamma.6 = (f32[256,512]{1,0:T(8,128)S(1)}, f32[1,1]{1,0:T(1,128)}) custom-call(bf16[4,256,1024]{2,1,0:T(8,128)(2,1)S(1)} %copy-done, bf16[4,256,1024]{2,1,0:T(8,128)(2,1)} %get-tuple-element.18.metric_low, bf16[512,1024]{1,0:T(8,128)(2,1)S(1)} %get-tuple-element.21.high, bf16[512,1024]{1,0:T(8,128)(2,1)S(1)} %get-tuple-element.22.low), custom_call_target="tpu_custom_call" | custom-call | flops 805306368 | bytes 3145728 | tf_op jit(solution)/shard_map/gamma/pallas_call | solution.py:357
  86.6 1.4 %collective-permute-start.18 = (f16[144,256]{1,0:T(8,128)(2,1)S(1)}, f16[144,256]{1,0:T(8,128)(2,1)S(1)}, u32[]{:S(2)}, u32[]{:S(2)}) collective-permute-start(f16[144,256]{1,0:T(8,128)(2,1)S(1)} %concatenate.32), channel_id=1, source_target_pairs={{0,16},{1,17},{2,18},{3,19},{4,20},{5,21},{6,22},{7,23},{8,24},{9,... | collective-permute-start | bytes 221192 | tf_op jit(solution)/shard_map/density/ppermute | solution.py:146
  88.0 2.3 %collective-permute-start.19 = (f16[144,256]{1,0:T(8,128)(2,1)S(1)}, f16[144,256]{1,0:T(8,128)(2,1)S(1)}, u32[]{:S(2)}, u32[]{:S(2)}) collective-permute-start(f16[144,256]{1,0:T(8,128)(2,1)S(1)} %concatenate.33), channel_id=1, source_target_pairs={{0,24},{1,25},{2,26},{3,27},{4,28},{5,29},{6,30},{7,31},{8,16},{9,... | collective-permute-start | bytes 221192 | tf_op jit(solution)/shard_map/density/ppermute | solution.py:146
  91.8 2.7 %collective-permute-start.15 = (f16[272,512]{1,0:T(8,128)(2,1)S(1)}, f16[272,512]{1,0:T(8,128)(2,1)S(1)}, u32[]{:S(2)}, u32[]{:S(2)}) collective-permute-start(f16[272,512]{1,0:T(8,128)(2,1)S(1)} %concatenate.30), channel_id=1, source_target_pairs={{0,3},{1,7},{2,1},{3,5},{4,2},{5,6},{6,0},{7,4},{8,11},{9,15},{10,... | collective-permute-start | bytes 835592 | tf_op jit(solution)/shard_map/gamma/ppermute | solution.py:146
  97.7 2.4 %collective-permute-start.21 = (f32[64,256]{1,0:T(8,128)S(1)}, f32[64,256]{1,0:T(8,128)S(1)}, u32[]{:S(2)}, u32[]{:S(2)}) collective-permute-start(f32[64,256]{1,0:T(8,128)S(1)} %get-tuple-element.48), channel_id=1, source_target_pairs={{0,4},{1,5},{2,6},{3,7},{4,0},{5,1},{6,2},{7,3},{8,12},{9,13},{10,... | collective-permute-start | bytes 196616 | tf_op jit(solution)/shard_map/density/ppermute | solution.py:146
  103.7 3.4 %collective-permute-done.15 = f16[272,512]{1,0:T(8,128)(2,1)S(1)} collective-permute-done((f16[272,512]{1,0:T(8,128)(2,1)S(1)}, f16[272,512]{1,0:T(8,128)(2,1)S(1)}, u32[]{:S(2)}, u32[]{:S(2)}) %collective-permute-start.15) | collective-permute-done | bytes 278560 | tf_op jit(solution)/shard_map/gamma/ppermute | solution.py:146
  109.8 1.3 %copy.9 = f32[256,1,512]{2,1,0:T(1,128)} copy(f32[256,1,512]{2,0,1:T(8,128)S(1)} %add_bitcast_fusion) | data formatting | bytes 1048576
  (77 shorter events, 18.0 us)
Async XLA Ops:
  0.6 8.5 %collective-permute-start.1 = (bf16[512,256]{1,0:T(8,128)(2,1)}, bf16[512,256]{1,0:T(8,128)(2,1)}, u32[]{:S(2)}, u32[]{:S(2)}) collective-permute-start(bf16[512,256]{1,0:T(8,128)(2,1)} %bitcast.11), channel_id=1, source_target_pairs={{0,2},{1,3},{2,0},{3,1},{4,6},{5,7},{6,4},{7,5},{8,10},{9,11},{10,... | collective-permute-start | bytes 786440 | tf_op jit(solution)/shard_map/gather/ppermute | solution.py:146
  2.8 7.5 %collective-permute-start = (bf16[512,256]{1,0:T(8,128)(2,1)}, bf16[512,256]{1,0:T(8,128)(2,1)S(1)}, u32[]{:S(2)}, u32[]{:S(2)}) collective-permute-start(bf16[512,256]{1,0:T(8,128)(2,1)} %bitcast.11), channel_id=1, source_target_pairs={{0,4},{1,5},{2,6},{3,7},{4,0},{5,1},{6,2},{7,3},{8,12},{9,13},{10,... | collective-permute-start | bytes 786440 | tf_op jit(solution)/shard_map/gather/ppermute | solution.py:146
  9.1 6.8 %collective-permute-start.2 = (bf16[512,256]{1,0:T(8,128)(2,1)}, bf16[512,256]{1,0:T(8,128)(2,1)S(1)}, u32[]{:S(2)}, u32[]{:S(2)}) collective-permute-start(bf16[512,256]{1,0:T(8,128)(2,1)} %collective-permute-done.1), channel_id=1, source_target_pairs={{0,4},{1,5},{2,6},{3,7},{4,0},{5,1},{6,2},{7,3},{8,12},{9,13},{10,... | collective-permute-start | bytes 786440 | tf_op jit(solution)/shard_map/gather/ppermute | solution.py:146
  16.9 40.7 %collective-permute-start.3 = (bf16[2,512,256]{2,1,0:T(8,128)(2,1)S(1)}, bf16[2,512,256]{2,1,0:T(8,128)(2,1)S(1)}, u32[]{:S(2)}, u32[]{:S(2)}) collective-permute-start(bf16[2,512,256]{2,1,0:T(8,128)(2,1)S(1)} %pad_maximum_fusion), channel_id=1, source_target_pairs={{0,1},{1,0},{2,3},{3,2},{4,5},{5,4},{6,7},{7,6},{8,9},{9,8},{10,11... | collective-permute-start | bytes 1572872 | tf_op jit(solution)/shard_map/gather/ppermute | solution.py:146
  19.2 18.9 %collective-permute-start.8 = (bf16[512,256]{1,0:T(8,128)(2,1)}, bf16[512,256]{1,0:T(8,128)(2,1)S(1)}, u32[]{:S(2)}, u32[]{:S(2)}) collective-permute-start(bf16[512,256]{1,0:T(8,128)(2,1)} %bitcast.11), channel_id=1, source_target_pairs={{0,8},{1,9},{2,2},{3,3},{4,12},{5,13},{6,6},{7,7},{8,0},{9,1},{10,... | collective-permute-start | bytes 786440 | tf_op jit(solution)/shard_map/gather/ppermute | solution.py:146
  22.3 21.4 %collective-permute-start.9 = (bf16[512,256]{1,0:T(8,128)(2,1)}, bf16[512,256]{1,0:T(8,128)(2,1)S(1)}, u32[]{:S(2)}, u32[]{:S(2)}) collective-permute-start(bf16[512,256]{1,0:T(8,128)(2,1)} %collective-permute-done.1), channel_id=1, source_target_pairs={{0,8},{1,9},{2,2},{3,3},{4,12},{5,13},{6,6},{7,7},{8,0},{9,1},{10,... | collective-permute-start | bytes 786440 | tf_op jit(solution)/shard_map/gather/ppermute | solution.py:146
  24.4 32.7 %collective-permute-start.4 = (bf16[512,256]{1,0:T(8,128)(2,1)}, bf16[512,256]{1,0:T(8,128)(2,1)S(1)}, u32[]{:S(2)}, u32[]{:S(2)}) collective-permute-start(bf16[512,256]{1,0:T(8,128)(2,1)} %bitcast.11), channel_id=1, source_target_pairs={{0,16},{1,17},{2,26},{3,27},{4,20},{5,21},{6,30},{7,31},{8,24},{9,... | collective-permute-start | bytes 786440 | tf_op jit(solution)/shard_map/gather/ppermute | solution.py:146
  26.7 30.4 %collective-permute-start.5 = (bf16[512,256]{1,0:T(8,128)(2,1)}, bf16[512,256]{1,0:T(8,128)(2,1)S(1)}, u32[]{:S(2)}, u32[]{:S(2)}) collective-permute-start(bf16[512,256]{1,0:T(8,128)(2,1)} %collective-permute-done.1), channel_id=1, source_target_pairs={{0,16},{1,17},{2,26},{3,27},{4,20},{5,21},{6,30},{7,31},{8,24},{9,... | collective-permute-start | bytes 786440 | tf_op jit(solution)/shard_map/gather/ppermute | solution.py:146
  38.0 19.6 %collective-permute-start.10 = (bf16[512,256]{1,0:T(8,128)(2,1)S(1)}, bf16[512,256]{1,0:T(8,128)(2,1)S(1)}, u32[]{:S(2)}, u32[]{:S(2)}) collective-permute-start(bf16[512,256]{1,0:T(8,128)(2,1)S(1)} %collective-permute-done.8.refs_4_), channel_id=1, source_target_pairs={{0,1},{1,0},{2,3},{3,2},{4,5},{5,4},{6,7},{7,6},{8,9},{9,8},{10,11... | collective-permute-start | bytes 786440 | tf_op jit(solution)/shard_map/gather/ppermute | solution.py:146
  43.7 14.0 %collective-permute-start.11 = (bf16[512,256]{1,0:T(8,128)(2,1)S(1)}, bf16[512,256]{1,0:T(8,128)(2,1)S(1)}, u32[]{:S(2)}, u32[]{:S(2)}) collective-permute-start(bf16[512,256]{1,0:T(8,128)(2,1)S(1)} %collective-permute-done.9.refs_5_), channel_id=1, source_target_pairs={{0,1},{1,0},{2,3},{3,2},{4,5},{5,4},{6,7},{7,6},{8,9},{9,8},{10,11... | collective-permute-start | bytes 786440 | tf_op jit(solution)/shard_map/gather/ppermute | solution.py:146
  57.1 5.8 %collective-permute-start.6 = (bf16[512,256]{1,0:T(8,128)(2,1)S(1)}, bf16[512,256]{1,0:T(8,128)(2,1)S(1)}, u32[]{:S(2)}, u32[]{:S(2)}) collective-permute-start(bf16[512,256]{1,0:T(8,128)(2,1)S(1)} %collective-permute-done.4.refs_4_), channel_id=1, source_target_pairs={{0,1},{1,0},{2,3},{3,2},{4,5},{5,4},{6,7},{7,6},{8,9},{9,8},{10,11... | collective-permute-start | bytes 786440 | tf_op jit(solution)/shard_map/gather/ppermute | solution.py:146
  57.1 5.7 %collective-permute-start.7 = (bf16[512,256]{1,0:T(8,128)(2,1)S(1)}, bf16[512,256]{1,0:T(8,128)(2,1)S(1)}, u32[]{:S(2)}, u32[]{:S(2)}) collective-permute-start(bf16[512,256]{1,0:T(8,128)(2,1)S(1)} %collective-permute-done.5.refs_5_), channel_id=1, source_target_pairs={{0,1},{1,0},{2,3},{3,2},{4,5},{5,4},{6,7},{7,6},{8,9},{9,8},{10,11... | collective-permute-start | bytes 786440 | tf_op jit(solution)/shard_map/gather/ppermute | solution.py:146
  77.4 7.5 %collective-permute-start.16 = (f32[512,256]{1,0:T(8,128)S(1)}, f32[512,256]{1,0:T(8,128)S(1)}, u32[]{:S(2)}, u32[]{:S(2)}) collective-permute-start(f32[512,256]{1,0:T(8,128)S(1)} %constant_dynamic-slice_fusion.2), channel_id=1, source_target_pairs={{0,1},{1,0},{2,3},{3,2},{4,5},{5,4},{6,7},{7,6},{8,9},{9,8},{10,11... | collective-permute-start | bytes 1572872 | tf_op jit(solution)/shard_map/density/ppermute | solution.py:146
  77.7 20.0 %collective-permute-start.12 = (f16[272,512]{1,0:T(8,128)(2,1)S(1)}, f16[272,512]{1,0:T(8,128)(2,1)S(1)}, u32[]{:S(2)}, u32[]{:S(2)}) collective-permute-start(f16[272,512]{1,0:T(8,128)(2,1)S(1)} %concatenate.27), channel_id=1, source_target_pairs={{0,0},{1,4},{2,2},{3,6},{4,1},{5,5},{6,3},{7,7},{8,8},{9,12},{10,1... | collective-permute-start | bytes 835592 | tf_op jit(solution)/shard_map/gamma/ppermute | solution.py:146
  81.4 18.7 %collective-permute-start.13 = (f16[272,512]{1,0:T(8,128)(2,1)S(1)}, f16[272,512]{1,0:T(8,128)(2,1)S(1)}, u32[]{:S(2)}, u32[]{:S(2)}) collective-permute-start(f16[272,512]{1,0:T(8,128)(2,1)S(1)} %concatenate.28), channel_id=1, source_target_pairs={{0,1},{1,5},{2,3},{3,7},{4,0},{5,4},{6,2},{7,6},{8,9},{9,13},{10,1... | collective-permute-start | bytes 835592 | tf_op jit(solution)/shard_map/gamma/ppermute | solution.py:146
  86.5 4.0 %collective-permute-start.17 = (f16[144,256]{1,0:T(8,128)(2,1)S(1)}, f16[144,256]{1,0:T(8,128)(2,1)S(1)}, u32[]{:S(2)}, u32[]{:S(2)}) collective-permute-start(f16[144,256]{1,0:T(8,128)(2,1)S(1)} %concatenate.31), channel_id=1, source_target_pairs={{0,8},{1,9},{2,10},{3,11},{4,12},{5,13},{6,14},{7,15},{8,0},{9,1},... | collective-permute-start | bytes 221192 | tf_op jit(solution)/shard_map/density/ppermute | solution.py:146
  86.6 5.2 %collective-permute-start.18 = (f16[144,256]{1,0:T(8,128)(2,1)S(1)}, f16[144,256]{1,0:T(8,128)(2,1)S(1)}, u32[]{:S(2)}, u32[]{:S(2)}) collective-permute-start(f16[144,256]{1,0:T(8,128)(2,1)S(1)} %concatenate.32), channel_id=1, source_target_pairs={{0,16},{1,17},{2,18},{3,19},{4,20},{5,21},{6,22},{7,23},{8,24},{9,... | collective-permute-start | bytes 221192 | tf_op jit(solution)/shard_map/density/ppermute | solution.py:146
  88.0 7.6 %collective-permute-start.19 = (f16[144,256]{1,0:T(8,128)(2,1)S(1)}, f16[144,256]{1,0:T(8,128)(2,1)S(1)}, u32[]{:S(2)}, u32[]{:S(2)}) collective-permute-start(f16[144,256]{1,0:T(8,128)(2,1)S(1)} %concatenate.33), channel_id=1, source_target_pairs={{0,24},{1,25},{2,26},{3,27},{4,28},{5,29},{6,30},{7,31},{8,16},{9,... | collective-permute-start | bytes 221192 | tf_op jit(solution)/shard_map/density/ppermute | solution.py:146
  90.5 12.0 %collective-permute-start.14 = (f16[272,512]{1,0:T(8,128)(2,1)S(1)}, f16[272,512]{1,0:T(8,128)(2,1)S(1)}, u32[]{:S(2)}, u32[]{:S(2)}) collective-permute-start(f16[272,512]{1,0:T(8,128)(2,1)S(1)} %concatenate.29), channel_id=1, source_target_pairs={{0,2},{1,6},{2,0},{3,4},{4,3},{5,7},{6,1},{7,5},{8,10},{9,14},{10,... | collective-permute-start | bytes 835592 | tf_op jit(solution)/shard_map/gamma/ppermute | solution.py:146
  91.8 15.3 %collective-permute-start.15 = (f16[272,512]{1,0:T(8,128)(2,1)S(1)}, f16[272,512]{1,0:T(8,128)(2,1)S(1)}, u32[]{:S(2)}, u32[]{:S(2)}) collective-permute-start(f16[272,512]{1,0:T(8,128)(2,1)S(1)} %concatenate.30), channel_id=1, source_target_pairs={{0,3},{1,7},{2,1},{3,5},{4,2},{5,6},{6,0},{7,4},{8,11},{9,15},{10,... | collective-permute-start | bytes 835592 | tf_op jit(solution)/shard_map/gamma/ppermute | solution.py:146
  97.0 11.3 %collective-permute-start.20 = (f32[64,256]{1,0:T(8,128)S(1)}, f32[64,256]{1,0:T(8,128)S(1)}, u32[]{:S(2)}, u32[]{:S(2)}) collective-permute-start(f32[64,256]{1,0:T(8,128)S(1)} %get-tuple-element.47), channel_id=1, source_target_pairs={{0,2},{1,3},{2,0},{3,1},{4,6},{5,7},{6,4},{7,5},{8,10},{9,11},{10,... | collective-permute-start | bytes 196616 | tf_op jit(solution)/shard_map/density/ppermute | solution.py:146
  97.7 10.6 %collective-permute-start.21 = (f32[64,256]{1,0:T(8,128)S(1)}, f32[64,256]{1,0:T(8,128)S(1)}, u32[]{:S(2)}, u32[]{:S(2)}) collective-permute-start(f32[64,256]{1,0:T(8,128)S(1)} %get-tuple-element.48), channel_id=1, source_target_pairs={{0,4},{1,5},{2,6},{3,7},{4,0},{5,1},{6,2},{7,3},{8,12},{9,13},{10,... | collective-permute-start | bytes 196616 | tf_op jit(solution)/shard_map/density/ppermute | solution.py:146
  100.1 8.7 %collective-permute-start.22 = (f32[64,256]{1,0:T(8,128)S(1)}, f32[64,256]{1,0:T(8,128)S(1)}, u32[]{:S(2)}, u32[]{:S(2)}) collective-permute-start(f32[64,256]{1,0:T(8,128)S(1)} %get-tuple-element.48), channel_id=1, source_target_pairs={{0,6},{1,7},{2,4},{3,5},{4,2},{5,3},{6,0},{7,1},{8,14},{9,15},{10,... | collective-permute-start | bytes 196616 | tf_op jit(solution)/shard_map/density/ppermute | solution.py:146
  108.8 2.3 %collective-permute-start.23 = (f32[64,256]{1,0:T(8,128)S(1)}, f32[64,256]{1,0:T(8,128)S(1)}, u32[]{:S(2)}, u32[]{:S(2)}) collective-permute-start(f32[64,256]{1,0:T(8,128)S(1)} %add_add_fusion), channel_id=1, source_target_pairs={{0,1},{1,0},{2,3},{3,2},{4,5},{5,4},{6,7},{7,6},{8,9},{9,8},{10,11... | collective-permute-start | bytes 196616 | tf_op jit(solution)/shard_map/density/ppermute | solution.py:146
  (5 other events, 76.9 us)

commit v2 on v0

--- a/solution.py
+++ b/solution.py
@@ -1,6 +1,8 @@
 import jax
 import jax.numpy as jnp
 from jax import lax
+from jax.experimental import pallas as pl
+from jax.experimental.pallas import tpu as pltpu
 from jax.sharding import PartitionSpec as P
 
 CYCLE_STEPS = 4
@@ -57,7 +59,7 @@
     return lax.fori_loop(0, per_batch * per_batch, one_pair, (acc_own, acc_part, density))
 
 
-def per_device(factors, occ_energy, vir_energy, metric):
+def general_device(factors, occ_energy, vir_energy, metric):
     n_blk = lax.axis_size("blk")
     n_sec = lax.axis_size("sec")
     blk_pos = lax.axis_index("blk")
@@ -117,7 +119,389 @@
     return (gamma_part, density_out)
 
 
+AXES = ("blk", "sec")
+NT = (((1,), (1,)), ((), ()))
+NN = (((1,), (0,)), ((), ()))
+TAIL_ROWS = 16
+VMEM_LIMIT = 20 * 1024 * 1024
+
+
+def dot(left, right, dims):
+    return lax.dot_general(left, right, dims, preferred_element_type=jnp.float32)
+
+
+def split_bits(device, n_sec):
+    blk, sec = device // n_sec, device % n_sec
+    return blk // 2, blk % 2, sec // 2, sec % 2
+
+
+def join_bits(z, y, x, c, n_sec):
+    return (2 * z + y) * n_sec + 2 * x + c
+
+
+def send(value, target, n_blk, n_sec):
+    pairs = []
+    for device in range(n_blk * n_sec):
+        pairs.append((device, join_bits(*target(*split_bits(device, n_sec)), n_sec)))
+    return lax.ppermute(value, AXES, pairs)
+
+
+def encode(value):
+    peak = jnp.max(jnp.abs(value), keepdims=True)
+    power = jnp.floor(15.4 - jnp.log2(jnp.maximum(peak, 1e-36)))
+    power = jnp.clip(power, -120.0, 120.0)
+    scaled = value * jnp.exp2(power)
+    second = scaled * scaled
+    fourth = second * second
+    eighth = fourth * fourth
+    coded = jnp.where(scaled < 0.0, -eighth, eighth).astype(jnp.bfloat16)
+    tail = jnp.broadcast_to(power, (TAIL_ROWS, value.shape[1])).astype(jnp.bfloat16)
+    return coded, tail
+
+
+def encode_into(out, value):
+    rows = value.shape[0]
+    coded, tail = encode(value)
+    out[:rows] = coded
+    out[rows:] = tail
+
+
+def decode(ref):
+    rows = ref.shape[0] - TAIL_ROWS
+    power = ref[rows:].astype(jnp.float32)[:1]
+    coded = ref[:rows].astype(jnp.float32)
+    root = jnp.sqrt(jnp.sqrt(jnp.sqrt(jnp.abs(coded)))) * jnp.exp2(-power)
+    return jnp.where(coded < 0.0, -root, root)
+
+
+def pair_terms(sum_energy, weight, row_energy, col_energy, left, right):
+    straight = dot(left[0], right[0], NT)
+    turned = dot(right[0], left[0], NT)
+    for part in range(1, len(left)):
+        straight += dot(left[part], right[part], NT)
+        turned += dot(right[part], left[part], NT)
+    amplitude = straight / (sum_energy - col_energy - row_energy)
+    amplitude_t = turned / (sum_energy - row_energy - col_energy)
+    mixed = (2.0 * amplitude - amplitude_t) * weight
+    return amplitude.astype(jnp.bfloat16), mixed.astype(jnp.bfloat16)
+
+
+def first_pair_kernel(scalars, row_energy, col_energy, *refs):
+    left = [ref[...] for ref in refs[:4]]
+    right = [ref[...] for ref in refs[4:8]]
+    grad_out, amp_out, mixed_out = refs[8:]
+    amp_half, mixed_half = pair_terms(
+        scalars[0], scalars[1], row_energy[...], col_energy[...], left, right
+    )
+    width = right[0].shape[1]
+    for part in range(4):
+        grad_out[:, part * width : (part + 1) * width] = dot(mixed_half, right[part], NN)
+    amp_out[...] = amp_half
+    mixed_out[...] = mixed_half
+
+
+def last_pair_kernel(place, scalars, row_energy, col_energy, *refs):
+    left = [ref[...] for ref in refs[:4]]
+    right = [ref[...] for ref in refs[4:8]]
+    grad_in, first_amp, first_mixed = refs[8:11]
+    high_out, low_out, dens_keep, dens_send, amp = refs[11:]
+    amp_half, mixed_half = pair_terms(
+        scalars[0], scalars[1], row_energy[...], col_energy[...], left, right
+    )
+    amp[...] = amp_half
+    half = amp.shape[0] // 2
+    mixed_first = first_mixed[...]
+    for out, core in ((dens_send, 1 - place[0]), (dens_keep, place[0])):
+        rows = pl.ds(pl.multiple_of(core * half, half), half)
+        out[...] = dot(mixed_half, amp[rows, :], NT) + dot(mixed_first, first_amp[rows, :], NT)
+    width = right[0].shape[1]
+    for part in range(4):
+        cols = slice(part * width, (part + 1) * width)
+        grad = grad_in[:, cols] + dot(mixed_half, right[part], NN)
+        high = grad.astype(jnp.bfloat16)
+        high_out[:, cols] = high
+        low_out[:, cols] = (grad - high.astype(jnp.float32)).astype(jnp.bfloat16)
+
+
+def metric_kernel(metric_high, metric_low, high, low, out):
+    metric_top = metric_high[0]
+    block = dot(metric_top, high[...], NT)
+    block += dot(metric_top, low[...], NT)
+    block += dot(metric_low[0], high[...], NT)
+    encode_into(out, block)
+
+
+def turn_metric_kernel(order, metric, high, low):
+    width = metric.shape[1]
+    row = lax.broadcasted_iota(jnp.int32, (width, width), 0)
+    col = lax.broadcasted_iota(jnp.int32, (width, width), 1)
+    unit = jnp.where(row == col, 1.0, 0.0).astype(jnp.bfloat16)
+    for part in range(metric.shape[0] // width):
+        rows = pl.ds(pl.multiple_of(order[part] * width, width), width)
+        cols = slice(part * width, (part + 1) * width)
+        value = metric[rows, :]
+        top = value.astype(jnp.bfloat16)
+        rest = (value - top.astype(jnp.float32)).astype(jnp.bfloat16)
+        high[0, :, cols] = dot(unit, top, NT).astype(jnp.bfloat16)
+        low[0, :, cols] = dot(unit, rest, NT).astype(jnp.bfloat16)
+
+
+def gamma_sum_kernel(*refs):
+    out = refs[-1]
+    total = decode(refs[0])
+    for ref in refs[1:-1]:
+        total += decode(ref)
+    out[:, 0, :] = total
+
+
+def density_layers_kernel(place, keep, got, layer, *outs):
+    rows = layer.shape[0]
+    here = pl.ds(pl.multiple_of(place[1] * rows, rows), rows)
+    layer[...] = keep[here, :] + got[here, :]
+    for step, out in enumerate(outs, 1):
+        there = pl.ds(pl.multiple_of((place[1] ^ step) * rows, rows), rows)
+        encode_into(out, keep[there, :] + got[there, :])
+
+
+def density_rows_kernel(place, layer, *refs):
+    mine, theirs, total = refs[-3:]
+    value = layer[...]
+    for ref in refs[:-3]:
+        value += decode(ref)
+    total[...] = value
+    rows = mine.shape[0]
+    mine[...] = total[pl.ds(pl.multiple_of(place[2] * rows, rows), rows), :]
+    theirs[...] = total[pl.ds(pl.multiple_of((1 - place[2]) * rows, rows), rows), :]
+
+
+def fast_device(factors, occ_energy, vir_energy, metric):
+    n_blk = lax.axis_size("blk")
+    n_sec = lax.axis_size("sec")
+    blk_pos = lax.axis_index("blk")
+    sec_pos = lax.axis_index("sec")
+    z, y = blk_pos // 2, blk_pos % 2
+    x, c = sec_pos // 2, sec_pos % 2
+    n_lay = n_blk // 2
+    own = factors[0]
+    virtuals, width = own.shape
+    aux_total = width * n_sec
+    half = virtuals // 2
+    place = jnp.stack([c, z, y]).astype(jnp.int32)
+
+    def move(value, target):
+        return send(value, target, n_blk, n_sec)
+
+    def core_swap(value):
+        return move(value, lambda z, y, x, c: (z, y, x, 1 - c))
+
+    def x_swap(value):
+        return move(value, lambda z, y, x, c: (z, y, 1 - x, c))
+
+    def y_swap(value):
+        return move(value, lambda z, y, x, c: (z, 1 - y, x, c))
+
+    def xy_swap(value):
+        return move(value, lambda z, y, x, c: (z, 1 - y, 1 - x, c))
+
+    def first_partner(value):
+        return move(value, lambda z, y, x, c: (z if x else z ^ 1, y, x, c))
+
+    def last_partner(value):
+        return move(value, lambda z, y, x, c: (z ^ 3 if x else z ^ 2, y, x, c))
+
+    smem = pl.BlockSpec(memory_space=pltpu.SMEM)
+    vmem = pl.BlockSpec(memory_space=pltpu.VMEM)
+    params = pltpu.CompilerParams(vmem_limit_bytes=VMEM_LIMIT)
+    square = 2 * virtuals * virtuals
+    grad_shape = (virtuals, aux_total)
+
+    def cost(flops, size):
+        return pl.CostEstimate(flops=flops, bytes_accessed=size, transcendentals=0)
+
+    def shape(rows, cols, dtype):
+        return jax.ShapeDtypeStruct((rows, cols), dtype)
+
+    with jax.named_scope("metric_turn"):
+        order = jnp.stack(
+            [sec_pos, sec_pos ^ 2, sec_pos ^ 1, sec_pos ^ 3]
+            + [2 * (x ^ (step >> 1)) + (y ^ (step & 1)) for step in range(4)]
+        ).astype(jnp.int32)
+        turned = jax.ShapeDtypeStruct((4, width, aux_total), jnp.bfloat16)
+        turned_spec = pl.BlockSpec((1, width, aux_total), lambda r, order: (r, 0, 0))
+        metric_high, metric_low = pl.pallas_call(
+            turn_metric_kernel,
+            grid_spec=pltpu.PrefetchScalarGridSpec(
+                num_scalar_prefetch=1,
+                grid=(4,),
+                in_specs=[pl.BlockSpec((aux_total, width), lambda r, order: (0, order[4 + r]))],
+                out_specs=[turned_spec, turned_spec],
+            ),
+            out_shape=[turned, turned],
+            cost_estimate=cost(4 * aux_total * aux_total * width, 8 * aux_total**2),
+        )(order, metric)
+
+    with jax.named_scope("gather"):
+        last_own = last_partner(own)
+        swapped = x_swap(own)
+        first_own = first_partner(own)
+        other_own = y_swap(own)
+        other_swapped = xy_swap(own)
+        swapped, other_own, other_swapped, first_own, last_own, metric_high, metric_low = (
+            lax.optimization_barrier(
+                (
+                    swapped,
+                    other_own,
+                    other_swapped,
+                    first_own,
+                    last_own,
+                    metric_high,
+                    metric_low,
+                )
+            )
+        )
+        last_swapped = last_partner(swapped)
+        first_swapped = first_partner(swapped)
+        first_own_other = core_swap(first_own)
+        last_own_other = core_swap(last_own)
+        at_home = c == y
+        left_mine = [
+            jnp.where(at_home, own, other_own),
+            jnp.where(at_home, swapped, other_swapped),
+        ]
+        left_sent = [
+            jnp.where(at_home, other_own, own),
+            jnp.where(at_home, other_swapped, swapped),
+        ]
+        left = left_mine + [core_swap(left_sent[0]), core_swap(left_sent[1])]
+        first = [first_own, first_swapped, first_own_other, core_swap(first_swapped)]
+        last = [last_own, last_swapped, last_own_other, core_swap(last_swapped)]
+
+    home_energy = lax.dynamic_index_in_dim(occ_energy, 2 * z + c, 0, keepdims=False)
+
+    def energy_of(layer):
+        return lax.dynamic_index_in_dim(occ_energy, 2 * layer + y, 0, keepdims=False)
+
+    first_layer = jnp.where(x == 1, z, z ^ 1)
+    last_layer = jnp.where(x == 1, z ^ 3, z ^ 2)
+    first_scalars = jnp.stack([home_energy + energy_of(first_layer), jnp.float32(1.0)])
+    last_weight = jnp.where((x == 0) & (c == y), jnp.float32(0.0), jnp.float32(1.0))
+    last_scalars = jnp.stack([home_energy + energy_of(last_layer), last_weight])
+    row_energy, col_energy = vir_energy[None, :], vir_energy[:, None]
+
+    with jax.named_scope("first_pair"):
+        grad, first_amp, first_mixed = pl.pallas_call(
+            first_pair_kernel,
+            in_specs=[smem] + [vmem] * 10,
+            out_specs=[vmem] * 3,
+            out_shape=[
+                shape(virtuals, aux_total, jnp.float32),
+                shape(virtuals, virtuals, jnp.bfloat16),
+                shape(virtuals, virtuals, jnp.bfloat16),
+            ],
+            compiler_params=params,
+            cost_estimate=cost(3 * square * aux_total, 8 * virtuals * aux_total),
+        )(first_scalars, row_energy, col_energy, *left, *first)
+
+    with jax.named_scope("last_pair"):
+        high, low, dens_keep, dens_send = pl.pallas_call(
+            last_pair_kernel,
+            in_specs=[smem] * 2 + [vmem] * 13,
+            out_specs=[vmem] * 4,
+            out_shape=[
+                shape(virtuals, aux_total, jnp.bfloat16),
+                shape(virtuals, aux_total, jnp.bfloat16),
+                shape(virtuals, half, jnp.float32),
+                shape(virtuals, half, jnp.float32),
+            ],
+            scratch_shapes=[pltpu.VMEM((virtuals, virtuals), jnp.bfloat16)],
+            compiler_params=params,
+            cost_estimate=cost(square * (3 * aux_total + 2 * virtuals), 12 * virtuals * aux_total),
+        )(
+            place,
+            last_scalars,
+            row_energy,
+            col_energy,
+            *left,
+            *last,
+            grad,
+            first_amp,
+            first_mixed,
+        )
+
+    def gamma_block(step, high):
+        metric_spec = pl.BlockSpec((1, width, aux_total), lambda i: (step, 0, 0))
+        whole = pl.BlockSpec(grad_shape, lambda i: (0, 0))
+        packed = pl.pallas_call(
+            metric_kernel,
+            grid=(1,),
+            in_specs=[metric_spec, metric_spec, whole, whole],
+            out_specs=pl.BlockSpec((width + TAIL_ROWS, virtuals), lambda i: (0, 0)),
+            out_shape=shape(width + TAIL_ROWS, virtuals, jnp.bfloat16),
+            compiler_params=params,
+            cost_estimate=cost(
+                6 * width * virtuals * aux_total, 4 * (width + virtuals) * aux_total
+            ),
+        )(metric_high, metric_low, high, low)
+        return move(packed, lambda z, y, x, c: (z, c, x ^ (step >> 1), y ^ (step & 1)))
+
+    layer_rows = virtuals // n_lay
+    rows = virtuals // n_blk
+    with jax.named_scope("gamma"):
+        got_third = gamma_block(3, high)
+    with jax.named_scope("density"):
+        dens_got = core_swap(dens_send)
+        coded = shape(layer_rows + TAIL_ROWS, half, jnp.bfloat16)
+        layer, *messages = pl.pallas_call(
+            density_layers_kernel,
+            in_specs=[smem, vmem, vmem],
+            out_specs=[vmem] * n_lay,
+            out_shape=[shape(layer_rows, half, jnp.float32)] + [coded] * (n_lay - 1),
+            compiler_params=params,
+        )(place, dens_keep, dens_got)
+        messages = [
+            move(message, lambda z, y, x, c, step=step: (z ^ step, y, x, c))
+            for step, message in enumerate(messages, 1)
+        ]
+    with jax.named_scope("gamma"):
+        got_second = gamma_block(2, high)
+        got_first = gamma_block(1, high)
+        got_zeroth = gamma_block(0, high)
+    with jax.named_scope("density"):
+        mine, theirs = pl.pallas_call(
+            density_rows_kernel,
+            in_specs=[smem] + [vmem] * n_lay,
+            out_specs=[vmem, vmem],
+            out_shape=[shape(rows, half, jnp.float32)] * 2,
+            scratch_shapes=[pltpu.VMEM((layer_rows, half), jnp.float32)],
+            compiler_params=params,
+        )(place, layer, *messages)
+        from_x, from_y, from_xy = x_swap(mine), y_swap(theirs), xy_swap(theirs)
+        block = (mine + from_x) + (from_y + from_xy)
+        other = core_swap(block)
+        density = jnp.where(
+            c == 0,
+            jnp.concatenate([block, other], 1),
+            jnp.concatenate([other, block], 1),
+        )
+    with jax.named_scope("gamma"):
+        gamma = pl.pallas_call(
+            gamma_sum_kernel,
+            in_specs=[vmem] * 4,
+            out_specs=vmem,
+            out_shape=jax.ShapeDtypeStruct((width, 1, virtuals), jnp.float32),
+            compiler_params=params,
+        )(got_third, got_second, got_first, got_zeroth)
+    return gamma, density
+
+
 def solution(mesh):
+    n_blk, n_sec = mesh.shape["blk"], mesh.shape["sec"]
+
+    def per_device(factors, occ_energy, vir_energy, metric):
+        two_rows_of_layers = n_sec == 4 and n_blk == 2 * n_sec and factors.shape[0] == 1
+        step = fast_device if two_rows_of_layers else general_device
+        return step(factors, occ_energy, vir_energy, metric)
+
     return jax.shard_map(
         per_device,
         mesh=mesh,

time: 251 us -> 81.2 us (0.32); the launches traced: 248 us -> 80.9 us
  waiting for transfers between devices: 173 us -> 21.4 us
  Pallas kernels: 0 us -> 22.1 us
  matrix products: 19.6 us -> 0 us
  between operations: 15.2 us -> 3.55 us
  local copies, waits for them, and re-layouts: 13.5 us -> 2.26 us
  starting transfers between devices: 21.5 us -> 29.8 us
  other arithmetic: 5.21 us -> 1.73 us
    reduce_scatter x2 -> x0, waiting for transfers between devices: 58.6 us -> none  [the longest x1 34.7 us: per_device(): lax.psum_scatter(own_term + jnp.einsum('pq,ipa->qia', metric_rows, carrie...]
    all_to_all x2 -> x0, waiting for transfers between devices: 33.7 us -> none  [the longest x1 22 us: per_device(): lax.all_to_all(acc_part[None], 'sec', split_axis=2, concat_axis=0, tiled=...]
    psum x1 -> x0, waiting for transfers between devices: 30.2 us -> none  [per_device(): density_out = lax.psum(density_rows, 'sec')]
    ppermute x6 -> x25, waiting for transfers between devices: 50.5 us -> 21.4 us  [send(): return lax.ppermute(value, AXES, pairs)]
    pallas_call x0 -> x10, Pallas kernels: none -> 22.1 us  [the longest x1 6.49 us: fast_device(): pl.pallas_call(turn_metric_kernel, grid_spec=pltpu.PrefetchScalarGridSpec...]
    dot_general x7 -> x0, matrix products: 19.6 us -> none  [the longest x1 6.83 us: per_device(): jnp.einsum('pq,ipa->qia', metric, acc_own, precision=lax.Precision.HIGHEST)]
    ppermute x6 -> x25, starting transfers between devices: 10.4 us -> 29.8 us  [send(): return lax.ppermute(value, AXES, pairs)]
    all_to_all x2 -> x0, starting transfers between devices: 11 us -> none  [the longest x1 6.55 us: per_device(): lax.all_to_all(jnp.stack(segmented, 0), 'sec', split_axis=0, concat_axis=...]
  transfers between devices with their start and end apart: 12 -> 25, of which waited for: 11 -> 6; matrix products, arithmetic and copies ran while one was open for 10% -> 4% of each run, Pallas kernels for 0% -> 24%
where the time goes in v2:
time: 81.2 us; the launch traced here: 80.9 us
  starting transfers between devices  29.8 us (37%)
  Pallas kernels  22.1 us (27%)
  waiting for transfers between devices  21.4 us (26%)
  between operations  3.55 us (4%)
  local copies, waits for them, and re-layouts  2.26 us (3%)
  other arithmetic  1.73 us (2%)
    ppermute x25, starting transfers between devices, send(): return lax.ppermute(value, AXES, pairs)  29.8 us
    ppermute x25, waiting for transfers between devices, send(): return lax.ppermute(value, AXES, pairs)  21.4 us
    pallas_call x1, Pallas kernels, fast_device(): pl.pallas_call(turn_metric_kernel, grid_spec=pltpu.PrefetchScalarGridSpec...  6.49 us
    pallas_call x4, Pallas kernels, gamma_block(): pl.pallas_call(metric_kernel, grid=(1,), in_specs=[metric_spec, metric_sp...  5.35 us
    pallas_call x1, Pallas kernels, fast_device(): pl.pallas_call(last_pair_kernel, in_specs=[smem] * 2 + [vmem] * 13, out_s...  3.09 us
    pallas_call x1, Pallas kernels, fast_device(): pl.pallas_call(gamma_sum_kernel, in_specs=[vmem] * 4, out_specs=vmem, out...  2.78 us
    pallas_call x1, Pallas kernels, fast_device(): pl.pallas_call(first_pair_kernel, in_specs=[smem] + [vmem] * 10, out_spec...  2.6 us
  transfers between devices with their start and end apart: 25, of which 6 were waited for; matrix products, arithmetic and copies ran while one was open for 4% of the time, Pallas kernels for 24%

profile of v2, /device:TPU:1, one launch (start us, length us, event | category | flops | bytes accessed | tf_op | source)
XLA Modules:
  0.0 80.9 jit_solution(11418441354537152022)
XLA Ops:
  0.6 3.2 %collective-permute-start.4 = (bf16[512,256]{1,0:T(8,128)(2,1)}, bf16[512,256]{1,0:T(8,128)(2,1)S(1)}, u32[]{:S(2)}, u32[]{:S(2)}) collective-permute-start(bf16[512,256]{1,0:T(8,128)(2,1)} %bitcast.20), channel_id=1, source_target_pairs={{0,16},{1,17},{2,26},{3,27},{4,20},{5,21},{6,30},{7,31},{8,24},{9,... | collective-permute-start | bytes 786440 | tf_op jit(solution)/shard_map/gather/ppermute | solution.py:146
  3.8 3.2 %collective-permute-start.3 = (bf16[512,256]{1,0:T(8,128)(2,1)}, bf16[512,256]{1,0:T(8,128)(2,1)S(1)}, u32[]{:S(2)}, u32[]{:S(2)}) collective-permute-start(bf16[512,256]{1,0:T(8,128)(2,1)} %bitcast.21), channel_id=1, source_target_pairs={{0,8},{1,9},{2,2},{3,3},{4,12},{5,13},{6,6},{7,7},{8,0},{9,1},{10,... | collective-permute-start | bytes 786440 | tf_op jit(solution)/shard_map/gather/ppermute | solution.py:146
  7.0 1.6 %collective-permute-start.2 = (bf16[512,256]{1,0:T(8,128)(2,1)}, bf16[512,256]{1,0:T(8,128)(2,1)S(1)}, u32[]{:S(2)}, u32[]{:S(2)}) collective-permute-start(bf16[512,256]{1,0:T(8,128)(2,1)} %bitcast.22), channel_id=1, source_target_pairs={{0,6},{1,7},{2,4},{3,5},{4,2},{5,3},{6,0},{7,1},{8,14},{9,15},{10,... | collective-permute-start | bytes 786440 | tf_op jit(solution)/shard_map/gather/ppermute | solution.py:146
  9.8 1.4 %fusion = (f32[1]{0:T(128)}, f32[1]{0:T(128)}, f32[1]{0:T(128)}) fusion(f32[8]{0:T(128)} %param.5, s32[]{:T(128)S(6)} %select_n.80, s32[]{:T(128)S(6)} %select_n.70, s32[]{:T(128)S(6)} %select_n.72), kind=kLoop, calls=%fused_computation.9 | loop fusion | bytes 36 | tf_op jit(solution)/shard_map/jit(dynamic_index_in_dim)/dynamic_slice | solution.py:382
  13.1 6.5 %metric_turn.1 = (bf16[4,256,1024]{2,1,0:T(8,128)(2,1)}, bf16[4,256,1024]{2,1,0:T(8,128)(2,1)}) custom-call(s32[8]{0:T(128)} %stack.58.order, f32[1024,1024]{1,0:T(8,128)} %metric.1), custom_call_target="tpu_custom_call" | custom-call | flops 1073741824 | bytes 8388608 | tf_op jit(solution)/shard_map/metric_turn/pallas_call | solution.py:331
  19.6 2.4 %collective-permute-done.1 = bf16[512,256]{1,0:T(8,128)(2,1)S(1)} collective-permute-done((bf16[512,256]{1,0:T(8,128)(2,1)}, bf16[512,256]{1,0:T(8,128)(2,1)S(1)}, u32[]{:S(2)}, u32[]{:S(2)}) %collective-permute-start.1) | collective-permute-done | bytes 262176 | tf_op jit(solution)/shard_map/gather/ppermute | solution.py:146
  22.1 2.1 %collective-permute-start.10 = (bf16[512,256]{1,0:T(8,128)(2,1)S(1)}, bf16[512,256]{1,0:T(8,128)(2,1)S(1)}, u32[]{:S(2)}, u32[]{:S(2)}) collective-permute-start(bf16[512,256]{1,0:T(8,128)(2,1)S(1)} %collective-permute-done), channel_id=1, source_target_pairs={{0,8},{1,9},{2,2},{3,3},{4,12},{5,13},{6,6},{7,7},{8,0},{9,1},{10,... | collective-permute-start | bytes 786440 | tf_op jit(solution)/shard_map/gather/ppermute | solution.py:146
  24.9 1.2 %collective-permute-start.6 = (bf16[512,256]{1,0:T(8,128)(2,1)}, bf16[512,256]{1,0:T(8,128)(2,1)S(1)}, u32[]{:S(2)}, u32[]{:S(2)}) collective-permute-start(bf16[512,256]{1,0:T(8,128)(2,1)} %get-tuple-element.46), channel_id=1, source_target_pairs={{0,1},{1,0},{2,3},{3,2},{4,5},{5,4},{6,7},{7,6},{8,9},{9,8},{10,11... | collective-permute-start | bytes 786440 | tf_op jit(solution)/shard_map/gather/ppermute | solution.py:146
  26.7 9.6 %collective-permute-done.10.refs_5_ = bf16[512,256]{1,0:T(8,128)(2,1)S(1)} collective-permute-done((bf16[512,256]{1,0:T(8,128)(2,1)S(1)}, bf16[512,256]{1,0:T(8,128)(2,1)S(1)}, u32[]{:S(2)}, u32[]{:S(2)}) %collective-permute-start.10) | collective-permute-done | bytes 262176 | tf_op jit(solution)/shard_map/gather/ppermute | solution.py:146
  36.4 1.8 %collective-permute-start.12 = (bf16[512,256]{1,0:T(8,128)(2,1)S(1)}, bf16[512,256]{1,0:T(8,128)(2,1)S(1)}, u32[]{:S(2)}, u32[]{:S(2)}) collective-permute-start(bf16[512,256]{1,0:T(8,128)(2,1)S(1)} %collective-permute-done.10.refs_5_), channel_id=1, source_target_pairs={{0,1},{1,0},{2,3},{3,2},{4,5},{5,4},{6,7},{7,6},{8,9},{9,8},{10,11... | collective-permute-start | bytes 786440 | tf_op jit(solution)/shard_map/gather/ppermute | solution.py:146
  40.5 2.6 %first_pair.1 = (f32[512,1024]{1,0:T(8,128)S(1)}, bf16[512,512]{1,0:T(8,128)(2,1)S(1)}, bf16[512,512]{1,0:T(8,128)(2,1)S(1)}) custom-call(f32[2]{0:T(128)S(1)} %pad_maximum_fusion.1.scalars, f32[1,512]{1,0:T(1,128)S(1)} %bitcast.18, f32[512,1]{1,0:T(8,128)S(1)} %copy.7.col_energy, bf16[512,256]{1,0:T(8,128)(2,1)S(1)} %get-tuple-element.49.refs_0_, ...), custom_call_target="tpu_custom_call" | custom-call | flops 1610612736 | bytes 4194304 | tf_op jit(solution)/shard_map/first_pair/pallas_call | solution.py:392
  43.1 3.1 %last_pair.1 = (bf16[512,1024]{1,0:T(8,128)(2,1)S(1)}, bf16[512,1024]{1,0:T(8,128)(2,1)S(1)}, f32[512,256]{1,0:T(8,128)S(1)}, f32[512,256]{1,0:T(8,128)S(1)}) custom-call(s32[3]{0:T(128)S(1)} %pad_add_fusion.place, f32[2]{0:T(128)S(1)} %pad_maximum_fusion.scalars, f32[1,512]{1,0:T(1,128)S(1)} %bitcast.19, f32[512,1]{1,0:T(8,128)S(1)} %copy.7.col_energy, ...), custom_call_target="tpu_custom_call" | custom-call | flops 2147483648 | bytes 6291456 | tf_op jit(solution)/shard_map/last_pair/pallas_call | solution.py:406
  46.4 1.3 %gamma.5 = bf16[272,512]{1,0:T(8,128)(2,1)S(1)} custom-call(bf16[4,256,1024]{2,1,0:T(8,128)(2,1)S(1)} %copy-done, bf16[4,256,1024]{2,1,0:T(8,128)(2,1)S(1)} %copy-done.1, bf16[512,1024]{1,0:T(8,128)(2,1)S(1)} %get-tuple-element.36.high, bf16[512,1024]{1,0:T(8,128)(2,1)S(1)} %get-tuple-element.37.low), custom_call_target="tpu_custom_call" | custom-call | flops 805306368 | bytes 3145728 | tf_op jit(solution)/shard_map/gamma/pallas_call | solution.py:434
  47.8 1.3 %gamma.6 = bf16[272,512]{1,0:T(8,128)(2,1)S(1)} custom-call(bf16[4,256,1024]{2,1,0:T(8,128)(2,1)S(1)} %copy-done, bf16[4,256,1024]{2,1,0:T(8,128)(2,1)S(1)} %copy-done.1, bf16[512,1024]{1,0:T(8,128)(2,1)S(1)} %get-tuple-element.36.high, bf16[512,1024]{1,0:T(8,128)(2,1)S(1)} %get-tuple-element.37.low), custom_call_target="tpu_custom_call" | custom-call | flops 805306368 | bytes 3145728 | tf_op jit(solution)/shard_map/gamma/pallas_call | solution.py:434
  49.2 3.0 %collective-permute-start.14 = (bf16[272,512]{1,0:T(8,128)(2,1)S(1)}, bf16[272,512]{1,0:T(8,128)(2,1)S(1)}, u32[]{:S(2)}, u32[]{:S(2)}) collective-permute-start(bf16[272,512]{1,0:T(8,128)(2,1)S(1)} %gamma.6), channel_id=1, source_target_pairs={{0,2},{1,6},{2,0},{3,4},{4,3},{5,7},{6,1},{7,5},{8,10},{9,14},{10,... | collective-permute-start | bytes 835592 | tf_op jit(solution)/shard_map/gamma/ppermute | solution.py:146
  53.1 1.4 %collective-permute-start.19 = (bf16[144,256]{1,0:T(8,128)(2,1)S(1)}, bf16[144,256]{1,0:T(8,128)(2,1)S(1)}, u32[]{:S(2)}, u32[]{:S(2)}) collective-permute-start(bf16[144,256]{1,0:T(8,128)(2,1)S(1)} %get-tuple-element.42), channel_id=1, source_target_pairs={{0,16},{1,17},{2,18},{3,19},{4,20},{5,21},{6,22},{7,23},{8,24},{9,... | collective-permute-start | bytes 221192 | tf_op jit(solution)/shard_map/density/ppermute | solution.py:146
  54.5 2.2 %collective-permute-start.20 = (bf16[144,256]{1,0:T(8,128)(2,1)S(1)}, bf16[144,256]{1,0:T(8,128)(2,1)S(1)}, u32[]{:S(2)}, u32[]{:S(2)}) collective-permute-start(bf16[144,256]{1,0:T(8,128)(2,1)S(1)} %get-tuple-element.43), channel_id=1, source_target_pairs={{0,24},{1,25},{2,26},{3,27},{4,28},{5,29},{6,30},{7,31},{8,16},{9,... | collective-permute-start | bytes 221192 | tf_op jit(solution)/shard_map/density/ppermute | solution.py:146
  56.6 1.3 %gamma.8 = bf16[272,512]{1,0:T(8,128)(2,1)S(1)} custom-call(bf16[4,256,1024]{2,1,0:T(8,128)(2,1)S(1)} %copy-done, bf16[4,256,1024]{2,1,0:T(8,128)(2,1)S(1)} %copy-done.1, bf16[512,1024]{1,0:T(8,128)(2,1)S(1)} %get-tuple-element.36.high, bf16[512,1024]{1,0:T(8,128)(2,1)S(1)} %get-tuple-element.37.low), custom_call_target="tpu_custom_call" | custom-call | flops 805306368 | bytes 3145728 | tf_op jit(solution)/shard_map/gamma/pallas_call | solution.py:434
  58.4 2.8 %collective-permute-done.19.refs_1_ = bf16[144,256]{1,0:T(8,128)(2,1)S(1)} collective-permute-done((bf16[144,256]{1,0:T(8,128)(2,1)S(1)}, bf16[144,256]{1,0:T(8,128)(2,1)S(1)}, u32[]{:S(2)}, u32[]{:S(2)}) %collective-permute-start.19) | collective-permute-done | bytes 73760 | tf_op jit(solution)/shard_map/density/ppermute | solution.py:146
  62.3 2.6 %collective-permute-start.21 = (f32[64,256]{1,0:T(8,128)S(1)}, f32[64,256]{1,0:T(8,128)S(1)}, u32[]{:S(2)}, u32[]{:S(2)}) collective-permute-start(f32[64,256]{1,0:T(8,128)S(1)} %get-tuple-element.44), channel_id=1, source_target_pairs={{0,2},{1,3},{2,0},{3,1},{4,6},{5,7},{6,4},{7,5},{8,10},{9,11},{10,... | collective-permute-start | bytes 196616 | tf_op jit(solution)/shard_map/density/ppermute | solution.py:146
  64.9 1.3 %gamma.7 = bf16[272,512]{1,0:T(8,128)(2,1)S(1)} custom-call(bf16[4,256,1024]{2,1,0:T(8,128)(2,1)S(1)} %copy-done, bf16[4,256,1024]{2,1,0:T(8,128)(2,1)S(1)} %copy-done.1, bf16[512,1024]{1,0:T(8,128)(2,1)S(1)} %get-tuple-element.36.high, bf16[512,1024]{1,0:T(8,128)(2,1)S(1)} %get-tuple-element.37.low), custom_call_target="tpu_custom_call" | custom-call | flops 805306368 | bytes 3145728 | tf_op jit(solution)/shard_map/gamma/pallas_call | solution.py:434
  68.3 3.8 %collective-permute-start.16 = (bf16[272,512]{1,0:T(8,128)(2,1)S(1)}, bf16[272,512]{1,0:T(8,128)(2,1)S(1)}, u32[]{:S(2)}, u32[]{:S(2)}) collective-permute-start(bf16[272,512]{1,0:T(8,128)(2,1)S(1)} %gamma.8), channel_id=1, source_target_pairs={{0,0},{1,4},{2,2},{3,6},{4,1},{5,5},{6,3},{7,7},{8,8},{9,12},{10,1... | collective-permute-start | bytes 835592 | tf_op jit(solution)/shard_map/gamma/ppermute | solution.py:146
  72.3 5.2 %collective-permute-done.16.refs_3_ = bf16[272,512]{1,0:T(8,128)(2,1)S(1)} collective-permute-done((bf16[272,512]{1,0:T(8,128)(2,1)S(1)}, bf16[272,512]{1,0:T(8,128)(2,1)S(1)}, u32[]{:S(2)}, u32[]{:S(2)}) %collective-permute-start.16) | collective-permute-done | bytes 278560 | tf_op jit(solution)/shard_map/gamma/ppermute | solution.py:146
  77.5 2.8 %gamma.9 = f32[256,1,512]{2,1,0:T(1,128)} custom-call(bf16[272,512]{1,0:T(8,128)(2,1)S(1)} %collective-permute-done.13.refs_0_, bf16[272,512]{1,0:T(8,128)(2,1)S(1)} %collective-permute-done.14.refs_1_, bf16[272,512]{1,0:T(8,128)(2,1)S(1)} %collective-permute-done.15.refs_2_, bf16[272,512]{1,0:T(8,128)(2,1)S(1)} %collective-permute-done.16.refs_3_), custom_call_target="tpu_custom_call" | custom-call | tf_op jit(solution)/shard_map/gamma/pallas_call | solution.py:487
  (54 shorter events, 9.7 us)
Async XLA Ops:
  0.6 19.0 %collective-permute-start.4 = (bf16[512,256]{1,0:T(8,128)(2,1)}, bf16[512,256]{1,0:T(8,128)(2,1)S(1)}, u32[]{:S(2)}, u32[]{:S(2)}) collective-permute-start(bf16[512,256]{1,0:T(8,128)(2,1)} %bitcast.20), channel_id=1, source_target_pairs={{0,16},{1,17},{2,26},{3,27},{4,20},{5,21},{6,30},{7,31},{8,24},{9,... | collective-permute-start | bytes 786440 | tf_op jit(solution)/shard_map/gather/ppermute | solution.py:146
  3.8 15.8 %collective-permute-start.3 = (bf16[512,256]{1,0:T(8,128)(2,1)}, bf16[512,256]{1,0:T(8,128)(2,1)S(1)}, u32[]{:S(2)}, u32[]{:S(2)}) collective-permute-start(bf16[512,256]{1,0:T(8,128)(2,1)} %bitcast.21), channel_id=1, source_target_pairs={{0,8},{1,9},{2,2},{3,3},{4,12},{5,13},{6,6},{7,7},{8,0},{9,1},{10,... | collective-permute-start | bytes 786440 | tf_op jit(solution)/shard_map/gather/ppermute | solution.py:146
  7.0 12.6 %collective-permute-start.2 = (bf16[512,256]{1,0:T(8,128)(2,1)}, bf16[512,256]{1,0:T(8,128)(2,1)S(1)}, u32[]{:S(2)}, u32[]{:S(2)}) collective-permute-start(bf16[512,256]{1,0:T(8,128)(2,1)} %bitcast.22), channel_id=1, source_target_pairs={{0,6},{1,7},{2,4},{3,5},{4,2},{5,3},{6,0},{7,1},{8,14},{9,15},{10,... | collective-permute-start | bytes 786440 | tf_op jit(solution)/shard_map/gather/ppermute | solution.py:146
  8.6 13.4 %collective-permute-start.1 = (bf16[512,256]{1,0:T(8,128)(2,1)}, bf16[512,256]{1,0:T(8,128)(2,1)S(1)}, u32[]{:S(2)}, u32[]{:S(2)}) collective-permute-start(bf16[512,256]{1,0:T(8,128)(2,1)} %bitcast.23), channel_id=1, source_target_pairs={{0,4},{1,5},{2,6},{3,7},{4,0},{5,1},{6,2},{7,3},{8,12},{9,13},{10,... | collective-permute-start | bytes 786440 | tf_op jit(solution)/shard_map/gather/ppermute | solution.py:146
  8.8 13.2 %collective-permute-start = (bf16[512,256]{1,0:T(8,128)(2,1)}, bf16[512,256]{1,0:T(8,128)(2,1)S(1)}, u32[]{:S(2)}, u32[]{:S(2)}) collective-permute-start(bf16[512,256]{1,0:T(8,128)(2,1)} %bitcast.24), channel_id=1, source_target_pairs={{0,2},{1,3},{2,0},{3,1},{4,6},{5,7},{6,4},{7,5},{8,10},{9,11},{10,... | collective-permute-start | bytes 786440 | tf_op jit(solution)/shard_map/gather/ppermute | solution.py:146
  22.1 17.9 %collective-permute-start.7 = (bf16[512,256]{1,0:T(8,128)(2,1)S(1)}, bf16[512,256]{1,0:T(8,128)(2,1)S(1)}, u32[]{:S(2)}, u32[]{:S(2)}) collective-permute-start(bf16[512,256]{1,0:T(8,128)(2,1)S(1)} %collective-permute-done), channel_id=1, source_target_pairs={{0,16},{1,17},{2,26},{3,27},{4,20},{5,21},{6,30},{7,31},{8,24},{9,... | collective-permute-start | bytes 786440 | tf_op jit(solution)/shard_map/gather/ppermute | solution.py:146
  22.1 14.3 %collective-permute-start.10 = (bf16[512,256]{1,0:T(8,128)(2,1)S(1)}, bf16[512,256]{1,0:T(8,128)(2,1)S(1)}, u32[]{:S(2)}, u32[]{:S(2)}) collective-permute-start(bf16[512,256]{1,0:T(8,128)(2,1)S(1)} %collective-permute-done), channel_id=1, source_target_pairs={{0,8},{1,9},{2,2},{3,3},{4,12},{5,13},{6,6},{7,7},{8,0},{9,1},{10,... | collective-permute-start | bytes 786440 | tf_op jit(solution)/shard_map/gather/ppermute | solution.py:146
  24.9 15.0 %collective-permute-start.6 = (bf16[512,256]{1,0:T(8,128)(2,1)}, bf16[512,256]{1,0:T(8,128)(2,1)S(1)}, u32[]{:S(2)}, u32[]{:S(2)}) collective-permute-start(bf16[512,256]{1,0:T(8,128)(2,1)} %get-tuple-element.46), channel_id=1, source_target_pairs={{0,1},{1,0},{2,3},{3,2},{4,5},{5,4},{6,7},{7,6},{8,9},{9,8},{10,11... | collective-permute-start | bytes 786440 | tf_op jit(solution)/shard_map/gather/ppermute | solution.py:146
  26.2 14.3 %collective-permute-start.5 = (bf16[512,256]{1,0:T(8,128)(2,1)S(1)}, bf16[512,256]{1,0:T(8,128)(2,1)S(1)}, u32[]{:S(2)}, u32[]{:S(2)}) collective-permute-start(bf16[512,256]{1,0:T(8,128)(2,1)S(1)} %get-tuple-element.48), channel_id=1, source_target_pairs={{0,1},{1,0},{2,3},{3,2},{4,5},{5,4},{6,7},{7,6},{8,9},{9,8},{10,11... | collective-permute-start | bytes 786440 | tf_op jit(solution)/shard_map/gather/ppermute | solution.py:146
  26.2 14.3 %collective-permute-start.11 = (bf16[512,256]{1,0:T(8,128)(2,1)S(1)}, bf16[512,256]{1,0:T(8,128)(2,1)S(1)}, u32[]{:S(2)}, u32[]{:S(2)}) collective-permute-start(bf16[512,256]{1,0:T(8,128)(2,1)S(1)} %collective-permute-done.3.refs_4_), channel_id=1, source_target_pairs={{0,1},{1,0},{2,3},{3,2},{4,5},{5,4},{6,7},{7,6},{8,9},{9,8},{10,11... | collective-permute-start | bytes 786440 | tf_op jit(solution)/shard_map/gather/ppermute | solution.py:146
  36.4 4.1 %collective-permute-start.12 = (bf16[512,256]{1,0:T(8,128)(2,1)S(1)}, bf16[512,256]{1,0:T(8,128)(2,1)S(1)}, u32[]{:S(2)}, u32[]{:S(2)}) collective-permute-start(bf16[512,256]{1,0:T(8,128)(2,1)S(1)} %collective-permute-done.10.refs_5_), channel_id=1, source_target_pairs={{0,1},{1,0},{2,3},{3,2},{4,5},{5,4},{6,7},{7,6},{8,9},{9,8},{10,11... | collective-permute-start | bytes 786440 | tf_op jit(solution)/shard_map/gather/ppermute | solution.py:146
  39.9 3.2 %collective-permute-start.8 = (bf16[512,256]{1,0:T(8,128)(2,1)S(1)}, bf16[512,256]{1,0:T(8,128)(2,1)S(1)}, u32[]{:S(2)}, u32[]{:S(2)}) collective-permute-start(bf16[512,256]{1,0:T(8,128)(2,1)S(1)} %collective-permute-done.4.refs_4_), channel_id=1, source_target_pairs={{0,1},{1,0},{2,3},{3,2},{4,5},{5,4},{6,7},{7,6},{8,9},{9,8},{10,11... | collective-permute-start | bytes 786440 | tf_op jit(solution)/shard_map/gather/ppermute | solution.py:146
  46.2 5.9 %collective-permute-start.17 = (f32[512,256]{1,0:T(8,128)S(1)}, f32[512,256]{1,0:T(8,128)S(1)}, u32[]{:S(2)}, u32[]{:S(2)}) collective-permute-start(f32[512,256]{1,0:T(8,128)S(1)} %get-tuple-element.39), channel_id=1, source_target_pairs={{0,1},{1,0},{2,3},{3,2},{4,5},{5,4},{6,7},{7,6},{8,9},{9,8},{10,11... | collective-permute-start | bytes 1572872 | tf_op jit(solution)/shard_map/density/ppermute | solution.py:146
  47.7 24.5 %collective-permute-start.13 = (bf16[272,512]{1,0:T(8,128)(2,1)S(1)}, bf16[272,512]{1,0:T(8,128)(2,1)S(1)}, u32[]{:S(2)}, u32[]{:S(2)}) collective-permute-start(bf16[272,512]{1,0:T(8,128)(2,1)S(1)} %gamma.5), channel_id=1, source_target_pairs={{0,3},{1,7},{2,1},{3,5},{4,2},{5,6},{6,0},{7,4},{8,11},{9,15},{10,... | collective-permute-start | bytes 835592 | tf_op jit(solution)/shard_map/gamma/ppermute | solution.py:146
  49.2 23.1 %collective-permute-start.14 = (bf16[272,512]{1,0:T(8,128)(2,1)S(1)}, bf16[272,512]{1,0:T(8,128)(2,1)S(1)}, u32[]{:S(2)}, u32[]{:S(2)}) collective-permute-start(bf16[272,512]{1,0:T(8,128)(2,1)S(1)} %gamma.6), channel_id=1, source_target_pairs={{0,2},{1,6},{2,0},{3,4},{4,3},{5,7},{6,1},{7,5},{8,10},{9,14},{10,... | collective-permute-start | bytes 835592 | tf_op jit(solution)/shard_map/gamma/ppermute | solution.py:146
  53.0 5.4 %collective-permute-start.18 = (bf16[144,256]{1,0:T(8,128)(2,1)S(1)}, bf16[144,256]{1,0:T(8,128)(2,1)S(1)}, u32[]{:S(2)}, u32[]{:S(2)}) collective-permute-start(bf16[144,256]{1,0:T(8,128)(2,1)S(1)} %get-tuple-element.41), channel_id=1, source_target_pairs={{0,8},{1,9},{2,10},{3,11},{4,12},{5,13},{6,14},{7,15},{8,0},{9,1},... | collective-permute-start | bytes 221192 | tf_op jit(solution)/shard_map/density/ppermute | solution.py:146
  53.1 8.1 %collective-permute-start.19 = (bf16[144,256]{1,0:T(8,128)(2,1)S(1)}, bf16[144,256]{1,0:T(8,128)(2,1)S(1)}, u32[]{:S(2)}, u32[]{:S(2)}) collective-permute-start(bf16[144,256]{1,0:T(8,128)(2,1)S(1)} %get-tuple-element.42), channel_id=1, source_target_pairs={{0,16},{1,17},{2,18},{3,19},{4,20},{5,21},{6,22},{7,23},{8,24},{9,... | collective-permute-start | bytes 221192 | tf_op jit(solution)/shard_map/density/ppermute | solution.py:146
  54.5 6.7 %collective-permute-start.20 = (bf16[144,256]{1,0:T(8,128)(2,1)S(1)}, bf16[144,256]{1,0:T(8,128)(2,1)S(1)}, u32[]{:S(2)}, u32[]{:S(2)}) collective-permute-start(bf16[144,256]{1,0:T(8,128)(2,1)S(1)} %get-tuple-element.43), channel_id=1, source_target_pairs={{0,24},{1,25},{2,26},{3,27},{4,28},{5,29},{6,30},{7,31},{8,16},{9,... | collective-permute-start | bytes 221192 | tf_op jit(solution)/shard_map/density/ppermute | solution.py:146
  62.2 6.2 %collective-permute-start.23 = (f32[64,256]{1,0:T(8,128)S(1)}, f32[64,256]{1,0:T(8,128)S(1)}, u32[]{:S(2)}, u32[]{:S(2)}) collective-permute-start(f32[64,256]{1,0:T(8,128)S(1)} %get-tuple-element.45), channel_id=1, source_target_pairs={{0,6},{1,7},{2,4},{3,5},{4,2},{5,3},{6,0},{7,1},{8,14},{9,15},{10,... | collective-permute-start | bytes 196616 | tf_op jit(solution)/shard_map/density/ppermute | solution.py:146
  62.2 9.9 %collective-permute-start.22 = (f32[64,256]{1,0:T(8,128)S(1)}, f32[64,256]{1,0:T(8,128)S(1)}, u32[]{:S(2)}, u32[]{:S(2)}) collective-permute-start(f32[64,256]{1,0:T(8,128)S(1)} %get-tuple-element.45), channel_id=1, source_target_pairs={{0,4},{1,5},{2,6},{3,7},{4,0},{5,1},{6,2},{7,3},{8,12},{9,13},{10,... | collective-permute-start | bytes 196616 | tf_op jit(solution)/shard_map/density/ppermute | solution.py:146
  62.3 4.9 %collective-permute-start.21 = (f32[64,256]{1,0:T(8,128)S(1)}, f32[64,256]{1,0:T(8,128)S(1)}, u32[]{:S(2)}, u32[]{:S(2)}) collective-permute-start(f32[64,256]{1,0:T(8,128)S(1)} %get-tuple-element.44), channel_id=1, source_target_pairs={{0,2},{1,3},{2,0},{3,1},{4,6},{5,7},{6,4},{7,5},{8,10},{9,11},{10,... | collective-permute-start | bytes 196616 | tf_op jit(solution)/shard_map/density/ppermute | solution.py:146
  67.2 5.1 %collective-permute-start.15 = (bf16[272,512]{1,0:T(8,128)(2,1)S(1)}, bf16[272,512]{1,0:T(8,128)(2,1)S(1)}, u32[]{:S(2)}, u32[]{:S(2)}) collective-permute-start(bf16[272,512]{1,0:T(8,128)(2,1)S(1)} %gamma.7), channel_id=1, source_target_pairs={{0,1},{1,5},{2,3},{3,7},{4,0},{5,4},{6,2},{7,6},{8,9},{9,13},{10,1... | collective-permute-start | bytes 835592 | tf_op jit(solution)/shard_map/gamma/ppermute | solution.py:146
  68.3 9.2 %collective-permute-start.16 = (bf16[272,512]{1,0:T(8,128)(2,1)S(1)}, bf16[272,512]{1,0:T(8,128)(2,1)S(1)}, u32[]{:S(2)}, u32[]{:S(2)}) collective-permute-start(bf16[272,512]{1,0:T(8,128)(2,1)S(1)} %gamma.8), channel_id=1, source_target_pairs={{0,0},{1,4},{2,2},{3,6},{4,1},{5,5},{6,3},{7,7},{8,8},{9,12},{10,1... | collective-permute-start | bytes 835592 | tf_op jit(solution)/shard_map/gamma/ppermute | solution.py:146
  72.2 8.1 %collective-permute-start.24 = (f32[64,256]{1,0:T(8,128)S(1)}, f32[64,256]{1,0:T(8,128)S(1)}, u32[]{:S(2)}, u32[]{:S(2)}) collective-permute-start(f32[64,256]{1,0:T(8,128)S(1)} %add_add_fusion), channel_id=1, source_target_pairs={{0,1},{1,0},{2,3},{3,2},{4,5},{5,4},{6,7},{7,6},{8,9},{9,8},{10,11... | collective-permute-start | bytes 196616 | tf_op jit(solution)/shard_map/density/ppermute | solution.py:146
  (5 other events, 42.7 us)

commit v3 on v0

--- a/solution.py
+++ b/solution.py
@@ -1,6 +1,10 @@
+import functools
+
 import jax
 import jax.numpy as jnp
 from jax import lax
+from jax.experimental import pallas as pl
+from jax.experimental.pallas import tpu as pltpu
 from jax.sharding import PartitionSpec as P
 
 CYCLE_STEPS = 4
@@ -57,7 +61,7 @@
     return lax.fori_loop(0, per_batch * per_batch, one_pair, (acc_own, acc_part, density))
 
 
-def per_device(factors, occ_energy, vir_energy, metric):
+def general_device(factors, occ_energy, vir_energy, metric):
     n_blk = lax.axis_size("blk")
     n_sec = lax.axis_size("sec")
     blk_pos = lax.axis_index("blk")
@@ -117,7 +121,459 @@
     return (gamma_part, density_out)
 
 
+AXES = ("blk", "sec")
+NT = (((1,), (1,)), ((), ()))
+NN = (((1,), (0,)), ((), ()))
+TAIL_ROWS = 16
+VMEM_LIMIT = 16 * 1024 * 1024
+
+
+def dot(left, right, dims):
+    return lax.dot_general(left, right, dims, preferred_element_type=jnp.float32)
+
+
+def split_bits(device, n_sec):
+    blk, sec = device // n_sec, device % n_sec
+    return blk // 2, blk % 2, sec // 2, sec % 2
+
+
+def join_bits(z, y, x, c, n_sec):
+    return (2 * z + y) * n_sec + 2 * x + c
+
+
+def send(value, target, n_blk, n_sec):
+    pairs = []
+    for device in range(n_blk * n_sec):
+        pairs.append((device, join_bits(*target(*split_bits(device, n_sec)), n_sec)))
+    return lax.ppermute(value, AXES, pairs)
+
+
+def encode(value):
+    peak = jnp.max(jnp.abs(value), keepdims=True)
+    power = jnp.floor(15.4 - jnp.log2(jnp.maximum(peak, 1e-36)))
+    power = jnp.clip(power, -120.0, 120.0)
+    scaled = value * jnp.exp2(power)
+    second = scaled * scaled
+    fourth = second * second
+    eighth = fourth * fourth
+    coded = jnp.where(scaled < 0.0, -eighth, eighth).astype(jnp.bfloat16)
+    tail = jnp.broadcast_to(power, (TAIL_ROWS, value.shape[1])).astype(jnp.bfloat16)
+    return coded, tail
+
+
+def encode_into(out, value):
+    rows = value.shape[0]
+    coded, tail = encode(value)
+    out[:rows] = coded
+    out[rows:] = tail
+
+
+def decode(ref):
+    rows = ref.shape[0] - TAIL_ROWS
+    power = ref[rows:].astype(jnp.float32)[:1]
+    coded = ref[:rows].astype(jnp.float32)
+    root = jnp.exp2(jnp.log2(jnp.abs(coded)) * 0.125 - power)
+    return jnp.where(coded < 0.0, -root, root)
+
+
+def place_bits():
+    blk, sec = lax.axis_index("blk"), lax.axis_index("sec")
+    return blk // 2, blk % 2, sec // 2, sec % 2
+
+
+def pair_terms(occupied, virtual, layer, left, right):
+    z, y, x, c = place_bits()
+    index = lax.broadcasted_iota(jnp.int32, occupied.shape, 1)
+
+    def energy(batch):
+        return jnp.sum(jnp.where(index == batch, occupied[...], 0.0), axis=1, keepdims=True)
+
+    row_energy = virtual[...]
+    row_sum = energy(2 * z + c) + energy(2 * layer + y) - row_energy
+    size = row_energy.shape[1]
+    col_energy = jnp.broadcast_to(row_energy, (128, size)).T[:, :1]
+    col_sum = jnp.broadcast_to(row_sum, (128, size)).T[:, :1]
+    straight = dot(left[0], right[0], NT)
+    turned = dot(right[0], left[0], NT)
+    for part in range(1, len(left)):
+        straight += dot(left[part], right[part], NT)
+        turned += dot(right[part], left[part], NT)
+    amplitude = straight / (col_sum - row_energy)
+    amplitude_t = turned / (row_sum - col_energy)
+    return amplitude.astype(jnp.bfloat16), 2.0 * amplitude - amplitude_t
+
+
+def read_left(refs):
+    z, y, x, c = place_bits()
+    home = c == y
+    own, swapped, near, near_swapped, far, far_swapped = [ref[...] for ref in refs]
+    return [
+        jnp.where(home, own, near),
+        jnp.where(home, swapped, near_swapped),
+        jnp.where(home, near, far),
+        jnp.where(home, near_swapped, far_swapped),
+    ]
+
+
+def first_pair_kernel(*refs):
+    z, y, x, c = place_bits()
+    left = read_left(refs[2:8])
+    right = [ref[...] for ref in refs[8:12]]
+    grad_out, amp_out, mixed_out = refs[-3:]
+    layer = jnp.where(x == 1, z, z ^ 1)
+    amp_half, mixed = pair_terms(refs[0], refs[1], layer, left, right)
+    mixed_half = mixed.astype(jnp.bfloat16)
+    width = right[0].shape[1]
+    for part in range(4):
+        grad_out[:, part * width : (part + 1) * width] = dot(mixed_half, right[part], NN)
+    amp_out[...] = amp_half
+    mixed_out[...] = mixed_half
+
+
+def last_pair_kernel(*refs):
+    z, y, x, c = place_bits()
+    left = read_left(refs[2:8])
+    right = [ref[...] for ref in refs[8:12]]
+    first_amp, first_mixed = refs[12:14]
+    mixed_out, dens_keep, dens_send, amp = refs[-4:]
+    layer = jnp.where(x == 1, z ^ 3, z ^ 2)
+    amp_half, mixed = pair_terms(refs[0], refs[1], layer, left, right)
+    outside = (x == 0) & (c == y)
+    mixed_half = jnp.where(outside, 0.0, mixed).astype(jnp.bfloat16)
+    amp[...] = amp_half
+    mixed_out[...] = mixed_half
+    half = amp.shape[0] // 2
+    mixed_first = first_mixed[...]
+    for out, core in ((dens_send, 1 - c), (dens_keep, c)):
+        rows = pl.ds(pl.multiple_of(core * half, half), half)
+        out[...] = dot(mixed_half, amp[rows, :], NT) + dot(mixed_first, first_amp[rows, :], NT)
+
+
+def metric_product(step, metric_high, metric_low, high, low):
+    metric_top = metric_high[step]
+    block = dot(metric_top, high[...], NT)
+    block += dot(metric_top, low[...], NT)
+    return block + dot(metric_low[step], high[...], NT)
+
+
+def gradient_kernel(step, mixed, *refs):
+    grad_in, metric_high, metric_low, high_out, low_out, out = refs[4:]
+    mixed_half = mixed[...]
+    width = refs[0].shape[1]
+    for part in range(4):
+        cols = slice(part * width, (part + 1) * width)
+        grad = grad_in[:, cols] + dot(mixed_half, refs[part][...], NN)
+        high = grad.astype(jnp.bfloat16)
+        high_out[:, cols] = high
+        low_out[:, cols] = (grad - high.astype(jnp.float32)).astype(jnp.bfloat16)
+    encode_into(out, metric_product(step, metric_high, metric_low, high_out, low_out))
+
+
+def metric_kernel(step, metric_high, metric_low, high, low, *refs):
+    encode_into(refs[-1], metric_product(step, metric_high, metric_low, high, low))
+
+
+def turn_metric_kernel(metric, *refs):
+    high, low = refs[-2:]
+    z, y, x, c = place_bits()
+    steps, width, aux_total = high.shape
+    row = lax.broadcasted_iota(jnp.int32, (width, width), 0)
+    col = lax.broadcasted_iota(jnp.int32, (width, width), 1)
+    unit = jnp.where(row == col, 1.0, 0.0).astype(jnp.bfloat16)
+    lane = 2 * x + c
+    for step in range(steps):
+        target = 2 * (x ^ (step >> 1)) + (y ^ (step & 1))
+        for part, order in enumerate((lane, lane ^ 2, lane ^ 1, lane ^ 3)):
+            value = metric[
+                pl.ds(pl.multiple_of(order * width, width), width),
+                pl.ds(pl.multiple_of(target * width, width), width),
+            ]
+            top = value.astype(jnp.bfloat16)
+            rest = (value - top.astype(jnp.float32)).astype(jnp.bfloat16)
+            cols = slice(part * width, (part + 1) * width)
+            high[step, :, cols] = dot(unit, top, NT).astype(jnp.bfloat16)
+            low[step, :, cols] = dot(unit, rest, NT).astype(jnp.bfloat16)
+
+
+def gamma_part_kernel(left, right, *refs):
+    refs[-1][...] = decode(left) + decode(right)
+
+
+def gamma_sum_kernel(part, left, right, *refs):
+    refs[-1][:, 0, :] = part[...] + decode(left) + decode(right)
+
+
+def halve(total, bit, keep_out, send_out):
+    rows = keep_out.shape[0]
+    keep_out[...] = total[pl.ds(pl.multiple_of(bit * rows, rows), rows), :]
+    encode_into(send_out, total[pl.ds(pl.multiple_of((1 - bit) * rows, rows), rows), :])
+
+
+def density_cores_kernel(keep, got, *refs):
+    keep_out, send_out, total = refs[-3:]
+    z, y, x, c = place_bits()
+    total[...] = keep[...] + got[...]
+    halve(total, z // 2, keep_out, send_out)
+
+
+def density_layers_kernel(keep, got, *refs):
+    keep_out, send_out, total = refs[-3:]
+    z, y, x, c = place_bits()
+    total[...] = keep[...] + decode(got)
+    halve(total, z % 2, keep_out, send_out)
+
+
+def density_rows_kernel(keep, got, *refs):
+    mine, theirs, total = refs[-3:]
+    z, y, x, c = place_bits()
+    total[...] = keep[...] + decode(got)
+    rows = mine.shape[0]
+    mine[...] = total[pl.ds(pl.multiple_of(y * rows, rows), rows), :]
+    theirs[...] = total[pl.ds(pl.multiple_of((1 - y) * rows, rows), rows), :]
+
+
+def density_block_kernel(mine, from_x, from_y, from_xy, *refs):
+    refs[-1][...] = (mine[...] + from_x[...]) + (from_y[...] + from_xy[...])
+
+
+def density_join_kernel(block, other, out):
+    z, y, x, c = place_bits()
+    half = block.shape[1]
+    out[:, :half] = jnp.where(c == 0, block[...], other[...])
+    out[:, half:] = jnp.where(c == 0, other[...], block[...])
+
+
+def fast_device(factors, occ_energy, vir_energy, metric):
+    n_blk = lax.axis_size("blk")
+    n_sec = lax.axis_size("sec")
+    own = factors[0]
+    virtuals, width = own.shape
+    aux_total = width * n_sec
+    half = virtuals // 2
+    rows = virtuals // n_blk
+    square = 2 * virtuals * virtuals
+
+    def move(value, target):
+        return send(value, target, n_blk, n_sec)
+
+    def core_swap(value):
+        return move(value, lambda z, y, x, c: (z, y, x, 1 - c))
+
+    def x_swap(value):
+        return move(value, lambda z, y, x, c: (z, y, 1 - x, c))
+
+    def y_swap(value):
+        return move(value, lambda z, y, x, c: (z, 1 - y, x, c))
+
+    def xy_swap(value):
+        return move(value, lambda z, y, x, c: (z, 1 - y, 1 - x, c))
+
+    def first_partner(value):
+        return move(value, lambda z, y, x, c: (z if x else z ^ 1, y, x, c))
+
+    def last_partner(value):
+        return move(value, lambda z, y, x, c: (z ^ 3 if x else z ^ 2, y, x, c))
+
+    def near_left(value):
+        return move(value, lambda z, y, x, c: (z, 1 - y, x, c) if c == y else (z, y, x, 1 - c))
+
+    def far_left(value):
+        return move(value, lambda z, y, x, c: (z, y, x, c) if c == y else (z, 1 - y, x, 1 - c))
+
+    vmem = pl.BlockSpec(memory_space=pltpu.VMEM)
+    unread = pl.BlockSpec(memory_space=pl.ANY)
+    params = pltpu.CompilerParams(vmem_limit_bytes=VMEM_LIMIT)
+
+    def shape(dtype, *dims):
+        return jax.ShapeDtypeStruct(dims, dtype)
+
+    def call(name, kernel, outs, operands, earlier=(), scratch=(), flops=0):
+        many = isinstance(outs, list)
+        with jax.named_scope(name):
+            return pl.pallas_call(
+                kernel,
+                in_specs=[vmem] * len(operands) + [unread] * len(earlier),
+                out_specs=[vmem] * len(outs) if many else vmem,
+                out_shape=outs,
+                scratch_shapes=list(scratch),
+                compiler_params=params,
+                cost_estimate=pl.CostEstimate(
+                    flops=flops,
+                    bytes_accessed=sum(2 * operand.size for operand in operands),
+                    transcendentals=0,
+                ),
+            )(*operands, *earlier)
+
+    with jax.named_scope("gather"):
+        far_own, near_own, swapped, first_own, last_own = lax.optimization_barrier(
+            (far_left(own), near_left(own), x_swap(own), first_partner(own), last_partner(own))
+        )
+
+    metric_high, metric_low = call(
+        "metric_turn",
+        turn_metric_kernel,
+        [shape(jnp.bfloat16, n_sec, width, aux_total)] * 2,
+        [metric],
+        [swapped],
+        flops=4 * aux_total * aux_total * width,
+    )
+
+    with jax.named_scope("gather"):
+        (
+            far_swapped,
+            near_swapped,
+            first_swapped,
+            last_swapped,
+            last_own_got,
+            first_own_got,
+            metric_high,
+            metric_low,
+        ) = lax.optimization_barrier(
+            (
+                far_left(swapped),
+                near_left(swapped),
+                first_partner(swapped),
+                last_partner(swapped),
+                core_swap(last_own),
+                core_swap(first_own),
+                metric_high,
+                metric_low,
+            )
+        )
+        left = [own, swapped, near_own, near_swapped, far_own, far_swapped]
+        first = [first_own, first_swapped, first_own_got, core_swap(first_swapped)]
+        last = [last_own, last_swapped, last_own_got, core_swap(last_swapped)]
+
+    energies = [occ_energy[None, :], vir_energy[None, :]]
+    pair_flops = 3 * square * aux_total
+    grad, first_amp, first_mixed = call(
+        "first_pair",
+        first_pair_kernel,
+        [
+            shape(jnp.float32, virtuals, aux_total),
+            shape(jnp.bfloat16, virtuals, virtuals),
+            shape(jnp.bfloat16, virtuals, virtuals),
+        ],
+        energies + left + first,
+        flops=pair_flops,
+    )
+    last_mixed, dens_keep, dens_send = call(
+        "last_pair",
+        last_pair_kernel,
+        [
+            shape(jnp.bfloat16, virtuals, virtuals),
+            shape(jnp.float32, virtuals, half),
+            shape(jnp.float32, virtuals, half),
+        ],
+        energies + left + last + [first_amp, first_mixed],
+        scratch=[pltpu.VMEM((virtuals, virtuals), jnp.bfloat16)],
+        flops=pair_flops,
+    )
+    dens_got = core_swap(dens_send)
+
+    message = shape(jnp.bfloat16, width + TAIL_ROWS, virtuals)
+    block_flops = 6 * width * virtuals * aux_total
+    high, low, third = call(
+        "gradient",
+        functools.partial(gradient_kernel, 3),
+        [
+            shape(jnp.bfloat16, virtuals, aux_total),
+            shape(jnp.bfloat16, virtuals, aux_total),
+            message,
+        ],
+        [last_mixed, *last, grad, metric_high, metric_low],
+        flops=2 * block_flops,
+    )
+
+    def gamma_block(step, *earlier):
+        return call(
+            "gamma_block",
+            functools.partial(metric_kernel, step),
+            message,
+            [metric_high, metric_low, high, low],
+            earlier,
+            flops=block_flops,
+        )
+
+    def gamma_move(step, block):
+        return move(block, lambda z, y, x, c: (z, c, x ^ (step >> 1), y ^ (step & 1)))
+
+    def density_half(name, kernel, count, keep, got, *earlier):
+        return call(
+            name,
+            kernel,
+            [
+                shape(jnp.float32, count, half),
+                shape(jnp.bfloat16, count + TAIL_ROWS, half),
+            ],
+            [keep, got],
+            earlier,
+            [pltpu.VMEM(keep.shape, jnp.float32)],
+        )
+
+    got_third = gamma_move(3, third)
+    keep, packed = density_half(
+        "density_cores", density_cores_kernel, 4 * rows, dens_keep, dens_got, third
+    )
+    got = move(packed, lambda z, y, x, c: (z ^ 2, y, x, c))
+    second = gamma_block(2, packed)
+    got_second = gamma_move(2, second)
+    first_block = gamma_block(1, second)
+    got_first = gamma_move(1, first_block)
+    keep, packed = density_half(
+        "density_layers", density_layers_kernel, 2 * rows, keep, got, first_block, got_third
+    )
+    got = move(packed, lambda z, y, x, c: (z ^ 1, y, x, c))
+    zeroth = gamma_block(0, packed)
+    got_zeroth = gamma_move(0, zeroth)
+    mine, theirs = call(
+        "density_rows",
+        density_rows_kernel,
+        [shape(jnp.float32, rows, half)] * 2,
+        [keep, got],
+        [zeroth, got_second],
+        [pltpu.VMEM(keep.shape, jnp.float32)],
+    )
+    from_x, from_y, from_xy = x_swap(mine), y_swap(theirs), xy_swap(theirs)
+    part = call(
+        "gamma_part",
+        gamma_part_kernel,
+        shape(jnp.float32, width, virtuals),
+        [got_third, got_second],
+        [mine],
+    )
+    block = call(
+        "density_block",
+        density_block_kernel,
+        shape(jnp.float32, rows, half),
+        [mine, from_x, from_y, from_xy],
+        [part, got_first],
+    )
+    other = core_swap(block)
+    gamma = call(
+        "gamma_sum",
+        gamma_sum_kernel,
+        shape(jnp.float32, width, 1, virtuals),
+        [part, got_first, got_zeroth],
+        [block],
+    )
+    density = call(
+        "density_join",
+        density_join_kernel,
+        shape(jnp.float32, rows, virtuals),
+        [block, other],
+    )
+    return gamma, density
+
+
 def solution(mesh):
+    n_blk, n_sec = mesh.shape["blk"], mesh.shape["sec"]
+
+    def per_device(factors, occ_energy, vir_energy, metric):
+        two_rows_of_layers = n_sec == 4 and n_blk == 2 * n_sec and factors.shape[0] == 1
+        step = fast_device if two_rows_of_layers else general_device
+        return step(factors, occ_energy, vir_energy, metric)
+
     return jax.shard_map(
         per_device,
         mesh=mesh,

time: 251 us -> 72.9 us (0.29)
  waiting for transfers between devices: 173 us -> 20.6 us
  matrix products: 19.6 us -> 0 us
  between operations: 15.2 us -> 0.84 us
  Pallas kernels: 0 us -> 14.1 us
  starting transfers between devices: 21.5 us -> 34.6 us
  local copies, waits for them, and re-layouts: 13.5 us -> 2.19 us
  other arithmetic: 5.21 us -> 0 us
    reduce_scatter x2 -> x0, waiting for transfers between devices: 58.6 us -> none  [the longest x1 34.7 us: per_device(): lax.psum_scatter(own_term + jnp.einsum('pq,ipa->qia', metric_rows, carrie...]
    all_to_all x2 -> x0, waiting for transfers between devices: 33.7 us -> none  [the longest x1 22 us: per_device(): lax.all_to_all(acc_part[None], 'sec', split_axis=2, concat_axis=0, tiled=...]
    psum x1 -> x0, waiting for transfers between devices: 30.2 us -> none  [per_device(): density_out = lax.psum(density_rows, 'sec')]
    ppermute x6 -> x24, waiting for transfers between devices: 50.5 us -> 20.6 us  [send(): return lax.ppermute(value, AXES, pairs)]
    ppermute x6 -> x24, starting transfers between devices: 10.4 us -> 34.6 us  [send(): return lax.ppermute(value, AXES, pairs)]
    dot_general x7 -> x0, matrix products: 19.6 us -> none  [the longest x1 6.83 us: per_device(): jnp.einsum('pq,ipa->qia', metric, acc_own, precision=lax.Precision.HIGHEST)]
    pallas_call x0 -> x14, Pallas kernels: none -> 14.1 us  [call(): pl.pallas_call(kernel, in_specs=[vmem] * len(operands) + [unread] * len(e...]
    all_to_all x2 -> x0, starting transfers between devices: 11 us -> none  [the longest x1 6.55 us: per_device(): lax.all_to_all(jnp.stack(segmented, 0), 'sec', split_axis=0, concat_axis=...]
  transfers between devices with their start and end apart: 12 -> 24, of which waited for: 11 -> 11; matrix products, arithmetic and copies ran while one was open for 10% -> 0% of each run, Pallas kernels for 0% -> 15%
where the time goes in v3:
time: 72.9 us; the launch traced here: 72.3 us
  starting transfers between devices  34.6 us (47%)
  waiting for transfers between devices  20.6 us (28%)
  Pallas kernels  14.1 us (19%)
  local copies, waits for them, and re-layouts  2.19 us (3%)
  between operations  0.84 us (1%)
    ppermute x24, starting transfers between devices, send(): return lax.ppermute(value, AXES, pairs)  34.6 us
    ppermute x24, waiting for transfers between devices, send(): return lax.ppermute(value, AXES, pairs)  20.6 us
    pallas_call x14, Pallas kernels, call(): pl.pallas_call(kernel, in_specs=[vmem] * len(operands) + [unread] * len(e...  14.1 us
    unnamed x8, local copies, waits for them, and re-layouts  2.19 us
  transfers between devices with their start and end apart: 24, of which 11 were waited for; matrix products, arithmetic and copies ran while one was open for 0% of the time, Pallas kernels for 15%

profile of v3, /device:TPU:1, one launch (start us, length us, event | category | flops | bytes accessed | tf_op | source)
XLA Modules:
  0.0 72.3 jit_solution(14181533958029606142)
XLA Ops:
  0.6 3.2 %collective-permute-start.4 = (bf16[512,256]{1,0:T(8,128)(2,1)}, bf16[512,256]{1,0:T(8,128)(2,1)S(1)}, u32[]{:S(2)}, u32[]{:S(2)}) collective-permute-start(bf16[512,256]{1,0:T(8,128)(2,1)} %bitcast.3), channel_id=1, source_target_pairs={{0,16},{1,17},{2,26},{3,27},{4,20},{5,21},{6,30},{7,31},{8,24},{9,... | collective-permute-start | bytes 786440 | tf_op jit(solution)/shard_map/gather/ppermute | solution.py:148
  3.8 3.2 %collective-permute-start.3 = (bf16[512,256]{1,0:T(8,128)(2,1)}, bf16[512,256]{1,0:T(8,128)(2,1)S(1)}, u32[]{:S(2)}, u32[]{:S(2)}) collective-permute-start(bf16[512,256]{1,0:T(8,128)(2,1)} %bitcast.4), channel_id=1, source_target_pairs={{0,8},{1,9},{2,2},{3,3},{4,12},{5,13},{6,6},{7,7},{8,0},{9,1},{10,... | collective-permute-start | bytes 786440 | tf_op jit(solution)/shard_map/gather/ppermute | solution.py:148
  8.9 3.0 %collective-permute-start = (bf16[512,256]{1,0:T(8,128)(2,1)}, bf16[512,256]{1,0:T(8,128)(2,1)S(1)}, u32[]{:S(2)}, u32[]{:S(2)}) collective-permute-start(bf16[512,256]{1,0:T(8,128)(2,1)} %bitcast.7), channel_id=1, source_target_pairs={{0,0},{1,4},{2,2},{3,6},{4,1},{5,5},{6,3},{7,7},{8,8},{9,12},{10,1... | collective-permute-start | bytes 786440 | tf_op jit(solution)/shard_map/gather/ppermute | solution.py:148
  11.9 3.8 %collective-permute-done.4.refs_8_.refs_0_ = bf16[512,256]{1,0:T(8,128)(2,1)S(1)} collective-permute-done((bf16[512,256]{1,0:T(8,128)(2,1)}, bf16[512,256]{1,0:T(8,128)(2,1)S(1)}, u32[]{:S(2)}, u32[]{:S(2)}) %collective-permute-start.4) | collective-permute-done | bytes 262176 | tf_op jit(solution)/shard_map/gather/ppermute | solution.py:148
  15.7 1.5 %collective-permute-done.3.refs_8_ = bf16[512,256]{1,0:T(8,128)(2,1)S(1)} collective-permute-done((bf16[512,256]{1,0:T(8,128)(2,1)}, bf16[512,256]{1,0:T(8,128)(2,1)S(1)}, u32[]{:S(2)}, u32[]{:S(2)}) %collective-permute-start.3) | collective-permute-done | bytes 262176 | tf_op jit(solution)/shard_map/gather/ppermute | solution.py:148
  17.3 1.9 %collective-permute-start.10 = (bf16[512,256]{1,0:T(8,128)(2,1)S(1)}, bf16[512,256]{1,0:T(8,128)(2,1)S(1)}, u32[]{:S(2)}, u32[]{:S(2)}) collective-permute-start(bf16[512,256]{1,0:T(8,128)(2,1)S(1)} %collective-permute-done.3.refs_8_), channel_id=1, source_target_pairs={{0,1},{1,0},{2,3},{3,2},{4,5},{5,4},{6,7},{7,6},{8,9},{9,8},{10,11... | collective-permute-start | bytes 786440 | tf_op jit(solution)/shard_map/gather/ppermute | solution.py:148
  19.6 4.0 %collective-permute-start.7 = (bf16[512,256]{1,0:T(8,128)(2,1)S(1)}, bf16[512,256]{1,0:T(8,128)(2,1)S(1)}, u32[]{:S(2)}, u32[]{:S(2)}) collective-permute-start(bf16[512,256]{1,0:T(8,128)(2,1)S(1)} %collective-permute-done.2.refs_0_.refs_3_), channel_id=1, source_target_pairs={{0,8},{1,9},{2,2},{3,3},{4,12},{5,13},{6,6},{7,7},{8,0},{9,1},{10,... | collective-permute-start | bytes 786440 | tf_op jit(solution)/shard_map/gather/ppermute | solution.py:148
  24.6 3.1 %collective-permute-start.5 = (bf16[512,256]{1,0:T(8,128)(2,1)S(1)}, bf16[512,256]{1,0:T(8,128)(2,1)S(1)}, u32[]{:S(2)}, u32[]{:S(2)}) collective-permute-start(bf16[512,256]{1,0:T(8,128)(2,1)S(1)} %collective-permute-done.2.refs_0_.refs_3_), channel_id=1, source_target_pairs={{0,0},{1,4},{2,2},{3,6},{4,1},{5,5},{6,3},{7,7},{8,8},{9,12},{10,1... | collective-permute-start | bytes 786440 | tf_op jit(solution)/shard_map/gather/ppermute | solution.py:148
  27.7 2.2 %copy-done = f32[1024,1024]{1,0:T(8,128)S(1)} copy-done((f32[1024,1024]{1,0:T(8,128)S(1)}, f32[1024,1024]{1,0:T(8,128)}, u32[]{:S(2)}) %copy-start) | copy-done | bytes 4194328
  29.9 1.3 %metric_turn.1 = (bf16[4,256,1024]{2,1,0:T(8,128)(2,1)S(1)}, bf16[4,256,1024]{2,1,0:T(8,128)(2,1)S(1)}) custom-call(f32[1024,1024]{1,0:T(8,128)S(1)} %copy-done, bf16[512,256]{1,0:T(8,128)(2,1)S(1)} %collective-permute-done.2.refs_0_.refs_3_), custom_call_target="tpu_custom_call" | custom-call | flops 1073741824 | bytes 2097152 | tf_op jit(solution)/shard_map/metric_turn/pallas_call | solution.py:393
  31.2 2.7 %collective-permute-done.8.refs_9_.refs_1_ = bf16[512,256]{1,0:T(8,128)(2,1)S(1)} collective-permute-done((bf16[512,256]{1,0:T(8,128)(2,1)S(1)}, bf16[512,256]{1,0:T(8,128)(2,1)S(1)}, u32[]{:S(2)}, u32[]{:S(2)}) %collective-permute-start.8) | collective-permute-done | bytes 262176 | tf_op jit(solution)/shard_map/gather/ppermute | solution.py:148
  35.1 1.3 %collective-permute-start.12 = (bf16[512,256]{1,0:T(8,128)(2,1)S(1)}, bf16[512,256]{1,0:T(8,128)(2,1)S(1)}, u32[]{:S(2)}, u32[]{:S(2)}) collective-permute-start(bf16[512,256]{1,0:T(8,128)(2,1)S(1)} %collective-permute-done.7.refs_9_), channel_id=1, source_target_pairs={{0,1},{1,0},{2,3},{3,2},{4,5},{5,4},{6,7},{7,6},{8,9},{9,8},{10,11... | collective-permute-start | bytes 786440 | tf_op jit(solution)/shard_map/gather/ppermute | solution.py:148
  37.5 1.9 %first_pair.1 = (f32[512,1024]{1,0:T(8,128)S(1)}, bf16[512,512]{1,0:T(8,128)(2,1)S(1)}, bf16[512,512]{1,0:T(8,128)(2,1)S(1)}) custom-call(f32[1,8]{1,0:T(1,128)S(1)} %bitcast.12, f32[1,512]{1,0:T(1,128)S(1)} %bitcast.10, bf16[512,256]{1,0:T(8,128)(2,1)S(1)} %bitcast.8, bf16[512,256]{1,0:T(8,128)(2,1)S(1)} %collective-permute-done.2.refs_0_.refs_3_, ...), custom_call_target="tpu_custom_call" | custom-call | flops 1610612736 | bytes 2622480 | tf_op jit(solution)/shard_map/first_pair/pallas_call | solution.py:393
  39.5 1.9 %last_pair.1 = (bf16[512,512]{1,0:T(8,128)(2,1)S(1)}, f32[512,256]{1,0:T(8,128)S(1)}, f32[512,256]{1,0:T(8,128)S(1)}) custom-call(f32[1,8]{1,0:T(1,128)S(1)} %bitcast.13, f32[1,512]{1,0:T(1,128)S(1)} %bitcast.11, bf16[512,256]{1,0:T(8,128)(2,1)S(1)} %bitcast.9, bf16[512,256]{1,0:T(8,128)(2,1)S(1)} %collective-permute-done.2.refs_0_.refs_3_, ...), custom_call_target="tpu_custom_call" | custom-call | flops 1610612736 | bytes 3671056 | tf_op jit(solution)/shard_map/last_pair/pallas_call | solution.py:393
  41.8 2.0 %gradient.1 = (bf16[512,1024]{1,0:T(8,128)(2,1)S(1)}, bf16[512,1024]{1,0:T(8,128)(2,1)S(1)}, bf16[272,512]{1,0:T(8,128)(2,1)S(1)}) custom-call(bf16[512,512]{1,0:T(8,128)(2,1)S(1)} %get-tuple-element.47.mixed, bf16[512,256]{1,0:T(8,128)(2,1)S(1)} %collective-permute-done.4.refs_8_.refs_0_, bf16[512,256]{1,0:T(8,128)(2,1)S(1)} %collective-permute-done.8.refs_9_.refs_1_, ...), custom_call_target="tpu_custom_call" | custom-call | flops 1610612736 | bytes 6815744 | tf_op jit(solution)/shard_map/gradient/pallas_call | solution.py:393
  44.3 1.3 %gamma_block.3.refs_0_ = bf16[272,512]{1,0:T(8,128)(2,1)S(1)} custom-call(bf16[4,256,1024]{2,1,0:T(8,128)(2,1)S(1)} %get-tuple-element.49.refs_5_.metric_high, bf16[4,256,1024]{2,1,0:T(8,128)(2,1)S(1)} %get-tuple-element.50.refs_6_.metric_low, bf16[512,1024]{1,0:T(8,128)(2,1)S(1)} %get-tuple-element.52.high, bf16[512,1024]{1,0:T(8,128)(2,1)S(1)} %get-tuple-element.53.low, ...), custom_call_target="tpu_custom_call" | custom-call | flops 805306368 | bytes 6291456 | tf_op jit(solution)/shard_map/gamma_block/pallas_call | solution.py:393
  45.7 2.7 %collective-permute-start.15 = (bf16[272,512]{1,0:T(8,128)(2,1)S(1)}, bf16[272,512]{1,0:T(8,128)(2,1)S(1)}, u32[]{:S(2)}, u32[]{:S(2)}) collective-permute-start(bf16[272,512]{1,0:T(8,128)(2,1)S(1)} %gamma_block.3.refs_0_), channel_id=1, source_target_pairs={{0,2},{1,6},{2,0},{3,4},{4,3},{5,7},{6,1},{7,5},{8,10},{9,14},{10,... | collective-permute-start | bytes 835592 | tf_op jit(solution)/shard_map/ppermute | solution.py:148
  48.3 1.3 %gamma_block.4.refs_0_ = bf16[272,512]{1,0:T(8,128)(2,1)S(1)} custom-call(bf16[4,256,1024]{2,1,0:T(8,128)(2,1)S(1)} %get-tuple-element.49.refs_5_.metric_high, bf16[4,256,1024]{2,1,0:T(8,128)(2,1)S(1)} %get-tuple-element.50.refs_6_.metric_low, bf16[512,1024]{1,0:T(8,128)(2,1)S(1)} %get-tuple-element.52.high, bf16[512,1024]{1,0:T(8,128)(2,1)S(1)} %get-tuple-element.53.low, ...), custom_call_target="tpu_custom_call" | custom-call | flops 805306368 | bytes 6291456 | tf_op jit(solution)/shard_map/gamma_block/pallas_call | solution.py:393
  49.8 3.1 %collective-permute-done.13.refs_1_.left = bf16[272,512]{1,0:T(8,128)(2,1)S(1)} collective-permute-done((bf16[272,512]{1,0:T(8,128)(2,1)S(1)}, bf16[272,512]{1,0:T(8,128)(2,1)S(1)}, u32[]{:S(2)}, u32[]{:S(2)}) %collective-permute-start.13) | collective-permute-done | bytes 278560 | tf_op jit(solution)/shard_map/ppermute | solution.py:148
  53.2 1.3 %gamma_block.5.refs_0_ = bf16[272,512]{1,0:T(8,128)(2,1)S(1)} custom-call(bf16[4,256,1024]{2,1,0:T(8,128)(2,1)S(1)} %get-tuple-element.49.refs_5_.metric_high, bf16[4,256,1024]{2,1,0:T(8,128)(2,1)S(1)} %get-tuple-element.50.refs_6_.metric_low, bf16[512,1024]{1,0:T(8,128)(2,1)S(1)} %get-tuple-element.52.high, bf16[512,1024]{1,0:T(8,128)(2,1)S(1)} %get-tuple-element.53.low, ...), custom_call_target="tpu_custom_call" | custom-call | flops 805306368 | bytes 6291456 | tf_op jit(solution)/shard_map/gamma_block/pallas_call | solution.py:393
  54.5 3.4 %collective-permute-start.19 = (bf16[272,512]{1,0:T(8,128)(2,1)S(1)}, bf16[272,512]{1,0:T(8,128)(2,1)S(1)}, u32[]{:S(2)}, u32[]{:S(2)}) collective-permute-start(bf16[272,512]{1,0:T(8,128)(2,1)S(1)} %gamma_block.5.refs_0_), channel_id=1, source_target_pairs={{0,0},{1,4},{2,2},{3,6},{4,1},{5,5},{6,3},{7,7},{8,8},{9,12},{10,1... | collective-permute-start | bytes 835592 | tf_op jit(solution)/shard_map/ppermute | solution.py:148
  58.0 3.2 %collective-permute-done.17.got = bf16[144,256]{1,0:T(8,128)(2,1)S(1)} collective-permute-done((bf16[144,256]{1,0:T(8,128)(2,1)S(1)}, bf16[144,256]{1,0:T(8,128)(2,1)S(1)}, u32[]{:S(2)}, u32[]{:S(2)}) %collective-permute-start.17) | collective-permute-done | bytes 73760 | tf_op jit(solution)/shard_map/ppermute | solution.py:148
  61.4 2.6 %collective-permute-start.21 = (f32[64,256]{1,0:T(8,128)S(1)}, f32[64,256]{1,0:T(8,128)S(1)}, u32[]{:S(2)}, u32[]{:S(2)}) collective-permute-start(f32[64,256]{1,0:T(8,128)S(1)} %get-tuple-element.61), channel_id=1, source_target_pairs={{0,4},{1,5},{2,6},{3,7},{4,0},{5,1},{6,2},{7,3},{8,12},{9,13},{10,... | collective-permute-start | bytes 196616 | tf_op jit(solution)/shard_map/ppermute | solution.py:148
  67.4 2.1 %collective-permute-start.23 = (f32[64,256]{1,0:T(8,128)S(1)}, f32[64,256]{1,0:T(8,128)S(1)}, u32[]{:S(2)}, u32[]{:S(2)}) collective-permute-start(f32[64,256]{1,0:T(8,128)S(1)} %density_block.1.refs_0_.block), channel_id=1, source_target_pairs={{0,1},{1,0},{2,3},{3,2},{4,5},{5,4},{6,7},{7,6},{8,9},{9,8},{10,11... | collective-permute-start | bytes 196616 | tf_op jit(solution)/shard_map/ppermute | solution.py:148
  (46 shorter events, 13.4 us)
Async XLA Ops:
  0.6 15.1 %collective-permute-start.4 = (bf16[512,256]{1,0:T(8,128)(2,1)}, bf16[512,256]{1,0:T(8,128)(2,1)S(1)}, u32[]{:S(2)}, u32[]{:S(2)}) collective-permute-start(bf16[512,256]{1,0:T(8,128)(2,1)} %bitcast.3), channel_id=1, source_target_pairs={{0,16},{1,17},{2,26},{3,27},{4,20},{5,21},{6,30},{7,31},{8,24},{9,... | collective-permute-start | bytes 786440 | tf_op jit(solution)/shard_map/gather/ppermute | solution.py:148
  3.8 13.4 %collective-permute-start.3 = (bf16[512,256]{1,0:T(8,128)(2,1)}, bf16[512,256]{1,0:T(8,128)(2,1)S(1)}, u32[]{:S(2)}, u32[]{:S(2)}) collective-permute-start(bf16[512,256]{1,0:T(8,128)(2,1)} %bitcast.4), channel_id=1, source_target_pairs={{0,8},{1,9},{2,2},{3,3},{4,12},{5,13},{6,6},{7,7},{8,0},{9,1},{10,... | collective-permute-start | bytes 786440 | tf_op jit(solution)/shard_map/gather/ppermute | solution.py:148
  7.0 10.2 %collective-permute-start.2 = (bf16[512,256]{1,0:T(8,128)(2,1)}, bf16[512,256]{1,0:T(8,128)(2,1)S(1)}, u32[]{:S(2)}, u32[]{:S(2)}) collective-permute-start(bf16[512,256]{1,0:T(8,128)(2,1)} %bitcast.5), channel_id=1, source_target_pairs={{0,2},{1,3},{2,0},{3,1},{4,6},{5,7},{6,4},{7,5},{8,10},{9,11},{10,... | collective-permute-start | bytes 786440 | tf_op jit(solution)/shard_map/gather/ppermute | solution.py:148
  7.7 9.6 %collective-permute-start.1 = (bf16[512,256]{1,0:T(8,128)(2,1)}, bf16[512,256]{1,0:T(8,128)(2,1)S(1)}, u32[]{:S(2)}, u32[]{:S(2)}) collective-permute-start(bf16[512,256]{1,0:T(8,128)(2,1)} %bitcast.6), channel_id=1, source_target_pairs={{0,4},{1,0},{2,6},{3,2},{4,5},{5,1},{6,7},{7,3},{8,12},{9,8},{10,1... | collective-permute-start | bytes 786440 | tf_op jit(solution)/shard_map/gather/ppermute | solution.py:148
  8.9 8.4 %collective-permute-start = (bf16[512,256]{1,0:T(8,128)(2,1)}, bf16[512,256]{1,0:T(8,128)(2,1)S(1)}, u32[]{:S(2)}, u32[]{:S(2)}) collective-permute-start(bf16[512,256]{1,0:T(8,128)(2,1)} %bitcast.7), channel_id=1, source_target_pairs={{0,0},{1,4},{2,2},{3,6},{4,1},{5,5},{6,3},{7,7},{8,8},{9,12},{10,1... | collective-permute-start | bytes 786440 | tf_op jit(solution)/shard_map/gather/ppermute | solution.py:148
  17.3 7.3 %collective-permute-start.10 = (bf16[512,256]{1,0:T(8,128)(2,1)S(1)}, bf16[512,256]{1,0:T(8,128)(2,1)S(1)}, u32[]{:S(2)}, u32[]{:S(2)}) collective-permute-start(bf16[512,256]{1,0:T(8,128)(2,1)S(1)} %collective-permute-done.3.refs_8_), channel_id=1, source_target_pairs={{0,1},{1,0},{2,3},{3,2},{4,5},{5,4},{6,7},{7,6},{8,9},{9,8},{10,11... | collective-permute-start | bytes 786440 | tf_op jit(solution)/shard_map/gather/ppermute | solution.py:148
  19.2 12.0 %collective-permute-start.9 = (bf16[512,256]{1,0:T(8,128)(2,1)S(1)}, bf16[512,256]{1,0:T(8,128)(2,1)S(1)}, u32[]{:S(2)}, u32[]{:S(2)}) collective-permute-start(bf16[512,256]{1,0:T(8,128)(2,1)S(1)} %collective-permute-done.4.refs_8_.refs_0_), channel_id=1, source_target_pairs={{0,1},{1,0},{2,3},{3,2},{4,5},{5,4},{6,7},{7,6},{8,9},{9,8},{10,11... | collective-permute-start | bytes 786440 | tf_op jit(solution)/shard_map/gather/ppermute | solution.py:148
  19.3 14.6 %collective-permute-start.8 = (bf16[512,256]{1,0:T(8,128)(2,1)S(1)}, bf16[512,256]{1,0:T(8,128)(2,1)S(1)}, u32[]{:S(2)}, u32[]{:S(2)}) collective-permute-start(bf16[512,256]{1,0:T(8,128)(2,1)S(1)} %collective-permute-done.2.refs_0_.refs_3_), channel_id=1, source_target_pairs={{0,16},{1,17},{2,26},{3,27},{4,20},{5,21},{6,30},{7,31},{8,24},{9,... | collective-permute-start | bytes 786440 | tf_op jit(solution)/shard_map/gather/ppermute | solution.py:148
  19.6 15.5 %collective-permute-start.7 = (bf16[512,256]{1,0:T(8,128)(2,1)S(1)}, bf16[512,256]{1,0:T(8,128)(2,1)S(1)}, u32[]{:S(2)}, u32[]{:S(2)}) collective-permute-start(bf16[512,256]{1,0:T(8,128)(2,1)S(1)} %collective-permute-done.2.refs_0_.refs_3_), channel_id=1, source_target_pairs={{0,8},{1,9},{2,2},{3,3},{4,12},{5,13},{6,6},{7,7},{8,0},{9,1},{10,... | collective-permute-start | bytes 786440 | tf_op jit(solution)/shard_map/gather/ppermute | solution.py:148
  23.6 11.5 %collective-permute-start.6 = (bf16[512,256]{1,0:T(8,128)(2,1)S(1)}, bf16[512,256]{1,0:T(8,128)(2,1)S(1)}, u32[]{:S(2)}, u32[]{:S(2)}) collective-permute-start(bf16[512,256]{1,0:T(8,128)(2,1)S(1)} %collective-permute-done.2.refs_0_.refs_3_), channel_id=1, source_target_pairs={{0,4},{1,0},{2,6},{3,2},{4,5},{5,1},{6,7},{7,3},{8,12},{9,8},{10,1... | collective-permute-start | bytes 786440 | tf_op jit(solution)/shard_map/gather/ppermute | solution.py:148
  24.6 10.5 %collective-permute-start.5 = (bf16[512,256]{1,0:T(8,128)(2,1)S(1)}, bf16[512,256]{1,0:T(8,128)(2,1)S(1)}, u32[]{:S(2)}, u32[]{:S(2)}) collective-permute-start(bf16[512,256]{1,0:T(8,128)(2,1)S(1)} %collective-permute-done.2.refs_0_.refs_3_), channel_id=1, source_target_pairs={{0,0},{1,4},{2,2},{3,6},{4,1},{5,5},{6,3},{7,7},{8,8},{9,12},{10,1... | collective-permute-start | bytes 786440 | tf_op jit(solution)/shard_map/gather/ppermute | solution.py:148
  35.1 2.4 %collective-permute-start.12 = (bf16[512,256]{1,0:T(8,128)(2,1)S(1)}, bf16[512,256]{1,0:T(8,128)(2,1)S(1)}, u32[]{:S(2)}, u32[]{:S(2)}) collective-permute-start(bf16[512,256]{1,0:T(8,128)(2,1)S(1)} %collective-permute-done.7.refs_9_), channel_id=1, source_target_pairs={{0,1},{1,0},{2,3},{3,2},{4,5},{5,4},{6,7},{7,6},{8,9},{9,8},{10,11... | collective-permute-start | bytes 786440 | tf_op jit(solution)/shard_map/gather/ppermute | solution.py:148
  36.4 3.1 %collective-permute-start.11 = (bf16[512,256]{1,0:T(8,128)(2,1)S(1)}, bf16[512,256]{1,0:T(8,128)(2,1)S(1)}, u32[]{:S(2)}, u32[]{:S(2)}) collective-permute-start(bf16[512,256]{1,0:T(8,128)(2,1)S(1)} %collective-permute-done.8.refs_9_.refs_1_), channel_id=1, source_target_pairs={{0,1},{1,0},{2,3},{3,2},{4,5},{5,4},{6,7},{7,6},{8,9},{9,8},{10,11... | collective-permute-start | bytes 786440 | tf_op jit(solution)/shard_map/gather/ppermute | solution.py:148
  41.4 2.5 %collective-permute-start.14 = (f32[512,256]{1,0:T(8,128)S(1)}, f32[512,256]{1,0:T(8,128)S(1)}, u32[]{:S(2)}, u32[]{:S(2)}) collective-permute-start(f32[512,256]{1,0:T(8,128)S(1)} %get-tuple-element.55), channel_id=1, source_target_pairs={{0,1},{1,0},{2,3},{3,2},{4,5},{5,4},{6,7},{7,6},{8,9},{9,8},{10,11... | collective-permute-start | bytes 1572872 | tf_op jit(solution)/shard_map/ppermute | solution.py:148
  43.8 9.0 %collective-permute-start.13 = (bf16[272,512]{1,0:T(8,128)(2,1)S(1)}, bf16[272,512]{1,0:T(8,128)(2,1)S(1)}, u32[]{:S(2)}, u32[]{:S(2)}) collective-permute-start(bf16[272,512]{1,0:T(8,128)(2,1)S(1)} %get-tuple-element.51.refs_0_), channel_id=1, source_target_pairs={{0,3},{1,7},{2,1},{3,5},{4,2},{5,6},{6,0},{7,4},{8,11},{9,15},{10,... | collective-permute-start | bytes 835592 | tf_op jit(solution)/shard_map/ppermute | solution.py:148
  44.2 8.6 %collective-permute-start.16 = (bf16[272,256]{1,0:T(8,128)(2,1)S(1)}, bf16[272,256]{1,0:T(8,128)(2,1)S(1)}, u32[]{:S(2)}, u32[]{:S(2)}) collective-permute-start(bf16[272,256]{1,0:T(8,128)(2,1)S(1)} %get-tuple-element.56.refs_0_), channel_id=1, source_target_pairs={{0,16},{1,17},{2,18},{3,19},{4,20},{5,21},{6,22},{7,23},{8,24},{9,... | collective-permute-start | bytes 417800 | tf_op jit(solution)/shard_map/ppermute | solution.py:148
  45.7 15.6 %collective-permute-start.15 = (bf16[272,512]{1,0:T(8,128)(2,1)S(1)}, bf16[272,512]{1,0:T(8,128)(2,1)S(1)}, u32[]{:S(2)}, u32[]{:S(2)}) collective-permute-start(bf16[272,512]{1,0:T(8,128)(2,1)S(1)} %gamma_block.3.refs_0_), channel_id=1, source_target_pairs={{0,2},{1,6},{2,0},{3,4},{4,3},{5,7},{6,1},{7,5},{8,10},{9,14},{10,... | collective-permute-start | bytes 835592 | tf_op jit(solution)/shard_map/ppermute | solution.py:148
  49.7 14.7 %collective-permute-start.18 = (bf16[272,512]{1,0:T(8,128)(2,1)S(1)}, bf16[272,512]{1,0:T(8,128)(2,1)S(1)}, u32[]{:S(2)}, u32[]{:S(2)}) collective-permute-start(bf16[272,512]{1,0:T(8,128)(2,1)S(1)} %gamma_block.4.refs_0_), channel_id=1, source_target_pairs={{0,1},{1,5},{2,3},{3,7},{4,0},{5,4},{6,2},{7,6},{8,9},{9,13},{10,1... | collective-permute-start | bytes 835592 | tf_op jit(solution)/shard_map/ppermute | solution.py:148
  54.5 16.5 %collective-permute-start.19 = (bf16[272,512]{1,0:T(8,128)(2,1)S(1)}, bf16[272,512]{1,0:T(8,128)(2,1)S(1)}, u32[]{:S(2)}, u32[]{:S(2)}) collective-permute-start(bf16[272,512]{1,0:T(8,128)(2,1)S(1)} %gamma_block.5.refs_0_), channel_id=1, source_target_pairs={{0,0},{1,4},{2,2},{3,6},{4,1},{5,5},{6,3},{7,7},{8,8},{9,12},{10,1... | collective-permute-start | bytes 835592 | tf_op jit(solution)/shard_map/ppermute | solution.py:148
  57.9 3.3 %collective-permute-start.17 = (bf16[144,256]{1,0:T(8,128)(2,1)S(1)}, bf16[144,256]{1,0:T(8,128)(2,1)S(1)}, u32[]{:S(2)}, u32[]{:S(2)}) collective-permute-start(bf16[144,256]{1,0:T(8,128)(2,1)S(1)} %get-tuple-element.59.refs_0_), channel_id=1, source_target_pairs={{0,8},{1,9},{2,10},{3,11},{4,12},{5,13},{6,14},{7,15},{8,0},{9,1},... | collective-permute-start | bytes 221192 | tf_op jit(solution)/shard_map/ppermute | solution.py:148
  61.3 4.1 %collective-permute-start.22 = (f32[64,256]{1,0:T(8,128)S(1)}, f32[64,256]{1,0:T(8,128)S(1)}, u32[]{:S(2)}, u32[]{:S(2)}) collective-permute-start(f32[64,256]{1,0:T(8,128)S(1)} %get-tuple-element.61), channel_id=1, source_target_pairs={{0,6},{1,7},{2,4},{3,5},{4,2},{5,3},{6,0},{7,1},{8,14},{9,15},{10,... | collective-permute-start | bytes 196616 | tf_op jit(solution)/shard_map/ppermute | solution.py:148
  61.4 5.2 %collective-permute-start.21 = (f32[64,256]{1,0:T(8,128)S(1)}, f32[64,256]{1,0:T(8,128)S(1)}, u32[]{:S(2)}, u32[]{:S(2)}) collective-permute-start(f32[64,256]{1,0:T(8,128)S(1)} %get-tuple-element.61), channel_id=1, source_target_pairs={{0,4},{1,5},{2,6},{3,7},{4,0},{5,1},{6,2},{7,3},{8,12},{9,13},{10,... | collective-permute-start | bytes 196616 | tf_op jit(solution)/shard_map/ppermute | solution.py:148
  64.0 3.4 %collective-permute-start.20 = (f32[64,256]{1,0:T(8,128)S(1)}, f32[64,256]{1,0:T(8,128)S(1)}, u32[]{:S(2)}, u32[]{:S(2)}) collective-permute-start(f32[64,256]{1,0:T(8,128)S(1)} %get-tuple-element.60.refs_0_.mine), channel_id=1, source_target_pairs={{0,2},{1,3},{2,0},{3,1},{4,6},{5,7},{6,4},{7,5},{8,10},{9,11},{10,... | collective-permute-start | bytes 196616 | tf_op jit(solution)/shard_map/ppermute | solution.py:148
  67.4 3.0 %collective-permute-start.23 = (f32[64,256]{1,0:T(8,128)S(1)}, f32[64,256]{1,0:T(8,128)S(1)}, u32[]{:S(2)}, u32[]{:S(2)}) collective-permute-start(f32[64,256]{1,0:T(8,128)S(1)} %density_block.1.refs_0_.block), channel_id=1, source_target_pairs={{0,1},{1,0},{2,3},{3,2},{4,5},{5,4},{6,7},{7,6},{8,9},{9,8},{10,11... | collective-permute-start | bytes 196616 | tf_op jit(solution)/shard_map/ppermute | solution.py:148
  (4 other events, 54.4 us)

commit v4 on v3

--- a/solution.py
+++ b/solution.py
@@ -234,19 +234,21 @@
     z, y, x, c = place_bits()
     left = read_left(refs[2:8])
     right = [ref[...] for ref in refs[8:12]]
-    first_amp, first_mixed = refs[12:14]
-    mixed_out, dens_keep, dens_send, amp = refs[-4:]
+    amp_out, mixed_out = refs[-2:]
     layer = jnp.where(x == 1, z ^ 3, z ^ 2)
     amp_half, mixed = pair_terms(refs[0], refs[1], layer, left, right)
     outside = (x == 0) & (c == y)
-    mixed_half = jnp.where(outside, 0.0, mixed).astype(jnp.bfloat16)
-    amp[...] = amp_half
-    mixed_out[...] = mixed_half
-    half = amp.shape[0] // 2
-    mixed_first = first_mixed[...]
-    for out, core in ((dens_send, 1 - c), (dens_keep, c)):
+    amp_out[...] = amp_half
+    mixed_out[...] = jnp.where(outside, 0.0, mixed).astype(jnp.bfloat16)
+
+
+def density_pairs_kernel(first_amp, first_mixed, last_amp, last_mixed, keep_out, send_out):
+    z, y, x, c = place_bits()
+    half = keep_out.shape[1]
+    for out, core in ((send_out, 1 - c), (keep_out, c)):
         rows = pl.ds(pl.multiple_of(core * half, half), half)
-        out[...] = dot(mixed_half, amp[rows, :], NT) + dot(mixed_first, first_amp[rows, :], NT)
+        first = dot(first_mixed[...], first_amp[rows, :], NT)
+        out[...] = first + dot(last_mixed[...], last_amp[rows, :], NT)
 
 
 def metric_product(step, metric_high, metric_low, high, low):
@@ -371,8 +373,14 @@
     def first_partner(value):
         return move(value, lambda z, y, x, c: (z if x else z ^ 1, y, x, c))
 
+    def first_partner_cross(value):
+        return move(value, lambda z, y, x, c: (z ^ 1 if x else z, y, 1 - x, c))
+
     def last_partner(value):
         return move(value, lambda z, y, x, c: (z ^ 3 if x else z ^ 2, y, x, c))
+
+    def last_partner_cross(value):
+        return move(value, lambda z, y, x, c: (z ^ 2 if x else z ^ 3, y, 1 - x, c))
 
     def near_left(value):
         return move(value, lambda z, y, x, c: (z, 1 - y, x, c) if c == y else (z, y, x, 1 - c))
@@ -399,75 +407,65 @@
                 compiler_params=params,
                 cost_estimate=pl.CostEstimate(
                     flops=flops,
-                    bytes_accessed=sum(2 * operand.size for operand in operands),
+                    bytes_accessed=0,
                     transcendentals=0,
                 ),
             )(*operands, *earlier)
-
-    with jax.named_scope("gather"):
-        far_own, near_own, swapped, first_own, last_own = lax.optimization_barrier(
-            (far_left(own), near_left(own), x_swap(own), first_partner(own), last_partner(own))
-        )
 
     metric_high, metric_low = call(
         "metric_turn",
         turn_metric_kernel,
         [shape(jnp.bfloat16, n_sec, width, aux_total)] * 2,
         [metric],
-        [swapped],
         flops=4 * aux_total * aux_total * width,
     )
-
     with jax.named_scope("gather"):
-        (
-            far_swapped,
-            near_swapped,
-            first_swapped,
-            last_swapped,
-            last_own_got,
-            first_own_got,
-            metric_high,
-            metric_low,
-        ) = lax.optimization_barrier(
+        swapped, last_own, metric_high, metric_low = (
+            lax.optimization_barrier(
+                (
+                    x_swap(own),
+                    last_partner(own),
+                    metric_high,
+                    metric_low,
+                )
+            )
+        )
+        far_own, near_own, first_own, first_cross, last_swapped = lax.optimization_barrier(
             (
-                far_left(swapped),
-                near_left(swapped),
-                first_partner(swapped),
+                far_left(own),
+                near_left(own),
+                first_partner(own),
+                first_partner_cross(own),
                 last_partner(swapped),
-                core_swap(last_own),
-                core_swap(first_own),
-                metric_high,
-                metric_low,
             )
         )
+        far_swapped, near_swapped = far_left(swapped), near_left(swapped)
         left = [own, swapped, near_own, near_swapped, far_own, far_swapped]
-        first = [first_own, first_swapped, first_own_got, core_swap(first_swapped)]
-        last = [last_own, last_swapped, last_own_got, core_swap(last_swapped)]
+        first = [first_own, first_cross, core_swap(first_own), core_swap(first_cross)]
+        last = [last_own, last_swapped, core_swap(last_own), core_swap(last_swapped)]
 
     energies = [occ_energy[None, :], vir_energy[None, :]]
-    pair_flops = 3 * square * aux_total
+    half_square = shape(jnp.bfloat16, virtuals, virtuals)
     grad, first_amp, first_mixed = call(
         "first_pair",
         first_pair_kernel,
-        [
-            shape(jnp.float32, virtuals, aux_total),
-            shape(jnp.bfloat16, virtuals, virtuals),
-            shape(jnp.bfloat16, virtuals, virtuals),
-        ],
+        [shape(jnp.float32, virtuals, aux_total), half_square, half_square],
         energies + left + first,
-        flops=pair_flops,
-    )
-    last_mixed, dens_keep, dens_send = call(
+    )
+    last_amp, last_mixed = call(
         "last_pair",
         last_pair_kernel,
-        [
-            shape(jnp.bfloat16, virtuals, virtuals),
-            shape(jnp.float32, virtuals, half),
-            shape(jnp.float32, virtuals, half),
-        ],
-        energies + left + last + [first_amp, first_mixed],
-        scratch=[pltpu.VMEM((virtuals, virtuals), jnp.bfloat16)],
-        flops=pair_flops,
+        [half_square, half_square],
+        energies + left + last,
+        [first_amp],
+        flops=4 * square * aux_total,
+    )
+    dens_keep, dens_send = call(
+        "density_pairs",
+        density_pairs_kernel,
+        [shape(jnp.float32, virtuals, half)] * 2,
+        [first_amp, first_mixed, last_amp, last_mixed],
+        flops=2 * square * virtuals,
     )
     dens_got = core_swap(dens_send)
 
@@ -520,18 +518,18 @@
     got_second = gamma_move(2, second)
     first_block = gamma_block(1, second)
     got_first = gamma_move(1, first_block)
+    zeroth = gamma_block(0, first_block)
+    got_zeroth = gamma_move(0, zeroth)
     keep, packed = density_half(
-        "density_layers", density_layers_kernel, 2 * rows, keep, got, first_block, got_third
+        "density_layers", density_layers_kernel, 2 * rows, keep, got, zeroth
     )
     got = move(packed, lambda z, y, x, c: (z ^ 1, y, x, c))
-    zeroth = gamma_block(0, packed)
-    got_zeroth = gamma_move(0, zeroth)
     mine, theirs = call(
         "density_rows",
         density_rows_kernel,
         [shape(jnp.float32, rows, half)] * 2,
         [keep, got],
-        [zeroth, got_second],
+        [got_third],
         [pltpu.VMEM(keep.shape, jnp.float32)],
     )
     from_x, from_y, from_xy = x_swap(mine), y_swap(theirs), xy_swap(theirs)

time: 72.9 us -> 65.7 us (0.901)
  waiting for transfers between devices: 20.6 us -> 13.7 us
    ppermute x24, waiting for transfers between devices: 20.6 us -> 13.7 us  [send(): return lax.ppermute(value, AXES, pairs)]
    pallas_call x14 -> x15, Pallas kernels: 14.1 us -> 14.3 us  [call(): pl.pallas_call(kernel, in_specs=[vmem] * len(operands) + [unread] * len(e...]
  transfers between devices with their start and end apart: 24 -> 24, of which waited for: 11 -> 8; matrix products, arithmetic and copies ran while one was open for 0% -> 0% of each run, Pallas kernels for 15% -> 18%
where the time goes in v4:
time: 65.7 us; the launch traced here: 65.4 us
  starting transfers between devices  34.4 us (52%)
  Pallas kernels  14.3 us (22%)
  waiting for transfers between devices  13.7 us (21%)
  local copies, waits for them, and re-layouts  2.19 us (3%)
  between operations  0.85 us (1%)
    ppermute x24, starting transfers between devices, send(): return lax.ppermute(value, AXES, pairs)  34.4 us
    pallas_call x15, Pallas kernels, call(): pl.pallas_call(kernel, in_specs=[vmem] * len(operands) + [unread] * len(e...  14.3 us
    ppermute x24, waiting for transfers between devices, send(): return lax.ppermute(value, AXES, pairs)  13.7 us
    unnamed x8, local copies, waits for them, and re-layouts  2.19 us
  transfers between devices with their start and end apart: 24, of which 8 were waited for; matrix products, arithmetic and copies ran while one was open for 0% of the time, Pallas kernels for 18%

profile of v4, /device:TPU:1, one launch (start us, length us, event | category | flops | bytes accessed | tf_op | source)
XLA Modules:
  0.0 65.4 jit_solution(16545601546572417863)
XLA Ops:
  0.6 2.1 %collective-permute-start = (bf16[512,256]{1,0:T(8,128)(2,1)}, bf16[512,256]{1,0:T(8,128)(2,1)S(1)}, u32[]{:S(2)}, u32[]{:S(2)}) collective-permute-start(bf16[512,256]{1,0:T(8,128)(2,1)} %bitcast.3), channel_id=1, source_target_pairs={{0,2},{1,3},{2,0},{3,1},{4,6},{5,7},{6,4},{7,5},{8,10},{9,11},{10,... | collective-permute-start | bytes 786440 | tf_op jit(solution)/shard_map/gather/ppermute | solution.py:148
  2.7 2.3 %collective-permute-start.1 = (bf16[512,256]{1,0:T(8,128)(2,1)}, bf16[512,256]{1,0:T(8,128)(2,1)S(1)}, u32[]{:S(2)}, u32[]{:S(2)}) collective-permute-start(bf16[512,256]{1,0:T(8,128)(2,1)} %bitcast.4), channel_id=1, source_target_pairs={{0,16},{1,17},{2,26},{3,27},{4,20},{5,21},{6,30},{7,31},{8,24},{9,... | collective-permute-start | bytes 786440 | tf_op jit(solution)/shard_map/gather/ppermute | solution.py:148
  5.1 4.3 %collective-permute-start.2 = (bf16[512,256]{1,0:T(8,128)(2,1)}, bf16[512,256]{1,0:T(8,128)(2,1)S(1)}, u32[]{:S(2)}, u32[]{:S(2)}) collective-permute-start(bf16[512,256]{1,0:T(8,128)(2,1)} %bitcast.5), channel_id=1, source_target_pairs={{0,0},{1,4},{2,2},{3,6},{4,1},{5,5},{6,3},{7,7},{8,8},{9,12},{10,1... | collective-permute-start | bytes 786440 | tf_op jit(solution)/shard_map/gather/ppermute | solution.py:148
  9.3 3.2 %collective-permute-start.4 = (bf16[512,256]{1,0:T(8,128)(2,1)}, bf16[512,256]{1,0:T(8,128)(2,1)S(1)}, u32[]{:S(2)}, u32[]{:S(2)}) collective-permute-start(bf16[512,256]{1,0:T(8,128)(2,1)} %bitcast.7), channel_id=1, source_target_pairs={{0,8},{1,9},{2,2},{3,3},{4,12},{5,13},{6,6},{7,7},{8,0},{9,1},{10,... | collective-permute-start | bytes 786440 | tf_op jit(solution)/shard_map/gather/ppermute | solution.py:148
  12.6 2.2 %copy-done = f32[1024,1024]{1,0:T(8,128)S(1)} copy-done((f32[1024,1024]{1,0:T(8,128)S(1)}, f32[1024,1024]{1,0:T(8,128)}, u32[]{:S(2)}) %copy-start) | copy-done | bytes 4194328
  14.8 1.3 %metric_turn.1 = (bf16[4,256,1024]{2,1,0:T(8,128)(2,1)S(1)}, bf16[4,256,1024]{2,1,0:T(8,128)(2,1)S(1)}) custom-call(f32[1024,1024]{1,0:T(8,128)S(1)} %copy-done), custom_call_target="tpu_custom_call" | custom-call | flops 1073741824 | tf_op jit(solution)/shard_map/metric_turn/pallas_call | solution.py:401
  16.7 1.6 %collective-permute-start.7 = (bf16[512,256]{1,0:T(8,128)(2,1)S(1)}, bf16[512,256]{1,0:T(8,128)(2,1)S(1)}, u32[]{:S(2)}, u32[]{:S(2)}) collective-permute-start(bf16[512,256]{1,0:T(8,128)(2,1)S(1)} %collective-permute-done.refs_3_), channel_id=1, source_target_pairs={{0,4},{1,0},{2,6},{3,2},{4,5},{5,1},{6,7},{7,3},{8,12},{9,8},{10,1... | collective-permute-start | bytes 786440 | tf_op jit(solution)/shard_map/gather/ppermute | solution.py:148
  18.3 3.0 %collective-permute-start.8 = (bf16[512,256]{1,0:T(8,128)(2,1)S(1)}, bf16[512,256]{1,0:T(8,128)(2,1)S(1)}, u32[]{:S(2)}, u32[]{:S(2)}) collective-permute-start(bf16[512,256]{1,0:T(8,128)(2,1)S(1)} %collective-permute-done.refs_3_), channel_id=1, source_target_pairs={{0,0},{1,4},{2,2},{3,6},{4,1},{5,5},{6,3},{7,7},{8,8},{9,12},{10,1... | collective-permute-start | bytes 786440 | tf_op jit(solution)/shard_map/gather/ppermute | solution.py:148
  21.4 3.9 %collective-permute-done.4.refs_8_ = bf16[512,256]{1,0:T(8,128)(2,1)S(1)} collective-permute-done((bf16[512,256]{1,0:T(8,128)(2,1)}, bf16[512,256]{1,0:T(8,128)(2,1)S(1)}, u32[]{:S(2)}, u32[]{:S(2)}) %collective-permute-start.4) | collective-permute-done | bytes 262176 | tf_op jit(solution)/shard_map/gather/ppermute | solution.py:148
  25.3 4.2 %collective-permute-done.6.refs_9_.refs_1_ = bf16[512,256]{1,0:T(8,128)(2,1)S(1)} collective-permute-done((bf16[512,256]{1,0:T(8,128)(2,1)S(1)}, bf16[512,256]{1,0:T(8,128)(2,1)S(1)}, u32[]{:S(2)}, u32[]{:S(2)}) %collective-permute-start.6) | collective-permute-done | bytes 262176 | tf_op jit(solution)/shard_map/gather/ppermute | solution.py:148
  29.6 2.4 %collective-permute-start.11 = (bf16[512,256]{1,0:T(8,128)(2,1)S(1)}, bf16[512,256]{1,0:T(8,128)(2,1)S(1)}, u32[]{:S(2)}, u32[]{:S(2)}) collective-permute-start(bf16[512,256]{1,0:T(8,128)(2,1)S(1)} %collective-permute-done.4.refs_8_), channel_id=1, source_target_pairs={{0,1},{1,0},{2,3},{3,2},{4,5},{5,4},{6,7},{7,6},{8,9},{9,8},{10,11... | collective-permute-start | bytes 786440 | tf_op jit(solution)/shard_map/gather/ppermute | solution.py:148
  33.5 1.9 %first_pair.1 = (f32[512,1024]{1,0:T(8,128)S(1)}, bf16[512,512]{1,0:T(8,128)(2,1)S(1)}, bf16[512,512]{1,0:T(8,128)(2,1)S(1)}) custom-call(f32[1,8]{1,0:T(1,128)S(1)} %bitcast.13, f32[1,512]{1,0:T(1,128)S(1)} %bitcast.11, bf16[512,256]{1,0:T(8,128)(2,1)S(1)} %bitcast.9, bf16[512,256]{1,0:T(8,128)(2,1)S(1)} %collective-permute-done.refs_3_, ...), custom_call_target="tpu_custom_call" | custom-call | tf_op jit(solution)/shard_map/first_pair/pallas_call | solution.py:401
  35.5 1.4 %last_pair.1 = (bf16[512,512]{1,0:T(8,128)(2,1)S(1)}, bf16[512,512]{1,0:T(8,128)(2,1)S(1)}) custom-call(f32[1,8]{1,0:T(1,128)S(1)} %bitcast.14, f32[1,512]{1,0:T(1,128)S(1)} %bitcast.12, bf16[512,256]{1,0:T(8,128)(2,1)S(1)} %bitcast.10, bf16[512,256]{1,0:T(8,128)(2,1)S(1)} %collective-permute-done.refs_3_, ...), custom_call_target="tpu_custom_call" | custom-call | flops 2147483648 | tf_op jit(solution)/shard_map/last_pair/pallas_call | solution.py:401
  38.1 2.0 %gradient.1 = (bf16[512,1024]{1,0:T(8,128)(2,1)S(1)}, bf16[512,1024]{1,0:T(8,128)(2,1)S(1)}, bf16[272,512]{1,0:T(8,128)(2,1)S(1)}) custom-call(bf16[512,512]{1,0:T(8,128)(2,1)S(1)} %get-tuple-element.39.mixed.last_mixed, bf16[512,256]{1,0:T(8,128)(2,1)S(1)} %collective-permute-done.1.refs_8_.refs_0_, ...), custom_call_target="tpu_custom_call" | custom-call | flops 1610612736 | tf_op jit(solution)/shard_map/gradient/pallas_call | solution.py:401
  40.5 2.1 %collective-permute-start.16 = (bf16[272,256]{1,0:T(8,128)(2,1)S(1)}, bf16[272,256]{1,0:T(8,128)(2,1)S(1)}, u32[]{:S(2)}, u32[]{:S(2)}) collective-permute-start(bf16[272,256]{1,0:T(8,128)(2,1)S(1)} %get-tuple-element.50.refs_0_), channel_id=1, source_target_pairs={{0,16},{1,17},{2,18},{3,19},{4,20},{5,21},{6,22},{7,23},{8,24},{9,... | collective-permute-start | bytes 417800 | tf_op jit(solution)/shard_map/ppermute | solution.py:148
  42.5 1.3 %gamma_block.3.refs_0_ = bf16[272,512]{1,0:T(8,128)(2,1)S(1)} custom-call(bf16[4,256,1024]{2,1,0:T(8,128)(2,1)S(1)} %get-tuple-element.41.refs_5_.metric_high, bf16[4,256,1024]{2,1,0:T(8,128)(2,1)S(1)} %get-tuple-element.42.refs_6_.metric_low, bf16[512,1024]{1,0:T(8,128)(2,1)S(1)} %get-tuple-element.44.high, bf16[512,1024]{1,0:T(8,128)(2,1)S(1)} %get-tuple-element.45.low, ...), custom_call_target="tpu_custom_call" | custom-call | flops 805306368 | tf_op jit(solution)/shard_map/gamma_block/pallas_call | solution.py:401
  44.6 1.3 %gamma_block.4.refs_0_ = bf16[272,512]{1,0:T(8,128)(2,1)S(1)} custom-call(bf16[4,256,1024]{2,1,0:T(8,128)(2,1)S(1)} %get-tuple-element.41.refs_5_.metric_high, bf16[4,256,1024]{2,1,0:T(8,128)(2,1)S(1)} %get-tuple-element.42.refs_6_.metric_low, bf16[512,1024]{1,0:T(8,128)(2,1)S(1)} %get-tuple-element.44.high, bf16[512,1024]{1,0:T(8,128)(2,1)S(1)} %get-tuple-element.45.low, ...), custom_call_target="tpu_custom_call" | custom-call | flops 805306368 | tf_op jit(solution)/shard_map/gamma_block/pallas_call | solution.py:401
  46.0 1.3 %gamma_block.5.refs_0_ = bf16[272,512]{1,0:T(8,128)(2,1)S(1)} custom-call(bf16[4,256,1024]{2,1,0:T(8,128)(2,1)S(1)} %get-tuple-element.41.refs_5_.metric_high, bf16[4,256,1024]{2,1,0:T(8,128)(2,1)S(1)} %get-tuple-element.42.refs_6_.metric_low, bf16[512,1024]{1,0:T(8,128)(2,1)S(1)} %get-tuple-element.44.high, bf16[512,1024]{1,0:T(8,128)(2,1)S(1)} %get-tuple-element.45.low, ...), custom_call_target="tpu_custom_call" | custom-call | flops 805306368 | tf_op jit(solution)/shard_map/gamma_block/pallas_call | solution.py:401
  47.4 3.1 %collective-permute-start.19 = (bf16[272,512]{1,0:T(8,128)(2,1)S(1)}, bf16[272,512]{1,0:T(8,128)(2,1)S(1)}, u32[]{:S(2)}, u32[]{:S(2)}) collective-permute-start(bf16[272,512]{1,0:T(8,128)(2,1)S(1)} %gamma_block.5.refs_0_), channel_id=1, source_target_pairs={{0,0},{1,4},{2,2},{3,6},{4,1},{5,5},{6,3},{7,7},{8,8},{9,12},{10,1... | collective-permute-start | bytes 835592 | tf_op jit(solution)/shard_map/ppermute | solution.py:148
  50.8 3.0 %collective-permute-start.17 = (bf16[144,256]{1,0:T(8,128)(2,1)S(1)}, bf16[144,256]{1,0:T(8,128)(2,1)S(1)}, u32[]{:S(2)}, u32[]{:S(2)}) collective-permute-start(bf16[144,256]{1,0:T(8,128)(2,1)S(1)} %get-tuple-element.53), channel_id=1, source_target_pairs={{0,8},{1,9},{2,10},{3,11},{4,12},{5,13},{6,14},{7,15},{8,0},{9,1},... | collective-permute-start | bytes 221192 | tf_op jit(solution)/shard_map/ppermute | solution.py:148
  53.8 1.7 %collective-permute-done.17.got = bf16[144,256]{1,0:T(8,128)(2,1)S(1)} collective-permute-done((bf16[144,256]{1,0:T(8,128)(2,1)S(1)}, bf16[144,256]{1,0:T(8,128)(2,1)S(1)}, u32[]{:S(2)}, u32[]{:S(2)}) %collective-permute-start.17) | collective-permute-done | bytes 73760 | tf_op jit(solution)/shard_map/ppermute | solution.py:148
  56.4 2.0 %collective-permute-start.22 = (f32[64,256]{1,0:T(8,128)S(1)}, f32[64,256]{1,0:T(8,128)S(1)}, u32[]{:S(2)}, u32[]{:S(2)}) collective-permute-start(f32[64,256]{1,0:T(8,128)S(1)} %get-tuple-element.55), channel_id=1, source_target_pairs={{0,6},{1,7},{2,4},{3,5},{4,2},{5,3},{6,0},{7,1},{8,14},{9,15},{10,... | collective-permute-start | bytes 196616 | tf_op jit(solution)/shard_map/ppermute | solution.py:148
  59.5 1.4 %collective-permute-done.22.from_xy = f32[64,256]{1,0:T(8,128)S(1)} collective-permute-done((f32[64,256]{1,0:T(8,128)S(1)}, f32[64,256]{1,0:T(8,128)S(1)}, u32[]{:S(2)}, u32[]{:S(2)}) %collective-permute-start.22) | collective-permute-done | bytes 65568 | tf_op jit(solution)/shard_map/ppermute | solution.py:148
  60.9 2.6 %collective-permute-start.23 = (f32[64,256]{1,0:T(8,128)S(1)}, f32[64,256]{1,0:T(8,128)S(1)}, u32[]{:S(2)}, u32[]{:S(2)}) collective-permute-start(f32[64,256]{1,0:T(8,128)S(1)} %density_block.1.refs_0_.block), channel_id=1, source_target_pairs={{0,1},{1,0},{2,3},{3,2},{4,5},{5,4},{6,7},{7,6},{8,9},{9,8},{10,11... | collective-permute-start | bytes 196616 | tf_op jit(solution)/shard_map/ppermute | solution.py:148
  (47 shorter events, 8.8 us)
Async XLA Ops:
  0.6 15.4 %collective-permute-start = (bf16[512,256]{1,0:T(8,128)(2,1)}, bf16[512,256]{1,0:T(8,128)(2,1)S(1)}, u32[]{:S(2)}, u32[]{:S(2)}) collective-permute-start(bf16[512,256]{1,0:T(8,128)(2,1)} %bitcast.3), channel_id=1, source_target_pairs={{0,2},{1,3},{2,0},{3,1},{4,6},{5,7},{6,4},{7,5},{8,10},{9,11},{10,... | collective-permute-start | bytes 786440 | tf_op jit(solution)/shard_map/gather/ppermute | solution.py:148
  2.7 13.9 %collective-permute-start.1 = (bf16[512,256]{1,0:T(8,128)(2,1)}, bf16[512,256]{1,0:T(8,128)(2,1)S(1)}, u32[]{:S(2)}, u32[]{:S(2)}) collective-permute-start(bf16[512,256]{1,0:T(8,128)(2,1)} %bitcast.4), channel_id=1, source_target_pairs={{0,16},{1,17},{2,26},{3,27},{4,20},{5,21},{6,30},{7,31},{8,24},{9,... | collective-permute-start | bytes 786440 | tf_op jit(solution)/shard_map/gather/ppermute | solution.py:148
  5.1 11.6 %collective-permute-start.2 = (bf16[512,256]{1,0:T(8,128)(2,1)}, bf16[512,256]{1,0:T(8,128)(2,1)S(1)}, u32[]{:S(2)}, u32[]{:S(2)}) collective-permute-start(bf16[512,256]{1,0:T(8,128)(2,1)} %bitcast.5), channel_id=1, source_target_pairs={{0,0},{1,4},{2,2},{3,6},{4,1},{5,5},{6,3},{7,7},{8,8},{9,12},{10,1... | collective-permute-start | bytes 786440 | tf_op jit(solution)/shard_map/gather/ppermute | solution.py:148
  9.3 9.0 %collective-permute-start.3 = (bf16[512,256]{1,0:T(8,128)(2,1)}, bf16[512,256]{1,0:T(8,128)(2,1)S(1)}, u32[]{:S(2)}, u32[]{:S(2)}) collective-permute-start(bf16[512,256]{1,0:T(8,128)(2,1)} %bitcast.6), channel_id=1, source_target_pairs={{0,4},{1,0},{2,6},{3,2},{4,5},{5,1},{6,7},{7,3},{8,12},{9,8},{10,1... | collective-permute-start | bytes 786440 | tf_op jit(solution)/shard_map/gather/ppermute | solution.py:148
  9.3 16.0 %collective-permute-start.4 = (bf16[512,256]{1,0:T(8,128)(2,1)}, bf16[512,256]{1,0:T(8,128)(2,1)S(1)}, u32[]{:S(2)}, u32[]{:S(2)}) collective-permute-start(bf16[512,256]{1,0:T(8,128)(2,1)} %bitcast.7), channel_id=1, source_target_pairs={{0,8},{1,9},{2,2},{3,3},{4,12},{5,13},{6,6},{7,7},{8,0},{9,1},{10,... | collective-permute-start | bytes 786440 | tf_op jit(solution)/shard_map/gather/ppermute | solution.py:148
  16.1 9.2 %collective-permute-start.5 = (bf16[512,256]{1,0:T(8,128)(2,1)S(1)}, bf16[512,256]{1,0:T(8,128)(2,1)S(1)}, u32[]{:S(2)}, u32[]{:S(2)}) collective-permute-start(bf16[512,256]{1,0:T(8,128)(2,1)S(1)} %bitcast.8), channel_id=1, source_target_pairs={{0,2},{1,3},{2,8},{3,9},{4,6},{5,7},{6,12},{7,13},{8,10},{9,11},{1... | collective-permute-start | bytes 786440 | tf_op jit(solution)/shard_map/gather/ppermute | solution.py:148
  16.7 12.9 %collective-permute-start.6 = (bf16[512,256]{1,0:T(8,128)(2,1)S(1)}, bf16[512,256]{1,0:T(8,128)(2,1)S(1)}, u32[]{:S(2)}, u32[]{:S(2)}) collective-permute-start(bf16[512,256]{1,0:T(8,128)(2,1)S(1)} %collective-permute-done.refs_3_), channel_id=1, source_target_pairs={{0,16},{1,17},{2,26},{3,27},{4,20},{5,21},{6,30},{7,31},{8,24},{9,... | collective-permute-start | bytes 786440 | tf_op jit(solution)/shard_map/gather/ppermute | solution.py:148
  16.7 15.8 %collective-permute-start.7 = (bf16[512,256]{1,0:T(8,128)(2,1)S(1)}, bf16[512,256]{1,0:T(8,128)(2,1)S(1)}, u32[]{:S(2)}, u32[]{:S(2)}) collective-permute-start(bf16[512,256]{1,0:T(8,128)(2,1)S(1)} %collective-permute-done.refs_3_), channel_id=1, source_target_pairs={{0,4},{1,0},{2,6},{3,2},{4,5},{5,1},{6,7},{7,3},{8,12},{9,8},{10,1... | collective-permute-start | bytes 786440 | tf_op jit(solution)/shard_map/gather/ppermute | solution.py:148
  18.3 14.2 %collective-permute-start.8 = (bf16[512,256]{1,0:T(8,128)(2,1)S(1)}, bf16[512,256]{1,0:T(8,128)(2,1)S(1)}, u32[]{:S(2)}, u32[]{:S(2)}) collective-permute-start(bf16[512,256]{1,0:T(8,128)(2,1)S(1)} %collective-permute-done.refs_3_), channel_id=1, source_target_pairs={{0,0},{1,4},{2,2},{3,6},{4,1},{5,5},{6,3},{7,7},{8,8},{9,12},{10,1... | collective-permute-start | bytes 786440 | tf_op jit(solution)/shard_map/gather/ppermute | solution.py:148
  29.6 3.6 %collective-permute-start.11 = (bf16[512,256]{1,0:T(8,128)(2,1)S(1)}, bf16[512,256]{1,0:T(8,128)(2,1)S(1)}, u32[]{:S(2)}, u32[]{:S(2)}) collective-permute-start(bf16[512,256]{1,0:T(8,128)(2,1)S(1)} %collective-permute-done.4.refs_8_), channel_id=1, source_target_pairs={{0,1},{1,0},{2,3},{3,2},{4,5},{5,4},{6,7},{7,6},{8,9},{9,8},{10,11... | collective-permute-start | bytes 786440 | tf_op jit(solution)/shard_map/gather/ppermute | solution.py:148
  32.0 1.5 %collective-permute-start.12 = (bf16[512,256]{1,0:T(8,128)(2,1)S(1)}, bf16[512,256]{1,0:T(8,128)(2,1)S(1)}, u32[]{:S(2)}, u32[]{:S(2)}) collective-permute-start(bf16[512,256]{1,0:T(8,128)(2,1)S(1)} %collective-permute-done.5.refs_9_), channel_id=1, source_target_pairs={{0,1},{1,0},{2,3},{3,2},{4,5},{5,4},{6,7},{7,6},{8,9},{9,8},{10,11... | collective-permute-start | bytes 786440 | tf_op jit(solution)/shard_map/gather/ppermute | solution.py:148
  32.0 3.5 %collective-permute-start.9 = (bf16[512,256]{1,0:T(8,128)(2,1)S(1)}, bf16[512,256]{1,0:T(8,128)(2,1)S(1)}, u32[]{:S(2)}, u32[]{:S(2)}) collective-permute-start(bf16[512,256]{1,0:T(8,128)(2,1)S(1)} %collective-permute-done.1.refs_8_.refs_0_), channel_id=1, source_target_pairs={{0,1},{1,0},{2,3},{3,2},{4,5},{5,4},{6,7},{7,6},{8,9},{9,8},{10,11... | collective-permute-start | bytes 786440 | tf_op jit(solution)/shard_map/gather/ppermute | solution.py:148
  32.5 3.0 %collective-permute-start.10 = (bf16[512,256]{1,0:T(8,128)(2,1)S(1)}, bf16[512,256]{1,0:T(8,128)(2,1)S(1)}, u32[]{:S(2)}, u32[]{:S(2)}) collective-permute-start(bf16[512,256]{1,0:T(8,128)(2,1)S(1)} %collective-permute-done.6.refs_9_.refs_1_), channel_id=1, source_target_pairs={{0,1},{1,0},{2,3},{3,2},{4,5},{5,4},{6,7},{7,6},{8,9},{9,8},{10,11... | collective-permute-start | bytes 786440 | tf_op jit(solution)/shard_map/gather/ppermute | solution.py:148
  37.6 2.5 %collective-permute-start.14 = (f32[512,256]{1,0:T(8,128)S(1)}, f32[512,256]{1,0:T(8,128)S(1)}, u32[]{:S(2)}, u32[]{:S(2)}) collective-permute-start(f32[512,256]{1,0:T(8,128)S(1)} %get-tuple-element.49), channel_id=1, source_target_pairs={{0,1},{1,0},{2,3},{3,2},{4,5},{5,4},{6,7},{7,6},{8,9},{9,8},{10,11... | collective-permute-start | bytes 1572872 | tf_op jit(solution)/shard_map/ppermute | solution.py:148
  40.1 13.7 %collective-permute-start.13 = (bf16[272,512]{1,0:T(8,128)(2,1)S(1)}, bf16[272,512]{1,0:T(8,128)(2,1)S(1)}, u32[]{:S(2)}, u32[]{:S(2)}) collective-permute-start(bf16[272,512]{1,0:T(8,128)(2,1)S(1)} %get-tuple-element.43.refs_0_), channel_id=1, source_target_pairs={{0,3},{1,7},{2,1},{3,5},{4,2},{5,6},{6,0},{7,4},{8,11},{9,15},{10,... | collective-permute-start | bytes 835592 | tf_op jit(solution)/shard_map/ppermute | solution.py:148
  40.5 10.0 %collective-permute-start.16 = (bf16[272,256]{1,0:T(8,128)(2,1)S(1)}, bf16[272,256]{1,0:T(8,128)(2,1)S(1)}, u32[]{:S(2)}, u32[]{:S(2)}) collective-permute-start(bf16[272,256]{1,0:T(8,128)(2,1)S(1)} %get-tuple-element.50.refs_0_), channel_id=1, source_target_pairs={{0,16},{1,17},{2,18},{3,19},{4,20},{5,21},{6,22},{7,23},{8,24},{9,... | collective-permute-start | bytes 417800 | tf_op jit(solution)/shard_map/ppermute | solution.py:148
  43.9 12.5 %collective-permute-start.15 = (bf16[272,512]{1,0:T(8,128)(2,1)S(1)}, bf16[272,512]{1,0:T(8,128)(2,1)S(1)}, u32[]{:S(2)}, u32[]{:S(2)}) collective-permute-start(bf16[272,512]{1,0:T(8,128)(2,1)S(1)} %gamma_block.3.refs_0_), channel_id=1, source_target_pairs={{0,2},{1,6},{2,0},{3,4},{4,3},{5,7},{6,1},{7,5},{8,10},{9,14},{10,... | collective-permute-start | bytes 835592 | tf_op jit(solution)/shard_map/ppermute | solution.py:148
  45.9 14.9 %collective-permute-start.18 = (bf16[272,512]{1,0:T(8,128)(2,1)S(1)}, bf16[272,512]{1,0:T(8,128)(2,1)S(1)}, u32[]{:S(2)}, u32[]{:S(2)}) collective-permute-start(bf16[272,512]{1,0:T(8,128)(2,1)S(1)} %gamma_block.4.refs_0_), channel_id=1, source_target_pairs={{0,1},{1,5},{2,3},{3,7},{4,0},{5,4},{6,2},{7,6},{8,9},{9,13},{10,1... | collective-permute-start | bytes 835592 | tf_op jit(solution)/shard_map/ppermute | solution.py:148
  47.4 16.1 %collective-permute-start.19 = (bf16[272,512]{1,0:T(8,128)(2,1)S(1)}, bf16[272,512]{1,0:T(8,128)(2,1)S(1)}, u32[]{:S(2)}, u32[]{:S(2)}) collective-permute-start(bf16[272,512]{1,0:T(8,128)(2,1)S(1)} %gamma_block.5.refs_0_), channel_id=1, source_target_pairs={{0,0},{1,4},{2,2},{3,6},{4,1},{5,5},{6,3},{7,7},{8,8},{9,12},{10,1... | collective-permute-start | bytes 835592 | tf_op jit(solution)/shard_map/ppermute | solution.py:148
  50.8 4.8 %collective-permute-start.17 = (bf16[144,256]{1,0:T(8,128)(2,1)S(1)}, bf16[144,256]{1,0:T(8,128)(2,1)S(1)}, u32[]{:S(2)}, u32[]{:S(2)}) collective-permute-start(bf16[144,256]{1,0:T(8,128)(2,1)S(1)} %get-tuple-element.53), channel_id=1, source_target_pairs={{0,8},{1,9},{2,10},{3,11},{4,12},{5,13},{6,14},{7,15},{8,0},{9,1},... | collective-permute-start | bytes 221192 | tf_op jit(solution)/shard_map/ppermute | solution.py:148
  55.6 3.9 %collective-permute-start.20 = (f32[64,256]{1,0:T(8,128)S(1)}, f32[64,256]{1,0:T(8,128)S(1)}, u32[]{:S(2)}, u32[]{:S(2)}) collective-permute-start(f32[64,256]{1,0:T(8,128)S(1)} %get-tuple-element.54.refs_0_.mine), channel_id=1, source_target_pairs={{0,2},{1,3},{2,0},{3,1},{4,6},{5,7},{6,4},{7,5},{8,10},{9,11},{10,... | collective-permute-start | bytes 196616 | tf_op jit(solution)/shard_map/ppermute | solution.py:148
  56.0 3.4 %collective-permute-start.21 = (f32[64,256]{1,0:T(8,128)S(1)}, f32[64,256]{1,0:T(8,128)S(1)}, u32[]{:S(2)}, u32[]{:S(2)}) collective-permute-start(f32[64,256]{1,0:T(8,128)S(1)} %get-tuple-element.55), channel_id=1, source_target_pairs={{0,4},{1,5},{2,6},{3,7},{4,0},{5,1},{6,2},{7,3},{8,12},{9,13},{10,... | collective-permute-start | bytes 196616 | tf_op jit(solution)/shard_map/ppermute | solution.py:148
  56.4 4.5 %collective-permute-start.22 = (f32[64,256]{1,0:T(8,128)S(1)}, f32[64,256]{1,0:T(8,128)S(1)}, u32[]{:S(2)}, u32[]{:S(2)}) collective-permute-start(f32[64,256]{1,0:T(8,128)S(1)} %get-tuple-element.55), channel_id=1, source_target_pairs={{0,6},{1,7},{2,4},{3,5},{4,2},{5,3},{6,0},{7,1},{8,14},{9,15},{10,... | collective-permute-start | bytes 196616 | tf_op jit(solution)/shard_map/ppermute | solution.py:148
  60.9 3.9 %collective-permute-start.23 = (f32[64,256]{1,0:T(8,128)S(1)}, f32[64,256]{1,0:T(8,128)S(1)}, u32[]{:S(2)}, u32[]{:S(2)}) collective-permute-start(f32[64,256]{1,0:T(8,128)S(1)} %density_block.1.refs_0_.block), channel_id=1, source_target_pairs={{0,1},{1,0},{2,3},{3,2},{4,5},{5,4},{6,7},{7,6},{8,9},{9,8},{10,11... | collective-permute-start | bytes 196616 | tf_op jit(solution)/shard_map/ppermute | solution.py:148
  (4 other events, 55.2 us)

commit v5 on v4

--- a/solution.py
+++ b/solution.py
@@ -190,17 +190,12 @@
 
     row_energy = virtual[...]
     row_sum = energy(2 * z + c) + energy(2 * layer + y) - row_energy
-    size = row_energy.shape[1]
-    col_energy = jnp.broadcast_to(row_energy, (128, size)).T[:, :1]
-    col_sum = jnp.broadcast_to(row_sum, (128, size)).T[:, :1]
-    straight = dot(left[0], right[0], NT)
-    turned = dot(right[0], left[0], NT)
+    col_sum = jnp.broadcast_to(row_sum, (128, row_sum.shape[1])).T[:, :1]
+    overlap = dot(left[0], right[0], NT)
     for part in range(1, len(left)):
-        straight += dot(left[part], right[part], NT)
-        turned += dot(right[part], left[part], NT)
-    amplitude = straight / (col_sum - row_energy)
-    amplitude_t = turned / (row_sum - col_energy)
-    return amplitude.astype(jnp.bfloat16), 2.0 * amplitude - amplitude_t
+        overlap += dot(left[part], right[part], NT)
+    amplitude = overlap / (col_sum - row_energy)
+    return amplitude.astype(jnp.bfloat16), 2.0 * amplitude - amplitude.T
 
 
 def read_left(refs):
@@ -244,11 +239,16 @@
 
 def density_pairs_kernel(first_amp, first_mixed, last_amp, last_mixed, keep_out, send_out):
     z, y, x, c = place_bits()
-    half = keep_out.shape[1]
-    for out, core in ((send_out, 1 - c), (keep_out, c)):
-        rows = pl.ds(pl.multiple_of(core * half, half), half)
-        first = dot(first_mixed[...], first_amp[rows, :], NT)
-        out[...] = first + dot(last_mixed[...], last_amp[rows, :], NT)
+    count, rows = keep_out.shape[:2]
+    for out, core in ((send_out, c), (keep_out, 1 - c)):
+        groups = [
+            pl.ds(pl.multiple_of((2 * layer + core) * rows, rows), rows) for layer in range(count)
+        ]
+        first = jnp.concatenate([first_mixed[group, :] for group in groups], 0)
+        last = jnp.concatenate([last_mixed[group, :] for group in groups], 0)
+        total = dot(first, first_amp[...], NT) + dot(last, last_amp[...], NT)
+        for layer in range(count):
+            out[layer] = total[layer * rows : (layer + 1) * rows]
 
 
 def metric_product(step, metric_high, metric_low, high, low):
@@ -301,48 +301,25 @@
     refs[-1][...] = decode(left) + decode(right)
 
 
-def gamma_sum_kernel(part, left, right, *refs):
-    refs[-1][:, 0, :] = part[...] + decode(left) + decode(right)
-
-
-def halve(total, bit, keep_out, send_out):
-    rows = keep_out.shape[0]
-    keep_out[...] = total[pl.ds(pl.multiple_of(bit * rows, rows), rows), :]
-    encode_into(send_out, total[pl.ds(pl.multiple_of((1 - bit) * rows, rows), rows), :])
-
-
 def density_cores_kernel(keep, got, *refs):
-    keep_out, send_out, total = refs[-3:]
-    z, y, x, c = place_bits()
-    total[...] = keep[...] + got[...]
-    halve(total, z // 2, keep_out, send_out)
-
-
-def density_layers_kernel(keep, got, *refs):
-    keep_out, send_out, total = refs[-3:]
-    z, y, x, c = place_bits()
-    total[...] = keep[...] + decode(got)
-    halve(total, z % 2, keep_out, send_out)
-
-
-def density_rows_kernel(keep, got, *refs):
-    mine, theirs, total = refs[-3:]
-    z, y, x, c = place_bits()
-    total[...] = keep[...] + decode(got)
-    rows = mine.shape[0]
-    mine[...] = total[pl.ds(pl.multiple_of(y * rows, rows), rows), :]
-    theirs[...] = total[pl.ds(pl.multiple_of((1 - y) * rows, rows), rows), :]
-
-
-def density_block_kernel(mine, from_x, from_y, from_xy, *refs):
-    refs[-1][...] = (mine[...] + from_x[...]) + (from_y[...] + from_xy[...])
-
-
-def density_join_kernel(block, other, out):
-    z, y, x, c = place_bits()
-    half = block.shape[1]
-    out[:, :half] = jnp.where(c == 0, block[...], other[...])
-    out[:, half:] = jnp.where(c == 0, other[...], block[...])
+    layer_out, one, two, three = refs[-4:]
+    z, y, x, c = place_bits()
+    layer_out[...] = keep[z] + got[z]
+    for step, out in enumerate((one, two, three), 1):
+        encode_into(out, keep[z ^ step] + got[z ^ step])
+
+
+def density_rows_kernel(layer, one, two, three, *refs):
+    encode_into(refs[-1], layer[...] + decode(one) + decode(two) + decode(three))
+
+
+def density_block_kernel(far, near, *refs):
+    refs[-1][...] = decode(far) + decode(near)
+
+
+def outcome_kernel(part, left, right, block, other, gamma_out, density_out):
+    gamma_out[:, 0, :] = part[...] + decode(left) + decode(right)
+    density_out[...] = block[...] + other[...]
 
 
 def fast_device(factors, occ_energy, vir_energy, metric):
@@ -420,23 +397,16 @@
         flops=4 * aux_total * aux_total * width,
     )
     with jax.named_scope("gather"):
-        swapped, last_own, metric_high, metric_low = (
-            lax.optimization_barrier(
-                (
-                    x_swap(own),
-                    last_partner(own),
-                    metric_high,
-                    metric_low,
-                )
-            )
-        )
-        far_own, near_own, first_own, first_cross, last_swapped = lax.optimization_barrier(
+        swapped = x_swap(own)
+        last_own, last_swapped, first_own, first_cross, near_own, far_own, metric_high = lax.optimization_barrier(
             (
-                far_left(own),
-                near_left(own),
+                last_partner(own),
+                last_partner(swapped),
                 first_partner(own),
                 first_partner_cross(own),
-                last_partner(swapped),
+                near_left(own),
+                far_left(own),
+                metric_high,
             )
         )
         far_swapped, near_swapped = far_left(swapped), near_left(swapped)
@@ -460,10 +430,11 @@
         [first_amp],
         flops=4 * square * aux_total,
     )
+    layers = n_blk // 2
     dens_keep, dens_send = call(
         "density_pairs",
         density_pairs_kernel,
-        [shape(jnp.float32, virtuals, half)] * 2,
+        [shape(jnp.float32, layers, rows, virtuals)] * 2,
         [first_amp, first_mixed, last_amp, last_mixed],
         flops=2 * square * virtuals,
     )
@@ -496,70 +467,58 @@
     def gamma_move(step, block):
         return move(block, lambda z, y, x, c: (z, c, x ^ (step >> 1), y ^ (step & 1)))
 
-    def density_half(name, kernel, count, keep, got, *earlier):
-        return call(
-            name,
-            kernel,
-            [
-                shape(jnp.float32, count, half),
-                shape(jnp.bfloat16, count + TAIL_ROWS, half),
-            ],
-            [keep, got],
-            earlier,
-            [pltpu.VMEM(keep.shape, jnp.float32)],
-        )
-
+    def across(value):
+        return move(value, lambda z, y, x, c: (z, 1 - c, 1 - x, y))
+
+    def along(value):
+        return move(value, lambda z, y, x, c: (z, 1 - c, x, y))
+
+    coded = shape(jnp.bfloat16, rows + TAIL_ROWS, virtuals)
     got_third = gamma_move(3, third)
-    keep, packed = density_half(
-        "density_cores", density_cores_kernel, 4 * rows, dens_keep, dens_got, third
-    )
-    got = move(packed, lambda z, y, x, c: (z ^ 2, y, x, c))
-    second = gamma_block(2, packed)
+    layer, *messages = call(
+        "density_cores",
+        density_cores_kernel,
+        [shape(jnp.float32, rows, virtuals)] + [coded] * (layers - 1),
+        [dens_keep, dens_got],
+        [third],
+    )
+    got = [
+        move(messages[step - 1], lambda z, y, x, c, step=step: (z ^ step, y, x, c))
+        for step in range(layers - 1, 0, -1)
+    ]
+    second = gamma_block(2, messages[0])
     got_second = gamma_move(2, second)
     first_block = gamma_block(1, second)
     got_first = gamma_move(1, first_block)
-    zeroth = gamma_block(0, first_block)
-    got_zeroth = gamma_move(0, zeroth)
-    keep, packed = density_half(
-        "density_layers", density_layers_kernel, 2 * rows, keep, got, zeroth
-    )
-    got = move(packed, lambda z, y, x, c: (z ^ 1, y, x, c))
-    mine, theirs = call(
+    partial_rows = call(
         "density_rows",
         density_rows_kernel,
-        [shape(jnp.float32, rows, half)] * 2,
-        [keep, got],
-        [got_third],
-        [pltpu.VMEM(keep.shape, jnp.float32)],
-    )
-    from_x, from_y, from_xy = x_swap(mine), y_swap(theirs), xy_swap(theirs)
+        coded,
+        [layer, *got],
+        [first_block],
+    )
+    rows_far, rows_near = across(partial_rows), along(partial_rows)
+    zeroth = gamma_block(0, partial_rows)
+    got_zeroth = gamma_move(0, zeroth)
     part = call(
         "gamma_part",
         gamma_part_kernel,
         shape(jnp.float32, width, virtuals),
         [got_third, got_second],
-        [mine],
+        [zeroth, partial_rows],
     )
     block = call(
         "density_block",
         density_block_kernel,
-        shape(jnp.float32, rows, half),
-        [mine, from_x, from_y, from_xy],
-        [part, got_first],
-    )
-    other = core_swap(block)
-    gamma = call(
-        "gamma_sum",
-        gamma_sum_kernel,
-        shape(jnp.float32, width, 1, virtuals),
-        [part, got_first, got_zeroth],
-        [block],
-    )
-    density = call(
-        "density_join",
-        density_join_kernel,
         shape(jnp.float32, rows, virtuals),
-        [block, other],
+        [rows_far, rows_near],
+        [part],
+    )
+    gamma, density = call(
+        "outcome",
+        outcome_kernel,
+        [shape(jnp.float32, width, 1, virtuals), shape(jnp.float32, rows, virtuals)],
+        [part, got_first, got_zeroth, block, core_swap(block)],
     )
     return gamma, density
 

time: 65.7 us -> 63.8 us (0.971)
  Pallas kernels: 14.3 us -> 12.8 us
  waiting for transfers between devices: 13.7 us -> 12.8 us
    pallas_call x15 -> x13, Pallas kernels: 14.3 us -> 12.8 us  [call(): pl.pallas_call(kernel, in_specs=[vmem] * len(operands) + [unread] * len(e...]
    ppermute x24, waiting for transfers between devices: 13.7 us -> 12.8 us  [send(): return lax.ppermute(value, AXES, pairs)]
  transfers between devices with their start and end apart: 24 -> 24, of which waited for: 8 -> 9; matrix products, arithmetic and copies ran while one was open for 0% -> 0% of each run, Pallas kernels for 18% -> 15%
where the time goes in v5:
time: 63.8 us; the launch traced here: 63.4 us
  starting transfers between devices  34.8 us (55%)
  waiting for transfers between devices  12.8 us (20%)
  Pallas kernels  12.8 us (20%)
  local copies, waits for them, and re-layouts  2.2 us (3%)
  between operations  0.89 us (1%)
    ppermute x24, starting transfers between devices, send(): return lax.ppermute(value, AXES, pairs)  34.8 us
    pallas_call x13, Pallas kernels, call(): pl.pallas_call(kernel, in_specs=[vmem] * len(operands) + [unread] * len(e...  12.8 us
    ppermute x24, waiting for transfers between devices, send(): return lax.ppermute(value, AXES, pairs)  12.8 us
    unnamed x8, local copies, waits for them, and re-layouts  2.2 us
  transfers between devices with their start and end apart: 24, of which 9 were waited for; matrix products, arithmetic and copies ran while one was open for 0% of the time, Pallas kernels for 15%

profile of v5, /device:TPU:1, one launch (start us, length us, event | category | flops | bytes accessed | tf_op | source)
XLA Modules:
  0.0 63.4 jit_solution(12520396746568925859)
XLA Ops:
  0.6 2.1 %collective-permute-start = (bf16[512,256]{1,0:T(8,128)(2,1)}, bf16[512,256]{1,0:T(8,128)(2,1)S(1)}, u32[]{:S(2)}, u32[]{:S(2)}) collective-permute-start(bf16[512,256]{1,0:T(8,128)(2,1)} %bitcast.3), channel_id=1, source_target_pairs={{0,2},{1,3},{2,0},{3,1},{4,6},{5,7},{6,4},{7,5},{8,10},{9,11},{10,... | collective-permute-start | bytes 786440 | tf_op jit(solution)/shard_map/gather/ppermute | solution.py:148
  2.7 2.3 %collective-permute-start.1 = (bf16[512,256]{1,0:T(8,128)(2,1)}, bf16[512,256]{1,0:T(8,128)(2,1)S(1)}, u32[]{:S(2)}, u32[]{:S(2)}) collective-permute-start(bf16[512,256]{1,0:T(8,128)(2,1)} %bitcast.4), channel_id=1, source_target_pairs={{0,16},{1,17},{2,26},{3,27},{4,20},{5,21},{6,30},{7,31},{8,24},{9,... | collective-permute-start | bytes 786440 | tf_op jit(solution)/shard_map/gather/ppermute | solution.py:148
  5.1 3.2 %collective-permute-start.3 = (bf16[512,256]{1,0:T(8,128)(2,1)}, bf16[512,256]{1,0:T(8,128)(2,1)S(1)}, u32[]{:S(2)}, u32[]{:S(2)}) collective-permute-start(bf16[512,256]{1,0:T(8,128)(2,1)} %bitcast.5), channel_id=1, source_target_pairs={{0,8},{1,9},{2,2},{3,3},{4,12},{5,13},{6,6},{7,7},{8,0},{9,1},{10,... | collective-permute-start | bytes 786440 | tf_op jit(solution)/shard_map/gather/ppermute | solution.py:148
  8.3 1.5 %collective-permute-start.5 = (bf16[512,256]{1,0:T(8,128)(2,1)}, bf16[512,256]{1,0:T(8,128)(2,1)S(1)}, u32[]{:S(2)}, u32[]{:S(2)}) collective-permute-start(bf16[512,256]{1,0:T(8,128)(2,1)} %bitcast.7), channel_id=1, source_target_pairs={{0,4},{1,0},{2,6},{3,2},{4,5},{5,1},{6,7},{7,3},{8,12},{9,8},{10,1... | collective-permute-start | bytes 786440 | tf_op jit(solution)/shard_map/gather/ppermute | solution.py:148
  9.9 3.6 %collective-permute-start.6 = (bf16[512,256]{1,0:T(8,128)(2,1)}, bf16[512,256]{1,0:T(8,128)(2,1)S(1)}, u32[]{:S(2)}, u32[]{:S(2)}) collective-permute-start(bf16[512,256]{1,0:T(8,128)(2,1)} %bitcast.8), channel_id=1, source_target_pairs={{0,0},{1,4},{2,2},{3,6},{4,1},{5,5},{6,3},{7,7},{8,8},{9,12},{10,1... | collective-permute-start | bytes 786440 | tf_op jit(solution)/shard_map/gather/ppermute | solution.py:148
  13.5 3.2 %collective-permute-done.1.refs_8_.refs_0_ = bf16[512,256]{1,0:T(8,128)(2,1)S(1)} collective-permute-done((bf16[512,256]{1,0:T(8,128)(2,1)}, bf16[512,256]{1,0:T(8,128)(2,1)S(1)}, u32[]{:S(2)}, u32[]{:S(2)}) %collective-permute-start.1) | collective-permute-done | bytes 262176 | tf_op jit(solution)/shard_map/gather/ppermute | solution.py:148
  16.7 1.5 %collective-permute-done.3.refs_8_ = bf16[512,256]{1,0:T(8,128)(2,1)S(1)} collective-permute-done((bf16[512,256]{1,0:T(8,128)(2,1)}, bf16[512,256]{1,0:T(8,128)(2,1)S(1)}, u32[]{:S(2)}, u32[]{:S(2)}) %collective-permute-start.3) | collective-permute-done | bytes 262176 | tf_op jit(solution)/shard_map/gather/ppermute | solution.py:148
  18.2 2.2 %collective-permute-start.7 = (bf16[512,256]{1,0:T(8,128)(2,1)S(1)}, bf16[512,256]{1,0:T(8,128)(2,1)S(1)}, u32[]{:S(2)}, u32[]{:S(2)}) collective-permute-start(bf16[512,256]{1,0:T(8,128)(2,1)S(1)} %collective-permute-done.refs_3_), channel_id=1, source_target_pairs={{0,4},{1,0},{2,6},{3,2},{4,5},{5,1},{6,7},{7,3},{8,12},{9,8},{10,1... | collective-permute-start | bytes 786440 | tf_op jit(solution)/shard_map/gather/ppermute | solution.py:148
  20.4 2.2 %copy-done = f32[1024,1024]{1,0:T(8,128)S(1)} copy-done((f32[1024,1024]{1,0:T(8,128)S(1)}, f32[1024,1024]{1,0:T(8,128)}, u32[]{:S(2)}) %copy-start) | copy-done | bytes 4194328
  22.6 1.3 %metric_turn.1 = (bf16[4,256,1024]{2,1,0:T(8,128)(2,1)S(1)}, bf16[4,256,1024]{2,1,0:T(8,128)(2,1)S(1)}) custom-call(f32[1024,1024]{1,0:T(8,128)S(1)} %copy-done), custom_call_target="tpu_custom_call" | custom-call | flops 1073741824 | tf_op jit(solution)/shard_map/metric_turn/pallas_call | solution.py:378
  23.9 3.0 %collective-permute-start.8 = (bf16[512,256]{1,0:T(8,128)(2,1)S(1)}, bf16[512,256]{1,0:T(8,128)(2,1)S(1)}, u32[]{:S(2)}, u32[]{:S(2)}) collective-permute-start(bf16[512,256]{1,0:T(8,128)(2,1)S(1)} %collective-permute-done.refs_3_), channel_id=1, source_target_pairs={{0,0},{1,4},{2,2},{3,6},{4,1},{5,5},{6,3},{7,7},{8,8},{9,12},{10,1... | collective-permute-start | bytes 786440 | tf_op jit(solution)/shard_map/gather/ppermute | solution.py:148
  27.0 2.5 %collective-permute-done.2.refs_9_.refs_1_ = bf16[512,256]{1,0:T(8,128)(2,1)S(1)} collective-permute-done((bf16[512,256]{1,0:T(8,128)(2,1)S(1)}, bf16[512,256]{1,0:T(8,128)(2,1)S(1)}, u32[]{:S(2)}, u32[]{:S(2)}) %collective-permute-start.2) | collective-permute-done | bytes 262176 | tf_op jit(solution)/shard_map/gather/ppermute | solution.py:148
  29.5 2.5 %collective-permute-start.11 = (bf16[512,256]{1,0:T(8,128)(2,1)S(1)}, bf16[512,256]{1,0:T(8,128)(2,1)S(1)}, u32[]{:S(2)}, u32[]{:S(2)}) collective-permute-start(bf16[512,256]{1,0:T(8,128)(2,1)S(1)} %collective-permute-done.3.refs_8_), channel_id=1, source_target_pairs={{0,1},{1,0},{2,3},{3,2},{4,5},{5,4},{6,7},{7,6},{8,9},{9,8},{10,11... | collective-permute-start | bytes 786440 | tf_op jit(solution)/shard_map/gather/ppermute | solution.py:148
  33.5 1.5 %first_pair.1 = (f32[512,1024]{1,0:T(8,128)S(1)}, bf16[512,512]{1,0:T(8,128)(2,1)S(1)}, bf16[512,512]{1,0:T(8,128)(2,1)S(1)}) custom-call(f32[1,8]{1,0:T(1,128)S(1)} %bitcast.13, f32[1,512]{1,0:T(1,128)S(1)} %bitcast.11, bf16[512,256]{1,0:T(8,128)(2,1)S(1)} %bitcast.9, bf16[512,256]{1,0:T(8,128)(2,1)S(1)} %collective-permute-done.refs_3_, ...), custom_call_target="tpu_custom_call" | custom-call | tf_op jit(solution)/shard_map/first_pair/pallas_call | solution.py:378
  37.1 2.0 %gradient.1 = (bf16[512,1024]{1,0:T(8,128)(2,1)S(1)}, bf16[512,1024]{1,0:T(8,128)(2,1)S(1)}, bf16[272,512]{1,0:T(8,128)(2,1)S(1)}) custom-call(bf16[512,512]{1,0:T(8,128)(2,1)S(1)} %get-tuple-element.33.mixed.last_mixed, bf16[512,256]{1,0:T(8,128)(2,1)S(1)} %collective-permute-done.1.refs_8_.refs_0_, ...), custom_call_target="tpu_custom_call" | custom-call | flops 1610612736 | tf_op jit(solution)/shard_map/gradient/pallas_call | solution.py:378
  40.7 2.5 %collective-permute-start.18 = (bf16[80,512]{1,0:T(8,128)(2,1)S(1)}, bf16[80,512]{1,0:T(8,128)(2,1)S(1)}, u32[]{:S(2)}, u32[]{:S(2)}) collective-permute-start(bf16[80,512]{1,0:T(8,128)(2,1)S(1)} %get-tuple-element.44.refs_0_), channel_id=1, source_target_pairs={{0,8},{1,9},{2,10},{3,11},{4,12},{5,13},{6,14},{7,15},{8,0},{9,1},... | collective-permute-start | bytes 245768 | tf_op jit(solution)/shard_map/ppermute | solution.py:148
  43.1 1.3 %gamma_block.3.refs_0_ = bf16[272,512]{1,0:T(8,128)(2,1)S(1)} custom-call(bf16[4,256,1024]{2,1,0:T(8,128)(2,1)S(1)} %get-tuple-element.35.refs_5_.metric_high, bf16[4,256,1024]{2,1,0:T(8,128)(2,1)S(1)} %get-tuple-element.36.refs_6_.metric_low, bf16[512,1024]{1,0:T(8,128)(2,1)S(1)} %get-tuple-element.38.high, bf16[512,1024]{1,0:T(8,128)(2,1)S(1)} %get-tuple-element.39.low, ...), custom_call_target="tpu_custom_call" | custom-call | flops 805306368 | tf_op jit(solution)/shard_map/gamma_block/pallas_call | solution.py:378
  44.5 3.5 %collective-permute-start.15 = (bf16[272,512]{1,0:T(8,128)(2,1)S(1)}, bf16[272,512]{1,0:T(8,128)(2,1)S(1)}, u32[]{:S(2)}, u32[]{:S(2)}) collective-permute-start(bf16[272,512]{1,0:T(8,128)(2,1)S(1)} %gamma_block.3.refs_0_), channel_id=1, source_target_pairs={{0,2},{1,6},{2,0},{3,4},{4,3},{5,7},{6,1},{7,5},{8,10},{9,14},{10,... | collective-permute-start | bytes 835592 | tf_op jit(solution)/shard_map/ppermute | solution.py:148
  48.0 1.3 %gamma_block.4.refs_0_ = bf16[272,512]{1,0:T(8,128)(2,1)S(1)} custom-call(bf16[4,256,1024]{2,1,0:T(8,128)(2,1)S(1)} %get-tuple-element.35.refs_5_.metric_high, bf16[4,256,1024]{2,1,0:T(8,128)(2,1)S(1)} %get-tuple-element.36.refs_6_.metric_low, bf16[512,1024]{1,0:T(8,128)(2,1)S(1)} %get-tuple-element.38.high, bf16[512,1024]{1,0:T(8,128)(2,1)S(1)} %get-tuple-element.39.low, ...), custom_call_target="tpu_custom_call" | custom-call | flops 805306368 | tf_op jit(solution)/shard_map/gamma_block/pallas_call | solution.py:378
  49.8 1.3 %gamma_block.5.refs_0_ = bf16[272,512]{1,0:T(8,128)(2,1)S(1)} custom-call(bf16[4,256,1024]{2,1,0:T(8,128)(2,1)S(1)} %get-tuple-element.35.refs_5_.metric_high, bf16[4,256,1024]{2,1,0:T(8,128)(2,1)S(1)} %get-tuple-element.36.refs_6_.metric_low, bf16[512,1024]{1,0:T(8,128)(2,1)S(1)} %get-tuple-element.38.high, bf16[512,1024]{1,0:T(8,128)(2,1)S(1)} %get-tuple-element.39.low, ...), custom_call_target="tpu_custom_call" | custom-call | flops 805306368 | tf_op jit(solution)/shard_map/gamma_block/pallas_call | solution.py:378
  51.1 3.4 %collective-permute-start.20 = (bf16[272,512]{1,0:T(8,128)(2,1)S(1)}, bf16[272,512]{1,0:T(8,128)(2,1)S(1)}, u32[]{:S(2)}, u32[]{:S(2)}) collective-permute-start(bf16[272,512]{1,0:T(8,128)(2,1)S(1)} %gamma_block.5.refs_0_), channel_id=1, source_target_pairs={{0,0},{1,4},{2,2},{3,6},{4,1},{5,5},{6,3},{7,7},{8,8},{9,12},{10,1... | collective-permute-start | bytes 835592 | tf_op jit(solution)/shard_map/ppermute | solution.py:148
  54.6 2.6 %collective-permute-start.22 = (bf16[80,512]{1,0:T(8,128)(2,1)S(1)}, bf16[80,512]{1,0:T(8,128)(2,1)S(1)}, u32[]{:S(2)}, u32[]{:S(2)}) collective-permute-start(bf16[80,512]{1,0:T(8,128)(2,1)S(1)} %density_rows.1.refs_0_.refs_1_), channel_id=1, source_target_pairs={{0,4},{1,0},{2,6},{3,2},{4,5},{5,1},{6,7},{7,3},{8,12},{9,8},{10,1... | collective-permute-start | bytes 245768 | tf_op jit(solution)/shard_map/ppermute | solution.py:148
  57.5 2.0 %collective-permute-done.21.far = bf16[80,512]{1,0:T(8,128)(2,1)S(1)} collective-permute-done((bf16[80,512]{1,0:T(8,128)(2,1)S(1)}, bf16[80,512]{1,0:T(8,128)(2,1)S(1)}, u32[]{:S(2)}, u32[]{:S(2)}) %collective-permute-start.21) | collective-permute-done | bytes 81952 | tf_op jit(solution)/shard_map/ppermute | solution.py:148
  62.2 1.3 %outcome.1 = (f32[256,1,512]{2,1,0:T(1,128)}, f32[64,512]{1,0:T(8,128)}) custom-call(f32[256,512]{1,0:T(8,128)S(1)} %gamma_part.1.refs_0_.part, bf16[272,512]{1,0:T(8,128)(2,1)S(1)} %collective-permute-done.19.left, bf16[272,512]{1,0:T(8,128)(2,1)S(1)} %collective-permute-done.20.right, f32[64,512]{1,0:T(8,128)S(1)} %density_block.1.block, ...), custom_call_target="tpu_custom_call" | custom-call | tf_op jit(solution)/shard_map/outcome/pallas_call | solution.py:378
  (45 shorter events, 8.7 us)
Async XLA Ops:
  0.6 9.2 %collective-permute-start = (bf16[512,256]{1,0:T(8,128)(2,1)}, bf16[512,256]{1,0:T(8,128)(2,1)S(1)}, u32[]{:S(2)}, u32[]{:S(2)}) collective-permute-start(bf16[512,256]{1,0:T(8,128)(2,1)} %bitcast.3), channel_id=1, source_target_pairs={{0,2},{1,3},{2,0},{3,1},{4,6},{5,7},{6,4},{7,5},{8,10},{9,11},{10,... | collective-permute-start | bytes 786440 | tf_op jit(solution)/shard_map/gather/ppermute | solution.py:148
  2.7 13.9 %collective-permute-start.1 = (bf16[512,256]{1,0:T(8,128)(2,1)}, bf16[512,256]{1,0:T(8,128)(2,1)S(1)}, u32[]{:S(2)}, u32[]{:S(2)}) collective-permute-start(bf16[512,256]{1,0:T(8,128)(2,1)} %bitcast.4), channel_id=1, source_target_pairs={{0,16},{1,17},{2,26},{3,27},{4,20},{5,21},{6,30},{7,31},{8,24},{9,... | collective-permute-start | bytes 786440 | tf_op jit(solution)/shard_map/gather/ppermute | solution.py:148
  5.1 13.2 %collective-permute-start.3 = (bf16[512,256]{1,0:T(8,128)(2,1)}, bf16[512,256]{1,0:T(8,128)(2,1)S(1)}, u32[]{:S(2)}, u32[]{:S(2)}) collective-permute-start(bf16[512,256]{1,0:T(8,128)(2,1)} %bitcast.5), channel_id=1, source_target_pairs={{0,8},{1,9},{2,2},{3,3},{4,12},{5,13},{6,6},{7,7},{8,0},{9,1},{10,... | collective-permute-start | bytes 786440 | tf_op jit(solution)/shard_map/gather/ppermute | solution.py:148
  8.3 15.6 %collective-permute-start.4 = (bf16[512,256]{1,0:T(8,128)(2,1)}, bf16[512,256]{1,0:T(8,128)(2,1)S(1)}, u32[]{:S(2)}, u32[]{:S(2)}) collective-permute-start(bf16[512,256]{1,0:T(8,128)(2,1)} %bitcast.6), channel_id=1, source_target_pairs={{0,2},{1,3},{2,8},{3,9},{4,6},{5,7},{6,12},{7,13},{8,10},{9,11},{1... | collective-permute-start | bytes 786440 | tf_op jit(solution)/shard_map/gather/ppermute | solution.py:148
  8.3 18.6 %collective-permute-start.5 = (bf16[512,256]{1,0:T(8,128)(2,1)}, bf16[512,256]{1,0:T(8,128)(2,1)S(1)}, u32[]{:S(2)}, u32[]{:S(2)}) collective-permute-start(bf16[512,256]{1,0:T(8,128)(2,1)} %bitcast.7), channel_id=1, source_target_pairs={{0,4},{1,0},{2,6},{3,2},{4,5},{5,1},{6,7},{7,3},{8,12},{9,8},{10,1... | collective-permute-start | bytes 786440 | tf_op jit(solution)/shard_map/gather/ppermute | solution.py:148
  9.9 17.1 %collective-permute-start.6 = (bf16[512,256]{1,0:T(8,128)(2,1)}, bf16[512,256]{1,0:T(8,128)(2,1)S(1)}, u32[]{:S(2)}, u32[]{:S(2)}) collective-permute-start(bf16[512,256]{1,0:T(8,128)(2,1)} %bitcast.8), channel_id=1, source_target_pairs={{0,0},{1,4},{2,2},{3,6},{4,1},{5,5},{6,3},{7,7},{8,8},{9,12},{10,1... | collective-permute-start | bytes 786440 | tf_op jit(solution)/shard_map/gather/ppermute | solution.py:148
  16.7 12.8 %collective-permute-start.2 = (bf16[512,256]{1,0:T(8,128)(2,1)S(1)}, bf16[512,256]{1,0:T(8,128)(2,1)S(1)}, u32[]{:S(2)}, u32[]{:S(2)}) collective-permute-start(bf16[512,256]{1,0:T(8,128)(2,1)S(1)} %collective-permute-done.refs_3_), channel_id=1, source_target_pairs={{0,16},{1,17},{2,26},{3,27},{4,20},{5,21},{6,30},{7,31},{8,24},{9,... | collective-permute-start | bytes 786440 | tf_op jit(solution)/shard_map/gather/ppermute | solution.py:148
  18.2 14.2 %collective-permute-start.7 = (bf16[512,256]{1,0:T(8,128)(2,1)S(1)}, bf16[512,256]{1,0:T(8,128)(2,1)S(1)}, u32[]{:S(2)}, u32[]{:S(2)}) collective-permute-start(bf16[512,256]{1,0:T(8,128)(2,1)S(1)} %collective-permute-done.refs_3_), channel_id=1, source_target_pairs={{0,4},{1,0},{2,6},{3,2},{4,5},{5,1},{6,7},{7,3},{8,12},{9,8},{10,1... | collective-permute-start | bytes 786440 | tf_op jit(solution)/shard_map/gather/ppermute | solution.py:148
  23.9 8.6 %collective-permute-start.8 = (bf16[512,256]{1,0:T(8,128)(2,1)S(1)}, bf16[512,256]{1,0:T(8,128)(2,1)S(1)}, u32[]{:S(2)}, u32[]{:S(2)}) collective-permute-start(bf16[512,256]{1,0:T(8,128)(2,1)S(1)} %collective-permute-done.refs_3_), channel_id=1, source_target_pairs={{0,0},{1,4},{2,2},{3,6},{4,1},{5,5},{6,3},{7,7},{8,8},{9,12},{10,1... | collective-permute-start | bytes 786440 | tf_op jit(solution)/shard_map/gather/ppermute | solution.py:148
  29.5 3.6 %collective-permute-start.11 = (bf16[512,256]{1,0:T(8,128)(2,1)S(1)}, bf16[512,256]{1,0:T(8,128)(2,1)S(1)}, u32[]{:S(2)}, u32[]{:S(2)}) collective-permute-start(bf16[512,256]{1,0:T(8,128)(2,1)S(1)} %collective-permute-done.3.refs_8_), channel_id=1, source_target_pairs={{0,1},{1,0},{2,3},{3,2},{4,5},{5,4},{6,7},{7,6},{8,9},{9,8},{10,11... | collective-permute-start | bytes 786440 | tf_op jit(solution)/shard_map/gather/ppermute | solution.py:148
  31.9 1.5 %collective-permute-start.12 = (bf16[512,256]{1,0:T(8,128)(2,1)S(1)}, bf16[512,256]{1,0:T(8,128)(2,1)S(1)}, u32[]{:S(2)}, u32[]{:S(2)}) collective-permute-start(bf16[512,256]{1,0:T(8,128)(2,1)S(1)} %collective-permute-done.4.refs_9_), channel_id=1, source_target_pairs={{0,1},{1,0},{2,3},{3,2},{4,5},{5,4},{6,7},{7,6},{8,9},{9,8},{10,11... | collective-permute-start | bytes 786440 | tf_op jit(solution)/shard_map/gather/ppermute | solution.py:148
  31.9 3.0 %collective-permute-start.10 = (bf16[512,256]{1,0:T(8,128)(2,1)S(1)}, bf16[512,256]{1,0:T(8,128)(2,1)S(1)}, u32[]{:S(2)}, u32[]{:S(2)}) collective-permute-start(bf16[512,256]{1,0:T(8,128)(2,1)S(1)} %collective-permute-done.2.refs_9_.refs_1_), channel_id=1, source_target_pairs={{0,1},{1,0},{2,3},{3,2},{4,5},{5,4},{6,7},{7,6},{8,9},{9,8},{10,11... | collective-permute-start | bytes 786440 | tf_op jit(solution)/shard_map/gather/ppermute | solution.py:148
  32.5 2.5 %collective-permute-start.9 = (bf16[512,256]{1,0:T(8,128)(2,1)S(1)}, bf16[512,256]{1,0:T(8,128)(2,1)S(1)}, u32[]{:S(2)}, u32[]{:S(2)}) collective-permute-start(bf16[512,256]{1,0:T(8,128)(2,1)S(1)} %collective-permute-done.1.refs_8_.refs_0_), channel_id=1, source_target_pairs={{0,1},{1,0},{2,3},{3,2},{4,5},{5,4},{6,7},{7,6},{8,9},{9,8},{10,11... | collective-permute-start | bytes 786440 | tf_op jit(solution)/shard_map/gather/ppermute | solution.py:148
  36.7 2.5 %collective-permute-start.14 = (f32[4,64,512]{2,1,0:T(8,128)S(1)}, f32[4,64,512]{2,1,0:T(8,128)S(1)}, u32[]{:S(2)}, u32[]{:S(2)}) collective-permute-start(f32[4,64,512]{2,1,0:T(8,128)S(1)} %get-tuple-element.43), channel_id=1, source_target_pairs={{0,1},{1,0},{2,3},{3,2},{4,5},{5,4},{6,7},{7,6},{8,9},{9,8},{10,11... | collective-permute-start | bytes 1572872 | tf_op jit(solution)/shard_map/ppermute | solution.py:148
  39.1 15.4 %collective-permute-start.13 = (bf16[272,512]{1,0:T(8,128)(2,1)S(1)}, bf16[272,512]{1,0:T(8,128)(2,1)S(1)}, u32[]{:S(2)}, u32[]{:S(2)}) collective-permute-start(bf16[272,512]{1,0:T(8,128)(2,1)S(1)} %get-tuple-element.37.refs_0_), channel_id=1, source_target_pairs={{0,3},{1,7},{2,1},{3,5},{4,2},{5,6},{6,0},{7,4},{8,11},{9,15},{10,... | collective-permute-start | bytes 835592 | tf_op jit(solution)/shard_map/ppermute | solution.py:148
  39.5 9.9 %collective-permute-start.16 = (bf16[80,512]{1,0:T(8,128)(2,1)S(1)}, bf16[80,512]{1,0:T(8,128)(2,1)S(1)}, u32[]{:S(2)}, u32[]{:S(2)}) collective-permute-start(bf16[80,512]{1,0:T(8,128)(2,1)S(1)} %get-tuple-element.46), channel_id=1, source_target_pairs={{0,24},{1,25},{2,26},{3,27},{4,28},{5,29},{6,30},{7,31},{8,16},{9,... | collective-permute-start | bytes 245768 | tf_op jit(solution)/shard_map/ppermute | solution.py:148
  40.5 8.9 %collective-permute-start.17 = (bf16[80,512]{1,0:T(8,128)(2,1)S(1)}, bf16[80,512]{1,0:T(8,128)(2,1)S(1)}, u32[]{:S(2)}, u32[]{:S(2)}) collective-permute-start(bf16[80,512]{1,0:T(8,128)(2,1)S(1)} %get-tuple-element.47), channel_id=1, source_target_pairs={{0,16},{1,17},{2,18},{3,19},{4,20},{5,21},{6,22},{7,23},{8,24},{9,... | collective-permute-start | bytes 245768 | tf_op jit(solution)/shard_map/ppermute | solution.py:148
  40.7 8.8 %collective-permute-start.18 = (bf16[80,512]{1,0:T(8,128)(2,1)S(1)}, bf16[80,512]{1,0:T(8,128)(2,1)S(1)}, u32[]{:S(2)}, u32[]{:S(2)}) collective-permute-start(bf16[80,512]{1,0:T(8,128)(2,1)S(1)} %get-tuple-element.44.refs_0_), channel_id=1, source_target_pairs={{0,8},{1,9},{2,10},{3,11},{4,12},{5,13},{6,14},{7,15},{8,0},{9,1},... | collective-permute-start | bytes 245768 | tf_op jit(solution)/shard_map/ppermute | solution.py:148
  44.5 12.7 %collective-permute-start.15 = (bf16[272,512]{1,0:T(8,128)(2,1)S(1)}, bf16[272,512]{1,0:T(8,128)(2,1)S(1)}, u32[]{:S(2)}, u32[]{:S(2)}) collective-permute-start(bf16[272,512]{1,0:T(8,128)(2,1)S(1)} %gamma_block.3.refs_0_), channel_id=1, source_target_pairs={{0,2},{1,6},{2,0},{3,4},{4,3},{5,7},{6,1},{7,5},{8,10},{9,14},{10,... | collective-permute-start | bytes 835592 | tf_op jit(solution)/shard_map/ppermute | solution.py:148
  49.4 11.4 %collective-permute-start.19 = (bf16[272,512]{1,0:T(8,128)(2,1)S(1)}, bf16[272,512]{1,0:T(8,128)(2,1)S(1)}, u32[]{:S(2)}, u32[]{:S(2)}) collective-permute-start(bf16[272,512]{1,0:T(8,128)(2,1)S(1)} %gamma_block.4.refs_0_), channel_id=1, source_target_pairs={{0,1},{1,5},{2,3},{3,7},{4,0},{5,4},{6,2},{7,6},{8,9},{9,13},{10,1... | collective-permute-start | bytes 835592 | tf_op jit(solution)/shard_map/ppermute | solution.py:148
  51.1 10.1 %collective-permute-start.20 = (bf16[272,512]{1,0:T(8,128)(2,1)S(1)}, bf16[272,512]{1,0:T(8,128)(2,1)S(1)}, u32[]{:S(2)}, u32[]{:S(2)}) collective-permute-start(bf16[272,512]{1,0:T(8,128)(2,1)S(1)} %gamma_block.5.refs_0_), channel_id=1, source_target_pairs={{0,0},{1,4},{2,2},{3,6},{4,1},{5,5},{6,3},{7,7},{8,8},{9,12},{10,1... | collective-permute-start | bytes 835592 | tf_op jit(solution)/shard_map/ppermute | solution.py:148
  54.5 5.0 %collective-permute-start.21 = (bf16[80,512]{1,0:T(8,128)(2,1)S(1)}, bf16[80,512]{1,0:T(8,128)(2,1)S(1)}, u32[]{:S(2)}, u32[]{:S(2)}) collective-permute-start(bf16[80,512]{1,0:T(8,128)(2,1)S(1)} %density_rows.1.refs_0_.refs_1_), channel_id=1, source_target_pairs={{0,6},{1,2},{2,4},{3,0},{4,7},{5,3},{6,5},{7,1},{8,14},{9,10},{10,... | collective-permute-start | bytes 245768 | tf_op jit(solution)/shard_map/ppermute | solution.py:148
  54.6 6.1 %collective-permute-start.22 = (bf16[80,512]{1,0:T(8,128)(2,1)S(1)}, bf16[80,512]{1,0:T(8,128)(2,1)S(1)}, u32[]{:S(2)}, u32[]{:S(2)}) collective-permute-start(bf16[80,512]{1,0:T(8,128)(2,1)S(1)} %density_rows.1.refs_0_.refs_1_), channel_id=1, source_target_pairs={{0,4},{1,0},{2,6},{3,2},{4,5},{5,1},{6,7},{7,3},{8,12},{9,8},{10,1... | collective-permute-start | bytes 245768 | tf_op jit(solution)/shard_map/ppermute | solution.py:148
  60.8 1.4 %collective-permute-start.23 = (f32[64,512]{1,0:T(8,128)S(1)}, f32[64,512]{1,0:T(8,128)S(1)}, u32[]{:S(2)}, u32[]{:S(2)}) collective-permute-start(f32[64,512]{1,0:T(8,128)S(1)} %density_block.1.block), channel_id=1, source_target_pairs={{0,1},{1,0},{2,3},{3,2},{4,5},{5,4},{6,7},{7,6},{8,9},{9,8},{10,11... | collective-permute-start | bytes 393224 | tf_op jit(solution)/shard_map/ppermute | solution.py:148
  (4 other events, 56.9 us)

commit v6 on v5

--- a/solution.py
+++ b/solution.py
@@ -181,7 +181,7 @@
     return blk // 2, blk % 2, sec // 2, sec % 2
 
 
-def pair_terms(occupied, virtual, layer, left, right):
+def pair_terms(occupied, virtual, layer, overlap):
     z, y, x, c = place_bits()
     index = lax.broadcasted_iota(jnp.int32, occupied.shape, 1)
 
@@ -191,47 +191,50 @@
     row_energy = virtual[...]
     row_sum = energy(2 * z + c) + energy(2 * layer + y) - row_energy
     col_sum = jnp.broadcast_to(row_sum, (128, row_sum.shape[1])).T[:, :1]
-    overlap = dot(left[0], right[0], NT)
-    for part in range(1, len(left)):
-        overlap += dot(left[part], right[part], NT)
     amplitude = overlap / (col_sum - row_energy)
     return amplitude.astype(jnp.bfloat16), 2.0 * amplitude - amplitude.T
 
 
-def read_left(refs):
+def half_overlap_kernel(own, swapped, near, near_swapped, *refs):
     z, y, x, c = place_bits()
     home = c == y
-    own, swapped, near, near_swapped, far, far_swapped = [ref[...] for ref in refs]
-    return [
-        jnp.where(home, own, near),
-        jnp.where(home, swapped, near_swapped),
-        jnp.where(home, near, far),
-        jnp.where(home, near_swapped, far_swapped),
-    ]
-
-
-def first_pair_kernel(*refs):
-    z, y, x, c = place_bits()
-    left = read_left(refs[2:8])
-    right = [ref[...] for ref in refs[8:12]]
+    left = jnp.where(home, own[...], near[...])
+    left_swapped = jnp.where(home, swapped[...], near_swapped[...])
+    for pair in range(2):
+        right, right_swapped = refs[2 * pair], refs[2 * pair + 1]
+        refs[4 + pair][...] = dot(left, right[...], NT) + dot(left_swapped, right_swapped[...], NT)
+
+
+def whole_overlap(half, lefts, rights):
+    z, y, x, c = place_bits()
+    home = c == y
+    near, near_swapped, far, far_swapped = [ref[...] for ref in lefts]
+    right, right_swapped = [ref[...] for ref in rights]
+    left = jnp.where(home, near, far)
+    left_swapped = jnp.where(home, near_swapped, far_swapped)
+    return half[...] + dot(left, right, NT) + dot(left_swapped, right_swapped, NT)
+
+
+def first_pair_kernel(occupied, virtual, half, *refs):
+    z, y, x, c = place_bits()
+    overlap = whole_overlap(half, refs[:4], refs[6:8])
     grad_out, amp_out, mixed_out = refs[-3:]
     layer = jnp.where(x == 1, z, z ^ 1)
-    amp_half, mixed = pair_terms(refs[0], refs[1], layer, left, right)
+    amp_half, mixed = pair_terms(occupied, virtual, layer, overlap)
     mixed_half = mixed.astype(jnp.bfloat16)
-    width = right[0].shape[1]
-    for part in range(4):
-        grad_out[:, part * width : (part + 1) * width] = dot(mixed_half, right[part], NN)
+    width = refs[4].shape[1]
+    for part, right in enumerate(refs[4:8]):
+        grad_out[:, part * width : (part + 1) * width] = dot(mixed_half, right[...], NN)
     amp_out[...] = amp_half
     mixed_out[...] = mixed_half
 
 
-def last_pair_kernel(*refs):
-    z, y, x, c = place_bits()
-    left = read_left(refs[2:8])
-    right = [ref[...] for ref in refs[8:12]]
+def last_pair_kernel(occupied, virtual, half, *refs):
+    z, y, x, c = place_bits()
+    overlap = whole_overlap(half, refs[:4], refs[4:6])
     amp_out, mixed_out = refs[-2:]
     layer = jnp.where(x == 1, z ^ 3, z ^ 2)
-    amp_half, mixed = pair_terms(refs[0], refs[1], layer, left, right)
+    amp_half, mixed = pair_terms(occupied, virtual, layer, overlap)
     outside = (x == 0) & (c == y)
     amp_out[...] = amp_half
     mixed_out[...] = jnp.where(outside, 0.0, mixed).astype(jnp.bfloat16)
@@ -317,9 +320,12 @@
     refs[-1][...] = decode(far) + decode(near)
 
 
-def outcome_kernel(part, left, right, block, other, gamma_out, density_out):
-    gamma_out[:, 0, :] = part[...] + decode(left) + decode(right)
-    density_out[...] = block[...] + other[...]
+def gamma_sum_kernel(part, left, right, *refs):
+    refs[-1][:, 0, :] = part[...] + decode(left) + decode(right)
+
+
+def density_sum_kernel(block, other, *refs):
+    refs[-1][...] = block[...] + other[...]
 
 
 def fast_device(factors, occ_energy, vir_energy, metric):
@@ -415,18 +421,25 @@
         last = [last_own, last_swapped, core_swap(last_own), core_swap(last_swapped)]
 
     energies = [occ_energy[None, :], vir_energy[None, :]]
+    first_half, last_half = call(
+        "half_overlap",
+        half_overlap_kernel,
+        [shape(jnp.float32, virtuals, virtuals)] * 2,
+        [*left[:4], *first[:2], *last[:2]],
+        flops=2 * square * aux_total,
+    )
     half_square = shape(jnp.bfloat16, virtuals, virtuals)
     grad, first_amp, first_mixed = call(
         "first_pair",
         first_pair_kernel,
         [shape(jnp.float32, virtuals, aux_total), half_square, half_square],
-        energies + left + first,
+        [*energies, first_half, *left[2:], *first],
     )
     last_amp, last_mixed = call(
         "last_pair",
         last_pair_kernel,
         [half_square, half_square],
-        energies + left + last,
+        [*energies, last_half, *left[2:], *last[2:]],
         [first_amp],
         flops=4 * square * aux_total,
     )
@@ -514,11 +527,19 @@
         [rows_far, rows_near],
         [part],
     )
-    gamma, density = call(
-        "outcome",
-        outcome_kernel,
-        [shape(jnp.float32, width, 1, virtuals), shape(jnp.float32, rows, virtuals)],
-        [part, got_first, got_zeroth, block, core_swap(block)],
+    other = core_swap(block)
+    gamma = call(
+        "gamma_sum",
+        gamma_sum_kernel,
+        shape(jnp.float32, width, 1, virtuals),
+        [part, got_first, got_zeroth],
+        [block],
+    )
+    density = call(
+        "density_sum",
+        density_sum_kernel,
+        shape(jnp.float32, rows, virtuals),
+        [block, other],
     )
     return gamma, density
 

time: 63.8 us -> 63 us (0.987)
  waiting for transfers between devices: 12.8 us -> 11.1 us
  Pallas kernels: 12.8 us -> 13.8 us
    ppermute x24, waiting for transfers between devices: 12.8 us -> 11.1 us  [send(): return lax.ppermute(value, AXES, pairs)]
    pallas_call x13 -> x15, Pallas kernels: 12.8 us -> 13.8 us  [call(): pl.pallas_call(kernel, in_specs=[vmem] * len(operands) + [unread] * len(e...]
  transfers between devices with their start and end apart: 24 -> 24, of which waited for: 9 -> 7; matrix products, arithmetic and copies ran while one was open for 0% -> 0% of each run, Pallas kernels for 15% -> 18%
where the time goes in v6:
time: 63 us; the launch traced here: 62.8 us
  starting transfers between devices  34.8 us (55%)
  Pallas kernels  13.8 us (22%)
  waiting for transfers between devices  11.1 us (18%)
  local copies, waits for them, and re-layouts  2.2 us (3%)
  between operations  0.92 us (1%)
    ppermute x24, starting transfers between devices, send(): return lax.ppermute(value, AXES, pairs)  34.8 us
    pallas_call x15, Pallas kernels, call(): pl.pallas_call(kernel, in_specs=[vmem] * len(operands) + [unread] * len(e...  13.8 us
    ppermute x24, waiting for transfers between devices, send(): return lax.ppermute(value, AXES, pairs)  11.1 us
    unnamed x8, local copies, waits for them, and re-layouts  2.2 us
  transfers between devices with their start and end apart: 24, of which 7 were waited for; matrix products, arithmetic and copies ran while one was open for 0% of the time, Pallas kernels for 18%

profile of v6, /device:TPU:1, one launch (start us, length us, event | category | flops | bytes accessed | tf_op | source)
XLA Modules:
  0.0 62.8 jit_solution(12455760155549462126)
XLA Ops:
  0.6 2.1 %collective-permute-start = (bf16[512,256]{1,0:T(8,128)(2,1)}, bf16[512,256]{1,0:T(8,128)(2,1)S(1)}, u32[]{:S(2)}, u32[]{:S(2)}) collective-permute-start(bf16[512,256]{1,0:T(8,128)(2,1)} %bitcast.7), channel_id=1, source_target_pairs={{0,2},{1,3},{2,0},{3,1},{4,6},{5,7},{6,4},{7,5},{8,10},{9,11},{10,... | collective-permute-start | bytes 786440 | tf_op jit(solution)/shard_map/gather/ppermute | solution.py:148
  2.7 2.3 %collective-permute-start.1 = (bf16[512,256]{1,0:T(8,128)(2,1)}, bf16[512,256]{1,0:T(8,128)(2,1)S(1)}, u32[]{:S(2)}, u32[]{:S(2)}) collective-permute-start(bf16[512,256]{1,0:T(8,128)(2,1)} %bitcast.8), channel_id=1, source_target_pairs={{0,16},{1,17},{2,26},{3,27},{4,20},{5,21},{6,30},{7,31},{8,24},{9,... | collective-permute-start | bytes 786440 | tf_op jit(solution)/shard_map/gather/ppermute | solution.py:148
  5.0 3.2 %collective-permute-start.3 = (bf16[512,256]{1,0:T(8,128)(2,1)}, bf16[512,256]{1,0:T(8,128)(2,1)S(1)}, u32[]{:S(2)}, u32[]{:S(2)}) collective-permute-start(bf16[512,256]{1,0:T(8,128)(2,1)} %bitcast.9), channel_id=1, source_target_pairs={{0,8},{1,9},{2,2},{3,3},{4,12},{5,13},{6,6},{7,7},{8,0},{9,1},{10,... | collective-permute-start | bytes 786440 | tf_op jit(solution)/shard_map/gather/ppermute | solution.py:148
  8.3 1.5 %collective-permute-start.5 = (bf16[512,256]{1,0:T(8,128)(2,1)}, bf16[512,256]{1,0:T(8,128)(2,1)S(1)}, u32[]{:S(2)}, u32[]{:S(2)}) collective-permute-start(bf16[512,256]{1,0:T(8,128)(2,1)} %bitcast.11), channel_id=1, source_target_pairs={{0,4},{1,0},{2,6},{3,2},{4,5},{5,1},{6,7},{7,3},{8,12},{9,8},{10,1... | collective-permute-start | bytes 786440 | tf_op jit(solution)/shard_map/gather/ppermute | solution.py:148
  9.8 3.6 %collective-permute-start.6 = (bf16[512,256]{1,0:T(8,128)(2,1)}, bf16[512,256]{1,0:T(8,128)(2,1)S(1)}, u32[]{:S(2)}, u32[]{:S(2)}) collective-permute-start(bf16[512,256]{1,0:T(8,128)(2,1)} %bitcast.12), channel_id=1, source_target_pairs={{0,0},{1,4},{2,2},{3,6},{4,1},{5,5},{6,3},{7,7},{8,8},{9,12},{10,1... | collective-permute-start | bytes 786440 | tf_op jit(solution)/shard_map/gather/ppermute | solution.py:148
  13.5 3.2 %collective-permute-done.1.refs_2_.refs_0_ = bf16[512,256]{1,0:T(8,128)(2,1)S(1)} collective-permute-done((bf16[512,256]{1,0:T(8,128)(2,1)}, bf16[512,256]{1,0:T(8,128)(2,1)S(1)}, u32[]{:S(2)}, u32[]{:S(2)}) %collective-permute-start.1) | collective-permute-done | bytes 262176 | tf_op jit(solution)/shard_map/gather/ppermute | solution.py:148
  16.7 1.5 %collective-permute-done.3.refs_0_.refs_4_ = bf16[512,256]{1,0:T(8,128)(2,1)S(1)} collective-permute-done((bf16[512,256]{1,0:T(8,128)(2,1)}, bf16[512,256]{1,0:T(8,128)(2,1)S(1)}, u32[]{:S(2)}, u32[]{:S(2)}) %collective-permute-start.3) | collective-permute-done | bytes 262176 | tf_op jit(solution)/shard_map/gather/ppermute | solution.py:148
  18.2 2.2 %collective-permute-start.7 = (bf16[512,256]{1,0:T(8,128)(2,1)S(1)}, bf16[512,256]{1,0:T(8,128)(2,1)S(1)}, u32[]{:S(2)}, u32[]{:S(2)}) collective-permute-start(bf16[512,256]{1,0:T(8,128)(2,1)S(1)} %collective-permute-done.swapped), channel_id=1, source_target_pairs={{0,4},{1,0},{2,6},{3,2},{4,5},{5,1},{6,7},{7,3},{8,12},{9,8},{10,1... | collective-permute-start | bytes 786440 | tf_op jit(solution)/shard_map/gather/ppermute | solution.py:148
  20.4 2.2 %copy-done = f32[1024,1024]{1,0:T(8,128)S(1)} copy-done((f32[1024,1024]{1,0:T(8,128)S(1)}, f32[1024,1024]{1,0:T(8,128)}, u32[]{:S(2)}) %copy-start) | copy-done | bytes 4194328
  22.6 1.3 %metric_turn.1 = (bf16[4,256,1024]{2,1,0:T(8,128)(2,1)S(1)}, bf16[4,256,1024]{2,1,0:T(8,128)(2,1)S(1)}) custom-call(f32[1024,1024]{1,0:T(8,128)S(1)} %copy-done), custom_call_target="tpu_custom_call" | custom-call | flops 1073741824 | tf_op jit(solution)/shard_map/metric_turn/pallas_call | solution.py:384
  23.9 3.0 %collective-permute-start.8 = (bf16[512,256]{1,0:T(8,128)(2,1)S(1)}, bf16[512,256]{1,0:T(8,128)(2,1)S(1)}, u32[]{:S(2)}, u32[]{:S(2)}) collective-permute-start(bf16[512,256]{1,0:T(8,128)(2,1)S(1)} %collective-permute-done.swapped), channel_id=1, source_target_pairs={{0,0},{1,4},{2,2},{3,6},{4,1},{5,5},{6,3},{7,7},{8,8},{9,12},{10,1... | collective-permute-start | bytes 786440 | tf_op jit(solution)/shard_map/gather/ppermute | solution.py:148
  27.0 2.5 %collective-permute-done.2.refs_3_.refs_1_ = bf16[512,256]{1,0:T(8,128)(2,1)S(1)} collective-permute-done((bf16[512,256]{1,0:T(8,128)(2,1)S(1)}, bf16[512,256]{1,0:T(8,128)(2,1)S(1)}, u32[]{:S(2)}, u32[]{:S(2)}) %collective-permute-start.2) | collective-permute-done | bytes 262176 | tf_op jit(solution)/shard_map/gather/ppermute | solution.py:148
  29.5 2.5 %collective-permute-start.11 = (bf16[512,256]{1,0:T(8,128)(2,1)S(1)}, bf16[512,256]{1,0:T(8,128)(2,1)S(1)}, u32[]{:S(2)}, u32[]{:S(2)}) collective-permute-start(bf16[512,256]{1,0:T(8,128)(2,1)S(1)} %collective-permute-done.3.refs_0_.refs_4_), channel_id=1, source_target_pairs={{0,1},{1,0},{2,3},{3,2},{4,5},{5,4},{6,7},{7,6},{8,9},{9,8},{10,11... | collective-permute-start | bytes 786440 | tf_op jit(solution)/shard_map/gather/ppermute | solution.py:148
  33.5 1.3 %first_pair.1 = (f32[512,1024]{1,0:T(8,128)S(1)}, bf16[512,512]{1,0:T(8,128)(2,1)S(1)}, bf16[512,512]{1,0:T(8,128)(2,1)S(1)}) custom-call(f32[1,8]{1,0:T(1,128)S(1)} %bitcast.5, f32[1,512]{1,0:T(1,128)S(1)} %bitcast.3, f32[512,512]{1,0:T(8,128)S(1)} %get-tuple-element.35.half, bf16[512,256]{1,0:T(8,128)(2,1)S(1)} %collective-permute-done.5.near.refs_0_, ...), custom_call_target="tpu_custom_call" | custom-call | tf_op jit(solution)/shard_map/first_pair/pallas_call | solution.py:384
  36.7 2.0 %gradient.1 = (bf16[512,1024]{1,0:T(8,128)(2,1)S(1)}, bf16[512,1024]{1,0:T(8,128)(2,1)S(1)}, bf16[272,512]{1,0:T(8,128)(2,1)S(1)}) custom-call(bf16[512,512]{1,0:T(8,128)(2,1)S(1)} %get-tuple-element.37.mixed.last_mixed, bf16[512,256]{1,0:T(8,128)(2,1)S(1)} %collective-permute-done.1.refs_2_.refs_0_, ...), custom_call_target="tpu_custom_call" | custom-call | flops 1610612736 | tf_op jit(solution)/shard_map/gradient/pallas_call | solution.py:384
  40.3 2.5 %collective-permute-start.18 = (bf16[80,512]{1,0:T(8,128)(2,1)S(1)}, bf16[80,512]{1,0:T(8,128)(2,1)S(1)}, u32[]{:S(2)}, u32[]{:S(2)}) collective-permute-start(bf16[80,512]{1,0:T(8,128)(2,1)S(1)} %get-tuple-element.48.refs_0_), channel_id=1, source_target_pairs={{0,8},{1,9},{2,10},{3,11},{4,12},{5,13},{6,14},{7,15},{8,0},{9,1},... | collective-permute-start | bytes 245768 | tf_op jit(solution)/shard_map/ppermute | solution.py:148
  42.7 1.3 %gamma_block.3.refs_0_ = bf16[272,512]{1,0:T(8,128)(2,1)S(1)} custom-call(bf16[4,256,1024]{2,1,0:T(8,128)(2,1)S(1)} %get-tuple-element.39.refs_5_.metric_high, bf16[4,256,1024]{2,1,0:T(8,128)(2,1)S(1)} %get-tuple-element.40.refs_6_.metric_low, bf16[512,1024]{1,0:T(8,128)(2,1)S(1)} %get-tuple-element.42.high, bf16[512,1024]{1,0:T(8,128)(2,1)S(1)} %get-tuple-element.43.low, ...), custom_call_target="tpu_custom_call" | custom-call | flops 805306368 | tf_op jit(solution)/shard_map/gamma_block/pallas_call | solution.py:384
  44.1 3.5 %collective-permute-start.15 = (bf16[272,512]{1,0:T(8,128)(2,1)S(1)}, bf16[272,512]{1,0:T(8,128)(2,1)S(1)}, u32[]{:S(2)}, u32[]{:S(2)}) collective-permute-start(bf16[272,512]{1,0:T(8,128)(2,1)S(1)} %gamma_block.3.refs_0_), channel_id=1, source_target_pairs={{0,2},{1,6},{2,0},{3,4},{4,3},{5,7},{6,1},{7,5},{8,10},{9,14},{10,... | collective-permute-start | bytes 835592 | tf_op jit(solution)/shard_map/ppermute | solution.py:148
  47.6 1.3 %gamma_block.4.refs_0_ = bf16[272,512]{1,0:T(8,128)(2,1)S(1)} custom-call(bf16[4,256,1024]{2,1,0:T(8,128)(2,1)S(1)} %get-tuple-element.39.refs_5_.metric_high, bf16[4,256,1024]{2,1,0:T(8,128)(2,1)S(1)} %get-tuple-element.40.refs_6_.metric_low, bf16[512,1024]{1,0:T(8,128)(2,1)S(1)} %get-tuple-element.42.high, bf16[512,1024]{1,0:T(8,128)(2,1)S(1)} %get-tuple-element.43.low, ...), custom_call_target="tpu_custom_call" | custom-call | flops 805306368 | tf_op jit(solution)/shard_map/gamma_block/pallas_call | solution.py:384
  49.4 1.3 %gamma_block.5.refs_0_ = bf16[272,512]{1,0:T(8,128)(2,1)S(1)} custom-call(bf16[4,256,1024]{2,1,0:T(8,128)(2,1)S(1)} %get-tuple-element.39.refs_5_.metric_high, bf16[4,256,1024]{2,1,0:T(8,128)(2,1)S(1)} %get-tuple-element.40.refs_6_.metric_low, bf16[512,1024]{1,0:T(8,128)(2,1)S(1)} %get-tuple-element.42.high, bf16[512,1024]{1,0:T(8,128)(2,1)S(1)} %get-tuple-element.43.low, ...), custom_call_target="tpu_custom_call" | custom-call | flops 805306368 | tf_op jit(solution)/shard_map/gamma_block/pallas_call | solution.py:384
  50.7 3.4 %collective-permute-start.20 = (bf16[272,512]{1,0:T(8,128)(2,1)S(1)}, bf16[272,512]{1,0:T(8,128)(2,1)S(1)}, u32[]{:S(2)}, u32[]{:S(2)}) collective-permute-start(bf16[272,512]{1,0:T(8,128)(2,1)S(1)} %gamma_block.5.refs_0_), channel_id=1, source_target_pairs={{0,0},{1,4},{2,2},{3,6},{4,1},{5,5},{6,3},{7,7},{8,8},{9,12},{10,1... | collective-permute-start | bytes 835592 | tf_op jit(solution)/shard_map/ppermute | solution.py:148
  54.2 2.6 %collective-permute-start.22 = (bf16[80,512]{1,0:T(8,128)(2,1)S(1)}, bf16[80,512]{1,0:T(8,128)(2,1)S(1)}, u32[]{:S(2)}, u32[]{:S(2)}) collective-permute-start(bf16[80,512]{1,0:T(8,128)(2,1)S(1)} %density_rows.1.refs_0_.refs_1_), channel_id=1, source_target_pairs={{0,4},{1,0},{2,6},{3,2},{4,5},{5,1},{6,7},{7,3},{8,12},{9,8},{10,1... | collective-permute-start | bytes 245768 | tf_op jit(solution)/shard_map/ppermute | solution.py:148
  57.1 2.0 %collective-permute-done.21.far = bf16[80,512]{1,0:T(8,128)(2,1)S(1)} collective-permute-done((bf16[80,512]{1,0:T(8,128)(2,1)S(1)}, bf16[80,512]{1,0:T(8,128)(2,1)S(1)}, u32[]{:S(2)}, u32[]{:S(2)}) %collective-permute-start.21) | collective-permute-done | bytes 81952 | tf_op jit(solution)/shard_map/ppermute | solution.py:148
  60.8 1.2 %gamma_sum.1 = f32[256,1,512]{2,1,0:T(1,128)} custom-call(f32[256,512]{1,0:T(8,128)S(1)} %gamma_part.1.refs_0_.part, bf16[272,512]{1,0:T(8,128)(2,1)S(1)} %collective-permute-done.19.left, bf16[272,512]{1,0:T(8,128)(2,1)S(1)} %collective-permute-done.20.right, f32[64,512]{1,0:T(8,128)S(1)} %density_block.1.refs_0_.block), custom_call_target="tpu_custom_call" | custom-call | tf_op jit(solution)/shard_map/gamma_sum/pallas_call | solution.py:384
  (47 shorter events, 8.2 us)
Async XLA Ops:
  0.6 9.2 %collective-permute-start = (bf16[512,256]{1,0:T(8,128)(2,1)}, bf16[512,256]{1,0:T(8,128)(2,1)S(1)}, u32[]{:S(2)}, u32[]{:S(2)}) collective-permute-start(bf16[512,256]{1,0:T(8,128)(2,1)} %bitcast.7), channel_id=1, source_target_pairs={{0,2},{1,3},{2,0},{3,1},{4,6},{5,7},{6,4},{7,5},{8,10},{9,11},{10,... | collective-permute-start | bytes 786440 | tf_op jit(solution)/shard_map/gather/ppermute | solution.py:148
  2.7 13.9 %collective-permute-start.1 = (bf16[512,256]{1,0:T(8,128)(2,1)}, bf16[512,256]{1,0:T(8,128)(2,1)S(1)}, u32[]{:S(2)}, u32[]{:S(2)}) collective-permute-start(bf16[512,256]{1,0:T(8,128)(2,1)} %bitcast.8), channel_id=1, source_target_pairs={{0,16},{1,17},{2,26},{3,27},{4,20},{5,21},{6,30},{7,31},{8,24},{9,... | collective-permute-start | bytes 786440 | tf_op jit(solution)/shard_map/gather/ppermute | solution.py:148
  5.0 13.2 %collective-permute-start.3 = (bf16[512,256]{1,0:T(8,128)(2,1)}, bf16[512,256]{1,0:T(8,128)(2,1)S(1)}, u32[]{:S(2)}, u32[]{:S(2)}) collective-permute-start(bf16[512,256]{1,0:T(8,128)(2,1)} %bitcast.9), channel_id=1, source_target_pairs={{0,8},{1,9},{2,2},{3,3},{4,12},{5,13},{6,6},{7,7},{8,0},{9,1},{10,... | collective-permute-start | bytes 786440 | tf_op jit(solution)/shard_map/gather/ppermute | solution.py:148
  8.2 15.6 %collective-permute-start.4 = (bf16[512,256]{1,0:T(8,128)(2,1)}, bf16[512,256]{1,0:T(8,128)(2,1)S(1)}, u32[]{:S(2)}, u32[]{:S(2)}) collective-permute-start(bf16[512,256]{1,0:T(8,128)(2,1)} %bitcast.10), channel_id=1, source_target_pairs={{0,2},{1,3},{2,8},{3,9},{4,6},{5,7},{6,12},{7,13},{8,10},{9,11},{1... | collective-permute-start | bytes 786440 | tf_op jit(solution)/shard_map/gather/ppermute | solution.py:148
  8.3 18.6 %collective-permute-start.5 = (bf16[512,256]{1,0:T(8,128)(2,1)}, bf16[512,256]{1,0:T(8,128)(2,1)S(1)}, u32[]{:S(2)}, u32[]{:S(2)}) collective-permute-start(bf16[512,256]{1,0:T(8,128)(2,1)} %bitcast.11), channel_id=1, source_target_pairs={{0,4},{1,0},{2,6},{3,2},{4,5},{5,1},{6,7},{7,3},{8,12},{9,8},{10,1... | collective-permute-start | bytes 786440 | tf_op jit(solution)/shard_map/gather/ppermute | solution.py:148
  9.8 17.1 %collective-permute-start.6 = (bf16[512,256]{1,0:T(8,128)(2,1)}, bf16[512,256]{1,0:T(8,128)(2,1)S(1)}, u32[]{:S(2)}, u32[]{:S(2)}) collective-permute-start(bf16[512,256]{1,0:T(8,128)(2,1)} %bitcast.12), channel_id=1, source_target_pairs={{0,0},{1,4},{2,2},{3,6},{4,1},{5,5},{6,3},{7,7},{8,8},{9,12},{10,1... | collective-permute-start | bytes 786440 | tf_op jit(solution)/shard_map/gather/ppermute | solution.py:148
  16.7 12.8 %collective-permute-start.2 = (bf16[512,256]{1,0:T(8,128)(2,1)S(1)}, bf16[512,256]{1,0:T(8,128)(2,1)S(1)}, u32[]{:S(2)}, u32[]{:S(2)}) collective-permute-start(bf16[512,256]{1,0:T(8,128)(2,1)S(1)} %collective-permute-done.swapped), channel_id=1, source_target_pairs={{0,16},{1,17},{2,26},{3,27},{4,20},{5,21},{6,30},{7,31},{8,24},{9,... | collective-permute-start | bytes 786440 | tf_op jit(solution)/shard_map/gather/ppermute | solution.py:148
  18.2 14.2 %collective-permute-start.7 = (bf16[512,256]{1,0:T(8,128)(2,1)S(1)}, bf16[512,256]{1,0:T(8,128)(2,1)S(1)}, u32[]{:S(2)}, u32[]{:S(2)}) collective-permute-start(bf16[512,256]{1,0:T(8,128)(2,1)S(1)} %collective-permute-done.swapped), channel_id=1, source_target_pairs={{0,4},{1,0},{2,6},{3,2},{4,5},{5,1},{6,7},{7,3},{8,12},{9,8},{10,1... | collective-permute-start | bytes 786440 | tf_op jit(solution)/shard_map/gather/ppermute | solution.py:148
  23.9 9.3 %collective-permute-start.8 = (bf16[512,256]{1,0:T(8,128)(2,1)S(1)}, bf16[512,256]{1,0:T(8,128)(2,1)S(1)}, u32[]{:S(2)}, u32[]{:S(2)}) collective-permute-start(bf16[512,256]{1,0:T(8,128)(2,1)S(1)} %collective-permute-done.swapped), channel_id=1, source_target_pairs={{0,0},{1,4},{2,2},{3,6},{4,1},{5,5},{6,3},{7,7},{8,8},{9,12},{10,1... | collective-permute-start | bytes 786440 | tf_op jit(solution)/shard_map/gather/ppermute | solution.py:148
  29.5 3.7 %collective-permute-start.11 = (bf16[512,256]{1,0:T(8,128)(2,1)S(1)}, bf16[512,256]{1,0:T(8,128)(2,1)S(1)}, u32[]{:S(2)}, u32[]{:S(2)}) collective-permute-start(bf16[512,256]{1,0:T(8,128)(2,1)S(1)} %collective-permute-done.3.refs_0_.refs_4_), channel_id=1, source_target_pairs={{0,1},{1,0},{2,3},{3,2},{4,5},{5,4},{6,7},{7,6},{8,9},{9,8},{10,11... | collective-permute-start | bytes 786440 | tf_op jit(solution)/shard_map/gather/ppermute | solution.py:148
  31.9 1.5 %collective-permute-start.12 = (bf16[512,256]{1,0:T(8,128)(2,1)S(1)}, bf16[512,256]{1,0:T(8,128)(2,1)S(1)}, u32[]{:S(2)}, u32[]{:S(2)}) collective-permute-start(bf16[512,256]{1,0:T(8,128)(2,1)S(1)} %collective-permute-done.4.refs_1_.refs_5_), channel_id=1, source_target_pairs={{0,1},{1,0},{2,3},{3,2},{4,5},{5,4},{6,7},{7,6},{8,9},{9,8},{10,11... | collective-permute-start | bytes 786440 | tf_op jit(solution)/shard_map/gather/ppermute | solution.py:148
  31.9 2.8 %collective-permute-start.10 = (bf16[512,256]{1,0:T(8,128)(2,1)S(1)}, bf16[512,256]{1,0:T(8,128)(2,1)S(1)}, u32[]{:S(2)}, u32[]{:S(2)}) collective-permute-start(bf16[512,256]{1,0:T(8,128)(2,1)S(1)} %collective-permute-done.2.refs_3_.refs_1_), channel_id=1, source_target_pairs={{0,1},{1,0},{2,3},{3,2},{4,5},{5,4},{6,7},{7,6},{8,9},{9,8},{10,11... | collective-permute-start | bytes 786440 | tf_op jit(solution)/shard_map/gather/ppermute | solution.py:148
  32.4 2.3 %collective-permute-start.9 = (bf16[512,256]{1,0:T(8,128)(2,1)S(1)}, bf16[512,256]{1,0:T(8,128)(2,1)S(1)}, u32[]{:S(2)}, u32[]{:S(2)}) collective-permute-start(bf16[512,256]{1,0:T(8,128)(2,1)S(1)} %collective-permute-done.1.refs_2_.refs_0_), channel_id=1, source_target_pairs={{0,1},{1,0},{2,3},{3,2},{4,5},{5,4},{6,7},{7,6},{8,9},{9,8},{10,11... | collective-permute-start | bytes 786440 | tf_op jit(solution)/shard_map/gather/ppermute | solution.py:148
  36.3 2.5 %collective-permute-start.14 = (f32[4,64,512]{2,1,0:T(8,128)S(1)}, f32[4,64,512]{2,1,0:T(8,128)S(1)}, u32[]{:S(2)}, u32[]{:S(2)}) collective-permute-start(f32[4,64,512]{2,1,0:T(8,128)S(1)} %get-tuple-element.47), channel_id=1, source_target_pairs={{0,1},{1,0},{2,3},{3,2},{4,5},{5,4},{6,7},{7,6},{8,9},{9,8},{10,11... | collective-permute-start | bytes 1572872 | tf_op jit(solution)/shard_map/ppermute | solution.py:148
  38.7 15.4 %collective-permute-start.13 = (bf16[272,512]{1,0:T(8,128)(2,1)S(1)}, bf16[272,512]{1,0:T(8,128)(2,1)S(1)}, u32[]{:S(2)}, u32[]{:S(2)}) collective-permute-start(bf16[272,512]{1,0:T(8,128)(2,1)S(1)} %get-tuple-element.41.refs_0_), channel_id=1, source_target_pairs={{0,3},{1,7},{2,1},{3,5},{4,2},{5,6},{6,0},{7,4},{8,11},{9,15},{10,... | collective-permute-start | bytes 835592 | tf_op jit(solution)/shard_map/ppermute | solution.py:148
  39.1 9.8 %collective-permute-start.16 = (bf16[80,512]{1,0:T(8,128)(2,1)S(1)}, bf16[80,512]{1,0:T(8,128)(2,1)S(1)}, u32[]{:S(2)}, u32[]{:S(2)}) collective-permute-start(bf16[80,512]{1,0:T(8,128)(2,1)S(1)} %get-tuple-element.50), channel_id=1, source_target_pairs={{0,24},{1,25},{2,26},{3,27},{4,28},{5,29},{6,30},{7,31},{8,16},{9,... | collective-permute-start | bytes 245768 | tf_op jit(solution)/shard_map/ppermute | solution.py:148
  40.1 8.9 %collective-permute-start.17 = (bf16[80,512]{1,0:T(8,128)(2,1)S(1)}, bf16[80,512]{1,0:T(8,128)(2,1)S(1)}, u32[]{:S(2)}, u32[]{:S(2)}) collective-permute-start(bf16[80,512]{1,0:T(8,128)(2,1)S(1)} %get-tuple-element.51), channel_id=1, source_target_pairs={{0,16},{1,17},{2,18},{3,19},{4,20},{5,21},{6,22},{7,23},{8,24},{9,... | collective-permute-start | bytes 245768 | tf_op jit(solution)/shard_map/ppermute | solution.py:148
  40.3 8.8 %collective-permute-start.18 = (bf16[80,512]{1,0:T(8,128)(2,1)S(1)}, bf16[80,512]{1,0:T(8,128)(2,1)S(1)}, u32[]{:S(2)}, u32[]{:S(2)}) collective-permute-start(bf16[80,512]{1,0:T(8,128)(2,1)S(1)} %get-tuple-element.48.refs_0_), channel_id=1, source_target_pairs={{0,8},{1,9},{2,10},{3,11},{4,12},{5,13},{6,14},{7,15},{8,0},{9,1},... | collective-permute-start | bytes 245768 | tf_op jit(solution)/shard_map/ppermute | solution.py:148
  44.1 12.7 %collective-permute-start.15 = (bf16[272,512]{1,0:T(8,128)(2,1)S(1)}, bf16[272,512]{1,0:T(8,128)(2,1)S(1)}, u32[]{:S(2)}, u32[]{:S(2)}) collective-permute-start(bf16[272,512]{1,0:T(8,128)(2,1)S(1)} %gamma_block.3.refs_0_), channel_id=1, source_target_pairs={{0,2},{1,6},{2,0},{3,4},{4,3},{5,7},{6,1},{7,5},{8,10},{9,14},{10,... | collective-permute-start | bytes 835592 | tf_op jit(solution)/shard_map/ppermute | solution.py:148
  49.0 11.4 %collective-permute-start.19 = (bf16[272,512]{1,0:T(8,128)(2,1)S(1)}, bf16[272,512]{1,0:T(8,128)(2,1)S(1)}, u32[]{:S(2)}, u32[]{:S(2)}) collective-permute-start(bf16[272,512]{1,0:T(8,128)(2,1)S(1)} %gamma_block.4.refs_0_), channel_id=1, source_target_pairs={{0,1},{1,5},{2,3},{3,7},{4,0},{5,4},{6,2},{7,6},{8,9},{9,13},{10,1... | collective-permute-start | bytes 835592 | tf_op jit(solution)/shard_map/ppermute | solution.py:148
  50.7 10.2 %collective-permute-start.20 = (bf16[272,512]{1,0:T(8,128)(2,1)S(1)}, bf16[272,512]{1,0:T(8,128)(2,1)S(1)}, u32[]{:S(2)}, u32[]{:S(2)}) collective-permute-start(bf16[272,512]{1,0:T(8,128)(2,1)S(1)} %gamma_block.5.refs_0_), channel_id=1, source_target_pairs={{0,0},{1,4},{2,2},{3,6},{4,1},{5,5},{6,3},{7,7},{8,8},{9,12},{10,1... | collective-permute-start | bytes 835592 | tf_op jit(solution)/shard_map/ppermute | solution.py:148
  54.1 5.0 %collective-permute-start.21 = (bf16[80,512]{1,0:T(8,128)(2,1)S(1)}, bf16[80,512]{1,0:T(8,128)(2,1)S(1)}, u32[]{:S(2)}, u32[]{:S(2)}) collective-permute-start(bf16[80,512]{1,0:T(8,128)(2,1)S(1)} %density_rows.1.refs_0_.refs_1_), channel_id=1, source_target_pairs={{0,6},{1,2},{2,4},{3,0},{4,7},{5,3},{6,5},{7,1},{8,14},{9,10},{10,... | collective-permute-start | bytes 245768 | tf_op jit(solution)/shard_map/ppermute | solution.py:148
  54.2 6.1 %collective-permute-start.22 = (bf16[80,512]{1,0:T(8,128)(2,1)S(1)}, bf16[80,512]{1,0:T(8,128)(2,1)S(1)}, u32[]{:S(2)}, u32[]{:S(2)}) collective-permute-start(bf16[80,512]{1,0:T(8,128)(2,1)S(1)} %density_rows.1.refs_0_.refs_1_), channel_id=1, source_target_pairs={{0,4},{1,0},{2,6},{3,2},{4,5},{5,1},{6,7},{7,3},{8,12},{9,8},{10,1... | collective-permute-start | bytes 245768 | tf_op jit(solution)/shard_map/ppermute | solution.py:148
  60.3 1.7 %collective-permute-start.23 = (f32[64,512]{1,0:T(8,128)S(1)}, f32[64,512]{1,0:T(8,128)S(1)}, u32[]{:S(2)}, u32[]{:S(2)}) collective-permute-start(f32[64,512]{1,0:T(8,128)S(1)} %density_block.1.refs_0_.block), channel_id=1, source_target_pairs={{0,1},{1,0},{2,3},{3,2},{4,5},{5,4},{6,7},{7,6},{8,9},{9,8},{10,11... | collective-permute-start | bytes 393224 | tf_op jit(solution)/shard_map/ppermute | solution.py:148
  (4 other events, 31.3 us)

commit v7 on v6

--- a/solution.py
+++ b/solution.py
@@ -300,8 +300,12 @@
             low[step, :, cols] = dot(unit, rest, NT).astype(jnp.bfloat16)
 
 
-def gamma_part_kernel(left, right, *refs):
-    refs[-1][...] = decode(left) + decode(right)
+def decode_kernel(message, *refs):
+    refs[-1][...] = decode(message)
+
+
+def gamma_part_kernel(part, message, *refs):
+    refs[-1][...] = part[...] + decode(message)
 
 
 def density_cores_kernel(keep, got, *refs):
@@ -359,11 +363,14 @@
     def first_partner_cross(value):
         return move(value, lambda z, y, x, c: (z ^ 1 if x else z, y, 1 - x, c))
 
-    def last_partner(value):
-        return move(value, lambda z, y, x, c: (z ^ 3 if x else z ^ 2, y, x, c))
-
-    def last_partner_cross(value):
-        return move(value, lambda z, y, x, c: (z ^ 2 if x else z ^ 3, y, 1 - x, c))
+    def opposite_layer(value):
+        return move(value, lambda z, y, x, c: (z ^ 2, y, x, c))
+
+    def last_forward(value):
+        return move(value, lambda z, y, x, c: (z ^ 1 if x else z, y, x, c))
+
+    def last_forward_cross(value):
+        return move(value, lambda z, y, x, c: (z if x else z ^ 1, y, 1 - x, c))
 
     def near_left(value):
         return move(value, lambda z, y, x, c: (z, 1 - y, x, c) if c == y else (z, y, x, 1 - c))
@@ -403,19 +410,25 @@
         flops=4 * aux_total * aux_total * width,
     )
     with jax.named_scope("gather"):
-        swapped = x_swap(own)
-        last_own, last_swapped, first_own, first_cross, near_own, far_own, metric_high = lax.optimization_barrier(
+        swapped, opposite, metric_high = lax.optimization_barrier(
             (
-                last_partner(own),
-                last_partner(swapped),
+                x_swap(own),
+                opposite_layer(own),
+                metric_high,
+            )
+        )
+        last_swapped, last_own, first_own, first_cross, near_own, far_own = lax.optimization_barrier(
+            (
+                last_forward_cross(opposite),
+                last_forward(opposite),
                 first_partner(own),
                 first_partner_cross(own),
                 near_left(own),
                 far_left(own),
-                metric_high,
             )
         )
-        far_swapped, near_swapped = far_left(swapped), near_left(swapped)
+        near_swapped = near_left(swapped)
+        far_swapped = far_left(swapped)
         left = [own, swapped, near_own, near_swapped, far_own, far_swapped]
         first = [first_own, first_cross, core_swap(first_own), core_swap(first_cross)]
         last = [last_own, last_swapped, core_swap(last_own), core_swap(last_swapped)]
@@ -501,7 +514,14 @@
     ]
     second = gamma_block(2, messages[0])
     got_second = gamma_move(2, second)
-    first_block = gamma_block(1, second)
+    third_part = call(
+        "gamma_third",
+        decode_kernel,
+        shape(jnp.float32, width, virtuals),
+        [got_third],
+        [second],
+    )
+    first_block = gamma_block(1, third_part)
     got_first = gamma_move(1, first_block)
     partial_rows = call(
         "density_rows",
@@ -517,7 +537,7 @@
         "gamma_part",
         gamma_part_kernel,
         shape(jnp.float32, width, virtuals),
-        [got_third, got_second],
+        [third_part, got_second],
         [zeroth, partial_rows],
     )
     block = call(

time: 63 us -> 61.7 us (0.979)
  waiting for transfers between devices: 11.1 us -> 9.75 us
    ppermute x24 -> x25, waiting for transfers between devices: 11.1 us -> 9.75 us  [send(): return lax.ppermute(value, AXES, pairs)]
    pallas_call x15 -> x16, Pallas kernels: 13.8 us -> 13.8 us  [call(): pl.pallas_call(kernel, in_specs=[vmem] * len(operands) + [unread] * len(e...]
    ppermute x24 -> x25, starting transfers between devices: 34.8 us -> 34.8 us  [send(): return lax.ppermute(value, AXES, pairs)]
  transfers between devices with their start and end apart: 24 -> 25, of which waited for: 7 -> 8; matrix products, arithmetic and copies ran while one was open for 0% -> 0% of each run, Pallas kernels for 18% -> 19%
where the time goes in v7:
time: 61.7 us; the launch traced here: 61.4 us
  starting transfers between devices  34.8 us (56%)
  Pallas kernels  13.8 us (22%)
  waiting for transfers between devices  9.75 us (16%)
  local copies, waits for them, and re-layouts  2.2 us (4%)
  between operations  0.88 us (1%)
    ppermute x25, starting transfers between devices, send(): return lax.ppermute(value, AXES, pairs)  34.8 us
    pallas_call x16, Pallas kernels, call(): pl.pallas_call(kernel, in_specs=[vmem] * len(operands) + [unread] * len(e...  13.8 us
    ppermute x25, waiting for transfers between devices, send(): return lax.ppermute(value, AXES, pairs)  9.75 us
    unnamed x8, local copies, waits for them, and re-layouts  2.2 us
  transfers between devices with their start and end apart: 25, of which 8 were waited for; matrix products, arithmetic and copies ran while one was open for 0% of the time, Pallas kernels for 19%

profile of v7, /device:TPU:1, one launch (start us, length us, event | category | flops | bytes accessed | tf_op | source)
XLA Modules:
  0.0 61.4 jit_solution(11590664515581532790)
XLA Ops:
  0.6 2.1 %collective-permute-start = (bf16[512,256]{1,0:T(8,128)(2,1)}, bf16[512,256]{1,0:T(8,128)(2,1)S(1)}, u32[]{:S(2)}, u32[]{:S(2)}) collective-permute-start(bf16[512,256]{1,0:T(8,128)(2,1)} %bitcast.7), channel_id=1, source_target_pairs={{0,2},{1,3},{2,0},{3,1},{4,6},{5,7},{6,4},{7,5},{8,10},{9,11},{10,... | collective-permute-start | bytes 786440 | tf_op jit(solution)/shard_map/gather/ppermute | solution.py:148
  2.7 2.3 %collective-permute-start.1 = (bf16[512,256]{1,0:T(8,128)(2,1)}, bf16[512,256]{1,0:T(8,128)(2,1)S(1)}, u32[]{:S(2)}, u32[]{:S(2)}) collective-permute-start(bf16[512,256]{1,0:T(8,128)(2,1)} %bitcast.8), channel_id=1, source_target_pairs={{0,16},{1,17},{2,18},{3,19},{4,20},{5,21},{6,22},{7,23},{8,24},{9,... | collective-permute-start | bytes 786440 | tf_op jit(solution)/shard_map/gather/ppermute | solution.py:148
  5.0 3.2 %collective-permute-start.4 = (bf16[512,256]{1,0:T(8,128)(2,1)}, bf16[512,256]{1,0:T(8,128)(2,1)S(1)}, u32[]{:S(2)}, u32[]{:S(2)}) collective-permute-start(bf16[512,256]{1,0:T(8,128)(2,1)} %bitcast.9), channel_id=1, source_target_pairs={{0,8},{1,9},{2,2},{3,3},{4,12},{5,13},{6,6},{7,7},{8,0},{9,1},{10,... | collective-permute-start | bytes 786440 | tf_op jit(solution)/shard_map/gather/ppermute | solution.py:148
  8.3 1.5 %collective-permute-start.6 = (bf16[512,256]{1,0:T(8,128)(2,1)}, bf16[512,256]{1,0:T(8,128)(2,1)S(1)}, u32[]{:S(2)}, u32[]{:S(2)}) collective-permute-start(bf16[512,256]{1,0:T(8,128)(2,1)} %bitcast.11), channel_id=1, source_target_pairs={{0,4},{1,0},{2,6},{3,2},{4,5},{5,1},{6,7},{7,3},{8,12},{9,8},{10,1... | collective-permute-start | bytes 786440 | tf_op jit(solution)/shard_map/gather/ppermute | solution.py:148
  9.8 2.2 %copy-done = f32[1024,1024]{1,0:T(8,128)S(1)} copy-done((f32[1024,1024]{1,0:T(8,128)S(1)}, f32[1024,1024]{1,0:T(8,128)}, u32[]{:S(2)}) %copy-start) | copy-done | bytes 4194328
  12.0 1.3 %metric_turn.1 = (bf16[4,256,1024]{2,1,0:T(8,128)(2,1)S(1)}, bf16[4,256,1024]{2,1,0:T(8,128)(2,1)S(1)}) custom-call(f32[1024,1024]{1,0:T(8,128)S(1)} %copy-done), custom_call_target="tpu_custom_call" | custom-call | flops 1073741824 | tf_op jit(solution)/shard_map/metric_turn/pallas_call | solution.py:391
  13.4 3.0 %collective-permute-start.7 = (bf16[512,256]{1,0:T(8,128)(2,1)S(1)}, bf16[512,256]{1,0:T(8,128)(2,1)S(1)}, u32[]{:S(2)}, u32[]{:S(2)}) collective-permute-start(bf16[512,256]{1,0:T(8,128)(2,1)S(1)} %bitcast.12), channel_id=1, source_target_pairs={{0,0},{1,4},{2,2},{3,6},{4,1},{5,5},{6,3},{7,7},{8,8},{9,12},{10,1... | collective-permute-start | bytes 786440 | tf_op jit(solution)/shard_map/gather/ppermute | solution.py:148
  16.7 2.4 %collective-permute-start.2 = (bf16[512,256]{1,0:T(8,128)(2,1)S(1)}, bf16[512,256]{1,0:T(8,128)(2,1)S(1)}, u32[]{:S(2)}, u32[]{:S(2)}) collective-permute-start(bf16[512,256]{1,0:T(8,128)(2,1)S(1)} %collective-permute-done.1), channel_id=1, source_target_pairs={{0,10},{1,11},{2,0},{3,1},{4,14},{5,15},{6,4},{7,5},{8,2},{9,3},{1... | collective-permute-start | bytes 786440 | tf_op jit(solution)/shard_map/gather/ppermute | solution.py:148
  19.8 1.4 %collective-permute-done.5.refs_1_.refs_5_ = bf16[512,256]{1,0:T(8,128)(2,1)S(1)} collective-permute-done((bf16[512,256]{1,0:T(8,128)(2,1)}, bf16[512,256]{1,0:T(8,128)(2,1)S(1)}, u32[]{:S(2)}, u32[]{:S(2)}) %collective-permute-start.5) | collective-permute-done | bytes 262176 | tf_op jit(solution)/shard_map/gather/ppermute | solution.py:148
  21.1 1.5 %collective-permute-start.8 = (bf16[512,256]{1,0:T(8,128)(2,1)S(1)}, bf16[512,256]{1,0:T(8,128)(2,1)S(1)}, u32[]{:S(2)}, u32[]{:S(2)}) collective-permute-start(bf16[512,256]{1,0:T(8,128)(2,1)S(1)} %collective-permute-done.swapped), channel_id=1, source_target_pairs={{0,4},{1,0},{2,6},{3,2},{4,5},{5,1},{6,7},{7,3},{8,12},{9,8},{10,1... | collective-permute-start | bytes 786440 | tf_op jit(solution)/shard_map/gather/ppermute | solution.py:148
  22.7 3.1 %collective-permute-start.9 = (bf16[512,256]{1,0:T(8,128)(2,1)S(1)}, bf16[512,256]{1,0:T(8,128)(2,1)S(1)}, u32[]{:S(2)}, u32[]{:S(2)}) collective-permute-start(bf16[512,256]{1,0:T(8,128)(2,1)S(1)} %collective-permute-done.swapped), channel_id=1, source_target_pairs={{0,0},{1,4},{2,2},{3,6},{4,1},{5,5},{6,3},{7,7},{8,8},{9,12},{10,1... | collective-permute-start | bytes 786440 | tf_op jit(solution)/shard_map/gather/ppermute | solution.py:148
  25.8 1.9 %collective-permute-done.2.refs_3_.refs_1_ = bf16[512,256]{1,0:T(8,128)(2,1)S(1)} collective-permute-done((bf16[512,256]{1,0:T(8,128)(2,1)S(1)}, bf16[512,256]{1,0:T(8,128)(2,1)S(1)}, u32[]{:S(2)}, u32[]{:S(2)}) %collective-permute-start.2) | collective-permute-done | bytes 262176 | tf_op jit(solution)/shard_map/gather/ppermute | solution.py:148
  30.6 1.3 %first_pair.1 = (f32[512,1024]{1,0:T(8,128)S(1)}, bf16[512,512]{1,0:T(8,128)(2,1)S(1)}, bf16[512,512]{1,0:T(8,128)(2,1)S(1)}) custom-call(f32[1,8]{1,0:T(1,128)S(1)} %bitcast.5, f32[1,512]{1,0:T(1,128)S(1)} %bitcast.3, f32[512,512]{1,0:T(8,128)S(1)} %get-tuple-element.39.half, bf16[512,256]{1,0:T(8,128)(2,1)S(1)} %collective-permute-done.6.near.refs_0_, ...), custom_call_target="tpu_custom_call" | custom-call | tf_op jit(solution)/shard_map/first_pair/pallas_call | solution.py:391
  33.5 2.0 %gradient.1 = (bf16[512,1024]{1,0:T(8,128)(2,1)S(1)}, bf16[512,1024]{1,0:T(8,128)(2,1)S(1)}, bf16[272,512]{1,0:T(8,128)(2,1)S(1)}) custom-call(bf16[512,512]{1,0:T(8,128)(2,1)S(1)} %get-tuple-element.41.mixed.last_mixed, bf16[512,256]{1,0:T(8,128)(2,1)S(1)} %collective-permute-done.3.refs_2_.refs_0_, ...), custom_call_target="tpu_custom_call" | custom-call | flops 1610612736 | tf_op jit(solution)/shard_map/gradient/pallas_call | solution.py:391
  35.5 2.3 %collective-permute-start.14 = (bf16[272,512]{1,0:T(8,128)(2,1)S(1)}, bf16[272,512]{1,0:T(8,128)(2,1)S(1)}, u32[]{:S(2)}, u32[]{:S(2)}) collective-permute-start(bf16[272,512]{1,0:T(8,128)(2,1)S(1)} %get-tuple-element.45.refs_0_), channel_id=1, source_target_pairs={{0,3},{1,7},{2,1},{3,5},{4,2},{5,6},{6,0},{7,4},{8,11},{9,15},{10,... | collective-permute-start | bytes 835592 | tf_op jit(solution)/shard_map/ppermute | solution.py:148
  38.1 3.1 %collective-permute-start.17 = (bf16[80,512]{1,0:T(8,128)(2,1)S(1)}, bf16[80,512]{1,0:T(8,128)(2,1)S(1)}, u32[]{:S(2)}, u32[]{:S(2)}) collective-permute-start(bf16[80,512]{1,0:T(8,128)(2,1)S(1)} %get-tuple-element.54), channel_id=1, source_target_pairs={{0,24},{1,25},{2,26},{3,27},{4,28},{5,29},{6,30},{7,31},{8,16},{9,... | collective-permute-start | bytes 245768 | tf_op jit(solution)/shard_map/ppermute | solution.py:148
  41.7 1.3 %gamma_block.3.refs_0_ = bf16[272,512]{1,0:T(8,128)(2,1)S(1)} custom-call(bf16[4,256,1024]{2,1,0:T(8,128)(2,1)S(1)} %get-tuple-element.43.refs_5_.metric_high, bf16[4,256,1024]{2,1,0:T(8,128)(2,1)S(1)} %get-tuple-element.44.refs_6_.metric_low, bf16[512,1024]{1,0:T(8,128)(2,1)S(1)} %get-tuple-element.46.high, bf16[512,1024]{1,0:T(8,128)(2,1)S(1)} %get-tuple-element.47.low, ...), custom_call_target="tpu_custom_call" | custom-call | flops 805306368 | tf_op jit(solution)/shard_map/gamma_block/pallas_call | solution.py:391
  43.1 1.7 %collective-permute-start.16 = (bf16[272,512]{1,0:T(8,128)(2,1)S(1)}, bf16[272,512]{1,0:T(8,128)(2,1)S(1)}, u32[]{:S(2)}, u32[]{:S(2)}) collective-permute-start(bf16[272,512]{1,0:T(8,128)(2,1)S(1)} %gamma_block.3.refs_0_), channel_id=1, source_target_pairs={{0,2},{1,6},{2,0},{3,4},{4,3},{5,7},{6,1},{7,5},{8,10},{9,14},{10,... | collective-permute-start | bytes 835592 | tf_op jit(solution)/shard_map/ppermute | solution.py:148
  44.9 1.3 %gamma_block.4.refs_0_ = bf16[272,512]{1,0:T(8,128)(2,1)S(1)} custom-call(bf16[4,256,1024]{2,1,0:T(8,128)(2,1)S(1)} %get-tuple-element.43.refs_5_.metric_high, bf16[4,256,1024]{2,1,0:T(8,128)(2,1)S(1)} %get-tuple-element.44.refs_6_.metric_low, bf16[512,1024]{1,0:T(8,128)(2,1)S(1)} %get-tuple-element.46.high, bf16[512,1024]{1,0:T(8,128)(2,1)S(1)} %get-tuple-element.47.low, ...), custom_call_target="tpu_custom_call" | custom-call | flops 805306368 | tf_op jit(solution)/shard_map/gamma_block/pallas_call | solution.py:391
  48.3 1.3 %gamma_block.5.refs_0_ = bf16[272,512]{1,0:T(8,128)(2,1)S(1)} custom-call(bf16[4,256,1024]{2,1,0:T(8,128)(2,1)S(1)} %get-tuple-element.43.refs_5_.metric_high, bf16[4,256,1024]{2,1,0:T(8,128)(2,1)S(1)} %get-tuple-element.44.refs_6_.metric_low, bf16[512,1024]{1,0:T(8,128)(2,1)S(1)} %get-tuple-element.46.high, bf16[512,1024]{1,0:T(8,128)(2,1)S(1)} %get-tuple-element.47.low, ...), custom_call_target="tpu_custom_call" | custom-call | flops 805306368 | tf_op jit(solution)/shard_map/gamma_block/pallas_call | solution.py:391
  49.6 3.3 %collective-permute-start.21 = (bf16[272,512]{1,0:T(8,128)(2,1)S(1)}, bf16[272,512]{1,0:T(8,128)(2,1)S(1)}, u32[]{:S(2)}, u32[]{:S(2)}) collective-permute-start(bf16[272,512]{1,0:T(8,128)(2,1)S(1)} %gamma_block.5.refs_0_), channel_id=1, source_target_pairs={{0,0},{1,4},{2,2},{3,6},{4,1},{5,5},{6,3},{7,7},{8,8},{9,12},{10,1... | collective-permute-start | bytes 835592 | tf_op jit(solution)/shard_map/ppermute | solution.py:148
  54.1 3.2 %collective-permute-done.22.far = bf16[80,512]{1,0:T(8,128)(2,1)S(1)} collective-permute-done((bf16[80,512]{1,0:T(8,128)(2,1)S(1)}, bf16[80,512]{1,0:T(8,128)(2,1)S(1)}, u32[]{:S(2)}, u32[]{:S(2)}) %collective-permute-start.22) | collective-permute-done | bytes 81952 | tf_op jit(solution)/shard_map/ppermute | solution.py:148
  57.3 1.3 %collective-permute-done.23.near = bf16[80,512]{1,0:T(8,128)(2,1)S(1)} collective-permute-done((bf16[80,512]{1,0:T(8,128)(2,1)S(1)}, bf16[80,512]{1,0:T(8,128)(2,1)S(1)}, u32[]{:S(2)}, u32[]{:S(2)}) %collective-permute-start.23) | collective-permute-done | bytes 81952 | tf_op jit(solution)/shard_map/ppermute | solution.py:148
  59.5 1.2 %gamma_sum.1 = f32[256,1,512]{2,1,0:T(1,128)} custom-call(f32[256,512]{1,0:T(8,128)S(1)} %gamma_part.1.refs_0_.part, bf16[272,512]{1,0:T(8,128)(2,1)S(1)} %collective-permute-done.20.left, bf16[272,512]{1,0:T(8,128)(2,1)S(1)} %collective-permute-done.21.right, f32[64,512]{1,0:T(8,128)S(1)} %density_block.1.refs_0_.block), custom_call_target="tpu_custom_call" | custom-call | tf_op jit(solution)/shard_map/gamma_sum/pallas_call | solution.py:391
  (50 shorter events, 11.1 us)
Async XLA Ops:
  0.6 12.7 %collective-permute-start = (bf16[512,256]{1,0:T(8,128)(2,1)}, bf16[512,256]{1,0:T(8,128)(2,1)S(1)}, u32[]{:S(2)}, u32[]{:S(2)}) collective-permute-start(bf16[512,256]{1,0:T(8,128)(2,1)} %bitcast.7), channel_id=1, source_target_pairs={{0,2},{1,3},{2,0},{3,1},{4,6},{5,7},{6,4},{7,5},{8,10},{9,11},{10,... | collective-permute-start | bytes 786440 | tf_op jit(solution)/shard_map/gather/ppermute | solution.py:148
  2.7 13.9 %collective-permute-start.1 = (bf16[512,256]{1,0:T(8,128)(2,1)}, bf16[512,256]{1,0:T(8,128)(2,1)S(1)}, u32[]{:S(2)}, u32[]{:S(2)}) collective-permute-start(bf16[512,256]{1,0:T(8,128)(2,1)} %bitcast.8), channel_id=1, source_target_pairs={{0,16},{1,17},{2,18},{3,19},{4,20},{5,21},{6,22},{7,23},{8,24},{9,... | collective-permute-start | bytes 786440 | tf_op jit(solution)/shard_map/gather/ppermute | solution.py:148
  5.0 14.1 %collective-permute-start.4 = (bf16[512,256]{1,0:T(8,128)(2,1)}, bf16[512,256]{1,0:T(8,128)(2,1)S(1)}, u32[]{:S(2)}, u32[]{:S(2)}) collective-permute-start(bf16[512,256]{1,0:T(8,128)(2,1)} %bitcast.9), channel_id=1, source_target_pairs={{0,8},{1,9},{2,2},{3,3},{4,12},{5,13},{6,6},{7,7},{8,0},{9,1},{10,... | collective-permute-start | bytes 786440 | tf_op jit(solution)/shard_map/gather/ppermute | solution.py:148
  8.2 12.9 %collective-permute-start.5 = (bf16[512,256]{1,0:T(8,128)(2,1)}, bf16[512,256]{1,0:T(8,128)(2,1)S(1)}, u32[]{:S(2)}, u32[]{:S(2)}) collective-permute-start(bf16[512,256]{1,0:T(8,128)(2,1)} %bitcast.10), channel_id=1, source_target_pairs={{0,2},{1,3},{2,8},{3,9},{4,6},{5,7},{6,12},{7,13},{8,10},{9,11},{1... | collective-permute-start | bytes 786440 | tf_op jit(solution)/shard_map/gather/ppermute | solution.py:148
  8.3 14.4 %collective-permute-start.6 = (bf16[512,256]{1,0:T(8,128)(2,1)}, bf16[512,256]{1,0:T(8,128)(2,1)S(1)}, u32[]{:S(2)}, u32[]{:S(2)}) collective-permute-start(bf16[512,256]{1,0:T(8,128)(2,1)} %bitcast.11), channel_id=1, source_target_pairs={{0,4},{1,0},{2,6},{3,2},{4,5},{5,1},{6,7},{7,3},{8,12},{9,8},{10,1... | collective-permute-start | bytes 786440 | tf_op jit(solution)/shard_map/gather/ppermute | solution.py:148
  13.4 12.4 %collective-permute-start.7 = (bf16[512,256]{1,0:T(8,128)(2,1)S(1)}, bf16[512,256]{1,0:T(8,128)(2,1)S(1)}, u32[]{:S(2)}, u32[]{:S(2)}) collective-permute-start(bf16[512,256]{1,0:T(8,128)(2,1)S(1)} %bitcast.12), channel_id=1, source_target_pairs={{0,0},{1,4},{2,2},{3,6},{4,1},{5,5},{6,3},{7,7},{8,8},{9,12},{10,1... | collective-permute-start | bytes 786440 | tf_op jit(solution)/shard_map/gather/ppermute | solution.py:148
  16.7 11.0 %collective-permute-start.2 = (bf16[512,256]{1,0:T(8,128)(2,1)S(1)}, bf16[512,256]{1,0:T(8,128)(2,1)S(1)}, u32[]{:S(2)}, u32[]{:S(2)}) collective-permute-start(bf16[512,256]{1,0:T(8,128)(2,1)S(1)} %collective-permute-done.1), channel_id=1, source_target_pairs={{0,10},{1,11},{2,0},{3,1},{4,14},{5,15},{6,4},{7,5},{8,2},{9,3},{1... | collective-permute-start | bytes 786440 | tf_op jit(solution)/shard_map/gather/ppermute | solution.py:148
  19.1 8.6 %collective-permute-start.3 = (bf16[512,256]{1,0:T(8,128)(2,1)S(1)}, bf16[512,256]{1,0:T(8,128)(2,1)S(1)}, u32[]{:S(2)}, u32[]{:S(2)}) collective-permute-start(bf16[512,256]{1,0:T(8,128)(2,1)S(1)} %collective-permute-done.1), channel_id=1, source_target_pairs={{0,0},{1,1},{2,10},{3,11},{4,4},{5,5},{6,14},{7,15},{8,8},{9,9},{1... | collective-permute-start | bytes 786440 | tf_op jit(solution)/shard_map/gather/ppermute | solution.py:148
  21.1 7.6 %collective-permute-start.8 = (bf16[512,256]{1,0:T(8,128)(2,1)S(1)}, bf16[512,256]{1,0:T(8,128)(2,1)S(1)}, u32[]{:S(2)}, u32[]{:S(2)}) collective-permute-start(bf16[512,256]{1,0:T(8,128)(2,1)S(1)} %collective-permute-done.swapped), channel_id=1, source_target_pairs={{0,4},{1,0},{2,6},{3,2},{4,5},{5,1},{6,7},{7,3},{8,12},{9,8},{10,1... | collective-permute-start | bytes 786440 | tf_op jit(solution)/shard_map/gather/ppermute | solution.py:148
  22.7 7.9 %collective-permute-start.9 = (bf16[512,256]{1,0:T(8,128)(2,1)S(1)}, bf16[512,256]{1,0:T(8,128)(2,1)S(1)}, u32[]{:S(2)}, u32[]{:S(2)}) collective-permute-start(bf16[512,256]{1,0:T(8,128)(2,1)S(1)} %collective-permute-done.swapped), channel_id=1, source_target_pairs={{0,0},{1,4},{2,2},{3,6},{4,1},{5,5},{6,3},{7,7},{8,8},{9,12},{10,1... | collective-permute-start | bytes 786440 | tf_op jit(solution)/shard_map/gather/ppermute | solution.py:148
  27.7 2.8 %collective-permute-start.12 = (bf16[512,256]{1,0:T(8,128)(2,1)S(1)}, bf16[512,256]{1,0:T(8,128)(2,1)S(1)}, u32[]{:S(2)}, u32[]{:S(2)}) collective-permute-start(bf16[512,256]{1,0:T(8,128)(2,1)S(1)} %collective-permute-done.4.refs_0_.refs_4_), channel_id=1, source_target_pairs={{0,1},{1,0},{2,3},{3,2},{4,5},{5,4},{6,7},{7,6},{8,9},{9,8},{10,11... | collective-permute-start | bytes 786440 | tf_op jit(solution)/shard_map/gather/ppermute | solution.py:148
  28.2 2.4 %collective-permute-start.13 = (bf16[512,256]{1,0:T(8,128)(2,1)S(1)}, bf16[512,256]{1,0:T(8,128)(2,1)S(1)}, u32[]{:S(2)}, u32[]{:S(2)}) collective-permute-start(bf16[512,256]{1,0:T(8,128)(2,1)S(1)} %collective-permute-done.5.refs_1_.refs_5_), channel_id=1, source_target_pairs={{0,1},{1,0},{2,3},{3,2},{4,5},{5,4},{6,7},{7,6},{8,9},{9,8},{10,11... | collective-permute-start | bytes 786440 | tf_op jit(solution)/shard_map/gather/ppermute | solution.py:148
  28.2 3.7 %collective-permute-start.10 = (bf16[512,256]{1,0:T(8,128)(2,1)S(1)}, bf16[512,256]{1,0:T(8,128)(2,1)S(1)}, u32[]{:S(2)}, u32[]{:S(2)}) collective-permute-start(bf16[512,256]{1,0:T(8,128)(2,1)S(1)} %collective-permute-done.3.refs_2_.refs_0_), channel_id=1, source_target_pairs={{0,1},{1,0},{2,3},{3,2},{4,5},{5,4},{6,7},{7,6},{8,9},{9,8},{10,11... | collective-permute-start | bytes 786440 | tf_op jit(solution)/shard_map/gather/ppermute | solution.py:148
  28.7 3.2 %collective-permute-start.11 = (bf16[512,256]{1,0:T(8,128)(2,1)S(1)}, bf16[512,256]{1,0:T(8,128)(2,1)S(1)}, u32[]{:S(2)}, u32[]{:S(2)}) collective-permute-start(bf16[512,256]{1,0:T(8,128)(2,1)S(1)} %collective-permute-done.2.refs_3_.refs_1_), channel_id=1, source_target_pairs={{0,1},{1,0},{2,3},{3,2},{4,5},{5,4},{6,7},{7,6},{8,9},{9,8},{10,11... | collective-permute-start | bytes 786440 | tf_op jit(solution)/shard_map/gather/ppermute | solution.py:148
  33.4 4.4 %collective-permute-start.15 = (f32[4,64,512]{2,1,0:T(8,128)S(1)}, f32[4,64,512]{2,1,0:T(8,128)S(1)}, u32[]{:S(2)}, u32[]{:S(2)}) collective-permute-start(f32[4,64,512]{2,1,0:T(8,128)S(1)} %get-tuple-element.51), channel_id=1, source_target_pairs={{0,1},{1,0},{2,3},{3,2},{4,5},{5,4},{6,7},{7,6},{8,9},{9,8},{10,11... | collective-permute-start | bytes 1572872 | tf_op jit(solution)/shard_map/ppermute | solution.py:148
  35.5 9.2 %collective-permute-start.14 = (bf16[272,512]{1,0:T(8,128)(2,1)S(1)}, bf16[272,512]{1,0:T(8,128)(2,1)S(1)}, u32[]{:S(2)}, u32[]{:S(2)}) collective-permute-start(bf16[272,512]{1,0:T(8,128)(2,1)S(1)} %get-tuple-element.45.refs_0_), channel_id=1, source_target_pairs={{0,3},{1,7},{2,1},{3,5},{4,2},{5,6},{6,0},{7,4},{8,11},{9,15},{10,... | collective-permute-start | bytes 835592 | tf_op jit(solution)/shard_map/ppermute | solution.py:148
  38.1 9.1 %collective-permute-start.17 = (bf16[80,512]{1,0:T(8,128)(2,1)S(1)}, bf16[80,512]{1,0:T(8,128)(2,1)S(1)}, u32[]{:S(2)}, u32[]{:S(2)}) collective-permute-start(bf16[80,512]{1,0:T(8,128)(2,1)S(1)} %get-tuple-element.54), channel_id=1, source_target_pairs={{0,24},{1,25},{2,26},{3,27},{4,28},{5,29},{6,30},{7,31},{8,16},{9,... | collective-permute-start | bytes 245768 | tf_op jit(solution)/shard_map/ppermute | solution.py:148
  41.3 6.7 %collective-permute-start.18 = (bf16[80,512]{1,0:T(8,128)(2,1)S(1)}, bf16[80,512]{1,0:T(8,128)(2,1)S(1)}, u32[]{:S(2)}, u32[]{:S(2)}) collective-permute-start(bf16[80,512]{1,0:T(8,128)(2,1)S(1)} %get-tuple-element.55), channel_id=1, source_target_pairs={{0,16},{1,17},{2,18},{3,19},{4,20},{5,21},{6,22},{7,23},{8,24},{9,... | collective-permute-start | bytes 245768 | tf_op jit(solution)/shard_map/ppermute | solution.py:148
  41.3 6.6 %collective-permute-start.19 = (bf16[80,512]{1,0:T(8,128)(2,1)S(1)}, bf16[80,512]{1,0:T(8,128)(2,1)S(1)}, u32[]{:S(2)}, u32[]{:S(2)}) collective-permute-start(bf16[80,512]{1,0:T(8,128)(2,1)S(1)} %get-tuple-element.52.refs_0_), channel_id=1, source_target_pairs={{0,8},{1,9},{2,10},{3,11},{4,12},{5,13},{6,14},{7,15},{8,0},{9,1},... | collective-permute-start | bytes 245768 | tf_op jit(solution)/shard_map/ppermute | solution.py:148
  43.1 10.8 %collective-permute-start.16 = (bf16[272,512]{1,0:T(8,128)(2,1)S(1)}, bf16[272,512]{1,0:T(8,128)(2,1)S(1)}, u32[]{:S(2)}, u32[]{:S(2)}) collective-permute-start(bf16[272,512]{1,0:T(8,128)(2,1)S(1)} %gamma_block.3.refs_0_), channel_id=1, source_target_pairs={{0,2},{1,6},{2,0},{3,4},{4,3},{5,7},{6,1},{7,5},{8,10},{9,14},{10,... | collective-permute-start | bytes 835592 | tf_op jit(solution)/shard_map/ppermute | solution.py:148
  46.3 12.5 %collective-permute-start.20 = (bf16[272,512]{1,0:T(8,128)(2,1)S(1)}, bf16[272,512]{1,0:T(8,128)(2,1)S(1)}, u32[]{:S(2)}, u32[]{:S(2)}) collective-permute-start(bf16[272,512]{1,0:T(8,128)(2,1)S(1)} %gamma_block.4.refs_0_), channel_id=1, source_target_pairs={{0,1},{1,5},{2,3},{3,7},{4,0},{5,4},{6,2},{7,6},{8,9},{9,13},{10,1... | collective-permute-start | bytes 835592 | tf_op jit(solution)/shard_map/ppermute | solution.py:148
  49.6 9.9 %collective-permute-start.21 = (bf16[272,512]{1,0:T(8,128)(2,1)S(1)}, bf16[272,512]{1,0:T(8,128)(2,1)S(1)}, u32[]{:S(2)}, u32[]{:S(2)}) collective-permute-start(bf16[272,512]{1,0:T(8,128)(2,1)S(1)} %gamma_block.5.refs_0_), channel_id=1, source_target_pairs={{0,0},{1,4},{2,2},{3,6},{4,1},{5,5},{6,3},{7,7},{8,8},{9,12},{10,1... | collective-permute-start | bytes 835592 | tf_op jit(solution)/shard_map/ppermute | solution.py:148
  53.0 4.4 %collective-permute-start.22 = (bf16[80,512]{1,0:T(8,128)(2,1)S(1)}, bf16[80,512]{1,0:T(8,128)(2,1)S(1)}, u32[]{:S(2)}, u32[]{:S(2)}) collective-permute-start(bf16[80,512]{1,0:T(8,128)(2,1)S(1)} %density_rows.1.refs_0_.refs_1_), channel_id=1, source_target_pairs={{0,6},{1,2},{2,4},{3,0},{4,7},{5,3},{6,5},{7,1},{8,14},{9,10},{10,... | collective-permute-start | bytes 245768 | tf_op jit(solution)/shard_map/ppermute | solution.py:148
  53.0 5.6 %collective-permute-start.23 = (bf16[80,512]{1,0:T(8,128)(2,1)S(1)}, bf16[80,512]{1,0:T(8,128)(2,1)S(1)}, u32[]{:S(2)}, u32[]{:S(2)}) collective-permute-start(bf16[80,512]{1,0:T(8,128)(2,1)S(1)} %density_rows.1.refs_0_.refs_1_), channel_id=1, source_target_pairs={{0,4},{1,0},{2,6},{3,2},{4,5},{5,1},{6,7},{7,3},{8,12},{9,8},{10,1... | collective-permute-start | bytes 245768 | tf_op jit(solution)/shard_map/ppermute | solution.py:148
  (5 other events, 40.0 us)

commit v8 on v7

--- a/solution.py
+++ b/solution.py
@@ -309,15 +309,13 @@
 
 
 def density_cores_kernel(keep, got, *refs):
-    layer_out, one, two, three = refs[-4:]
-    z, y, x, c = place_bits()
-    layer_out[...] = keep[z] + got[z]
-    for step, out in enumerate((one, two, three), 1):
+    z, y, x, c = place_bits()
+    for step, out in enumerate(refs[-keep.shape[0] :]):
         encode_into(out, keep[z ^ step] + got[z ^ step])
 
 
-def density_rows_kernel(layer, one, two, three, *refs):
-    encode_into(refs[-1], layer[...] + decode(one) + decode(two) + decode(three))
+def density_rows_kernel(here, one, two, three, *refs):
+    encode_into(refs[-1], decode(here) + decode(one) + decode(two) + decode(three))
 
 
 def density_block_kernel(far, near, *refs):
@@ -493,25 +491,19 @@
     def gamma_move(step, block):
         return move(block, lambda z, y, x, c: (z, c, x ^ (step >> 1), y ^ (step & 1)))
 
-    def across(value):
-        return move(value, lambda z, y, x, c: (z, 1 - c, 1 - x, y))
-
-    def along(value):
-        return move(value, lambda z, y, x, c: (z, 1 - c, x, y))
+    def to_rows(step, value):
+        return move(value, lambda z, y, x, c: (z ^ step, 1 - c, x, y))
 
     coded = shape(jnp.bfloat16, rows + TAIL_ROWS, virtuals)
     got_third = gamma_move(3, third)
-    layer, *messages = call(
+    messages = call(
         "density_cores",
         density_cores_kernel,
-        [shape(jnp.float32, rows, virtuals)] + [coded] * (layers - 1),
+        [coded] * layers,
         [dens_keep, dens_got],
         [third],
     )
-    got = [
-        move(messages[step - 1], lambda z, y, x, c, step=step: (z ^ step, y, x, c))
-        for step in range(layers - 1, 0, -1)
-    ]
+    got = [to_rows(step, messages[step]) for step in range(layers - 1, -1, -1)]
     second = gamma_block(2, messages[0])
     got_second = gamma_move(2, second)
     third_part = call(
@@ -527,10 +519,10 @@
         "density_rows",
         density_rows_kernel,
         coded,
-        [layer, *got],
+        got,
         [first_block],
     )
-    rows_far, rows_near = across(partial_rows), along(partial_rows)
+    rows_got = x_swap(partial_rows)
     zeroth = gamma_block(0, partial_rows)
     got_zeroth = gamma_move(0, zeroth)
     part = call(
@@ -544,7 +536,7 @@
         "density_block",
         density_block_kernel,
         shape(jnp.float32, rows, virtuals),
-        [rows_far, rows_near],
+        [partial_rows, rows_got],
         [part],
     )
     other = core_swap(block)

time: 61.7 us -> 61.3 us (level)
  waiting for transfers between devices: 9.75 us -> 8.21 us
  starting transfers between devices: 34.8 us -> 35.9 us
    ppermute x25, waiting for transfers between devices: 9.75 us -> 8.21 us  [send(): return lax.ppermute(value, AXES, pairs)]
    ppermute x25, starting transfers between devices: 34.8 us -> 35.9 us  [send(): return lax.ppermute(value, AXES, pairs)]
  transfers between devices with their start and end apart: 25 -> 25, of which waited for: 8 -> 7; matrix products, arithmetic and copies ran while one was open for 0% -> 0% of each run, Pallas kernels for 19% -> 19%
where the time goes in v8:
time: 61.3 us; the launch traced here: 61.1 us
  starting transfers between devices  35.9 us (59%)
  Pallas kernels  13.9 us (23%)
  waiting for transfers between devices  8.21 us (13%)
  local copies, waits for them, and re-layouts  2.2 us (4%)
  between operations  0.89 us (1%)
    ppermute x25, starting transfers between devices, send(): return lax.ppermute(value, AXES, pairs)  35.9 us
    pallas_call x16, Pallas kernels, call(): pl.pallas_call(kernel, in_specs=[vmem] * len(operands) + [unread] * len(e...  13.9 us
    ppermute x25, waiting for transfers between devices, send(): return lax.ppermute(value, AXES, pairs)  8.21 us
    unnamed x8, local copies, waits for them, and re-layouts  2.2 us
  transfers between devices with their start and end apart: 25, of which 7 were waited for; matrix products, arithmetic and copies ran while one was open for 0% of the time, Pallas kernels for 19%

profile of v8, /device:TPU:1, one launch (start us, length us, event | category | flops | bytes accessed | tf_op | source)
XLA Modules:
  0.0 61.1 jit_solution(6826788621635251416)
XLA Ops:
  0.6 2.1 %collective-permute-start = (bf16[512,256]{1,0:T(8,128)(2,1)}, bf16[512,256]{1,0:T(8,128)(2,1)S(1)}, u32[]{:S(2)}, u32[]{:S(2)}) collective-permute-start(bf16[512,256]{1,0:T(8,128)(2,1)} %bitcast.7), channel_id=1, source_target_pairs={{0,2},{1,3},{2,0},{3,1},{4,6},{5,7},{6,4},{7,5},{8,10},{9,11},{10,... | collective-permute-start | bytes 786440 | tf_op jit(solution)/shard_map/gather/ppermute | solution.py:148
  2.7 2.3 %collective-permute-start.1 = (bf16[512,256]{1,0:T(8,128)(2,1)}, bf16[512,256]{1,0:T(8,128)(2,1)S(1)}, u32[]{:S(2)}, u32[]{:S(2)}) collective-permute-start(bf16[512,256]{1,0:T(8,128)(2,1)} %bitcast.8), channel_id=1, source_target_pairs={{0,16},{1,17},{2,18},{3,19},{4,20},{5,21},{6,22},{7,23},{8,24},{9,... | collective-permute-start | bytes 786440 | tf_op jit(solution)/shard_map/gather/ppermute | solution.py:148
  5.0 3.2 %collective-permute-start.4 = (bf16[512,256]{1,0:T(8,128)(2,1)}, bf16[512,256]{1,0:T(8,128)(2,1)S(1)}, u32[]{:S(2)}, u32[]{:S(2)}) collective-permute-start(bf16[512,256]{1,0:T(8,128)(2,1)} %bitcast.9), channel_id=1, source_target_pairs={{0,8},{1,9},{2,2},{3,3},{4,12},{5,13},{6,6},{7,7},{8,0},{9,1},{10,... | collective-permute-start | bytes 786440 | tf_op jit(solution)/shard_map/gather/ppermute | solution.py:148
  8.3 1.5 %collective-permute-start.6 = (bf16[512,256]{1,0:T(8,128)(2,1)}, bf16[512,256]{1,0:T(8,128)(2,1)S(1)}, u32[]{:S(2)}, u32[]{:S(2)}) collective-permute-start(bf16[512,256]{1,0:T(8,128)(2,1)} %bitcast.11), channel_id=1, source_target_pairs={{0,4},{1,0},{2,6},{3,2},{4,5},{5,1},{6,7},{7,3},{8,12},{9,8},{10,1... | collective-permute-start | bytes 786440 | tf_op jit(solution)/shard_map/gather/ppermute | solution.py:148
  9.8 2.2 %copy-done = f32[1024,1024]{1,0:T(8,128)S(1)} copy-done((f32[1024,1024]{1,0:T(8,128)S(1)}, f32[1024,1024]{1,0:T(8,128)}, u32[]{:S(2)}) %copy-start) | copy-done | bytes 4194328
  12.0 1.3 %metric_turn.1 = (bf16[4,256,1024]{2,1,0:T(8,128)(2,1)S(1)}, bf16[4,256,1024]{2,1,0:T(8,128)(2,1)S(1)}) custom-call(f32[1024,1024]{1,0:T(8,128)S(1)} %copy-done), custom_call_target="tpu_custom_call" | custom-call | flops 1073741824 | tf_op jit(solution)/shard_map/metric_turn/pallas_call | solution.py:389
  13.4 3.0 %collective-permute-start.7 = (bf16[512,256]{1,0:T(8,128)(2,1)S(1)}, bf16[512,256]{1,0:T(8,128)(2,1)S(1)}, u32[]{:S(2)}, u32[]{:S(2)}) collective-permute-start(bf16[512,256]{1,0:T(8,128)(2,1)S(1)} %bitcast.12), channel_id=1, source_target_pairs={{0,0},{1,4},{2,2},{3,6},{4,1},{5,5},{6,3},{7,7},{8,8},{9,12},{10,1... | collective-permute-start | bytes 786440 | tf_op jit(solution)/shard_map/gather/ppermute | solution.py:148
  16.7 2.4 %collective-permute-start.2 = (bf16[512,256]{1,0:T(8,128)(2,1)S(1)}, bf16[512,256]{1,0:T(8,128)(2,1)S(1)}, u32[]{:S(2)}, u32[]{:S(2)}) collective-permute-start(bf16[512,256]{1,0:T(8,128)(2,1)S(1)} %collective-permute-done.1), channel_id=1, source_target_pairs={{0,10},{1,11},{2,0},{3,1},{4,14},{5,15},{6,4},{7,5},{8,2},{9,3},{1... | collective-permute-start | bytes 786440 | tf_op jit(solution)/shard_map/gather/ppermute | solution.py:148
  19.8 1.4 %collective-permute-done.5.refs_1_.refs_5_ = bf16[512,256]{1,0:T(8,128)(2,1)S(1)} collective-permute-done((bf16[512,256]{1,0:T(8,128)(2,1)}, bf16[512,256]{1,0:T(8,128)(2,1)S(1)}, u32[]{:S(2)}, u32[]{:S(2)}) %collective-permute-start.5) | collective-permute-done | bytes 262176 | tf_op jit(solution)/shard_map/gather/ppermute | solution.py:148
  21.1 1.5 %collective-permute-start.8 = (bf16[512,256]{1,0:T(8,128)(2,1)S(1)}, bf16[512,256]{1,0:T(8,128)(2,1)S(1)}, u32[]{:S(2)}, u32[]{:S(2)}) collective-permute-start(bf16[512,256]{1,0:T(8,128)(2,1)S(1)} %collective-permute-done.swapped), channel_id=1, source_target_pairs={{0,4},{1,0},{2,6},{3,2},{4,5},{5,1},{6,7},{7,3},{8,12},{9,8},{10,1... | collective-permute-start | bytes 786440 | tf_op jit(solution)/shard_map/gather/ppermute | solution.py:148
  22.7 3.1 %collective-permute-start.9 = (bf16[512,256]{1,0:T(8,128)(2,1)S(1)}, bf16[512,256]{1,0:T(8,128)(2,1)S(1)}, u32[]{:S(2)}, u32[]{:S(2)}) collective-permute-start(bf16[512,256]{1,0:T(8,128)(2,1)S(1)} %collective-permute-done.swapped), channel_id=1, source_target_pairs={{0,0},{1,4},{2,2},{3,6},{4,1},{5,5},{6,3},{7,7},{8,8},{9,12},{10,1... | collective-permute-start | bytes 786440 | tf_op jit(solution)/shard_map/gather/ppermute | solution.py:148
  25.8 1.9 %collective-permute-done.2.refs_3_.refs_1_ = bf16[512,256]{1,0:T(8,128)(2,1)S(1)} collective-permute-done((bf16[512,256]{1,0:T(8,128)(2,1)S(1)}, bf16[512,256]{1,0:T(8,128)(2,1)S(1)}, u32[]{:S(2)}, u32[]{:S(2)}) %collective-permute-start.2) | collective-permute-done | bytes 262176 | tf_op jit(solution)/shard_map/gather/ppermute | solution.py:148
  30.6 1.3 %first_pair.1 = (f32[512,1024]{1,0:T(8,128)S(1)}, bf16[512,512]{1,0:T(8,128)(2,1)S(1)}, bf16[512,512]{1,0:T(8,128)(2,1)S(1)}) custom-call(f32[1,8]{1,0:T(1,128)S(1)} %bitcast.5, f32[1,512]{1,0:T(1,128)S(1)} %bitcast.3, f32[512,512]{1,0:T(8,128)S(1)} %get-tuple-element.39.half, bf16[512,256]{1,0:T(8,128)(2,1)S(1)} %collective-permute-done.6.near.refs_0_, ...), custom_call_target="tpu_custom_call" | custom-call | tf_op jit(solution)/shard_map/first_pair/pallas_call | solution.py:389
  33.5 2.0 %gradient.1 = (bf16[512,1024]{1,0:T(8,128)(2,1)S(1)}, bf16[512,1024]{1,0:T(8,128)(2,1)S(1)}, bf16[272,512]{1,0:T(8,128)(2,1)S(1)}) custom-call(bf16[512,512]{1,0:T(8,128)(2,1)S(1)} %get-tuple-element.41.mixed.last_mixed, bf16[512,256]{1,0:T(8,128)(2,1)S(1)} %collective-permute-done.3.refs_2_.refs_0_, ...), custom_call_target="tpu_custom_call" | custom-call | flops 1610612736 | tf_op jit(solution)/shard_map/gradient/pallas_call | solution.py:389
  35.5 2.3 %collective-permute-start.14 = (bf16[272,512]{1,0:T(8,128)(2,1)S(1)}, bf16[272,512]{1,0:T(8,128)(2,1)S(1)}, u32[]{:S(2)}, u32[]{:S(2)}) collective-permute-start(bf16[272,512]{1,0:T(8,128)(2,1)S(1)} %get-tuple-element.45.refs_0_), channel_id=1, source_target_pairs={{0,3},{1,7},{2,1},{3,5},{4,2},{5,6},{6,0},{7,4},{8,11},{9,15},{10,... | collective-permute-start | bytes 835592 | tf_op jit(solution)/shard_map/ppermute | solution.py:148
  38.2 2.4 %collective-permute-start.17 = (bf16[80,512]{1,0:T(8,128)(2,1)S(1)}, bf16[80,512]{1,0:T(8,128)(2,1)S(1)}, u32[]{:S(2)}, u32[]{:S(2)}) collective-permute-start(bf16[80,512]{1,0:T(8,128)(2,1)S(1)} %get-tuple-element.53), channel_id=1, source_target_pairs={{0,28},{1,24},{2,30},{3,26},{4,29},{5,25},{6,31},{7,27},{8,20},{9,... | collective-permute-start | bytes 245768 | tf_op jit(solution)/shard_map/ppermute | solution.py:148
  40.6 1.8 %collective-permute-start.19 = (bf16[80,512]{1,0:T(8,128)(2,1)S(1)}, bf16[80,512]{1,0:T(8,128)(2,1)S(1)}, u32[]{:S(2)}, u32[]{:S(2)}) collective-permute-start(bf16[80,512]{1,0:T(8,128)(2,1)S(1)} %get-tuple-element.55), channel_id=1, source_target_pairs={{0,12},{1,8},{2,14},{3,10},{4,13},{5,9},{6,15},{7,11},{8,4},{9,0},... | collective-permute-start | bytes 245768 | tf_op jit(solution)/shard_map/ppermute | solution.py:148
  43.4 1.3 %gamma_block.3.refs_0_ = bf16[272,512]{1,0:T(8,128)(2,1)S(1)} custom-call(bf16[4,256,1024]{2,1,0:T(8,128)(2,1)S(1)} %get-tuple-element.43.refs_5_.metric_high, bf16[4,256,1024]{2,1,0:T(8,128)(2,1)S(1)} %get-tuple-element.44.refs_6_.metric_low, bf16[512,1024]{1,0:T(8,128)(2,1)S(1)} %get-tuple-element.46.high, bf16[512,1024]{1,0:T(8,128)(2,1)S(1)} %get-tuple-element.47.low, ...), custom_call_target="tpu_custom_call" | custom-call | flops 805306368 | tf_op jit(solution)/shard_map/gamma_block/pallas_call | solution.py:389
  44.7 1.9 %collective-permute-start.16 = (bf16[272,512]{1,0:T(8,128)(2,1)S(1)}, bf16[272,512]{1,0:T(8,128)(2,1)S(1)}, u32[]{:S(2)}, u32[]{:S(2)}) collective-permute-start(bf16[272,512]{1,0:T(8,128)(2,1)S(1)} %gamma_block.3.refs_0_), channel_id=1, source_target_pairs={{0,2},{1,6},{2,0},{3,4},{4,3},{5,7},{6,1},{7,5},{8,10},{9,14},{10,... | collective-permute-start | bytes 835592 | tf_op jit(solution)/shard_map/ppermute | solution.py:148
  46.8 1.3 %gamma_block.4.refs_0_ = bf16[272,512]{1,0:T(8,128)(2,1)S(1)} custom-call(bf16[4,256,1024]{2,1,0:T(8,128)(2,1)S(1)} %get-tuple-element.43.refs_5_.metric_high, bf16[4,256,1024]{2,1,0:T(8,128)(2,1)S(1)} %get-tuple-element.44.refs_6_.metric_low, bf16[512,1024]{1,0:T(8,128)(2,1)S(1)} %get-tuple-element.46.high, bf16[512,1024]{1,0:T(8,128)(2,1)S(1)} %get-tuple-element.47.low, ...), custom_call_target="tpu_custom_call" | custom-call | flops 805306368 | tf_op jit(solution)/shard_map/gamma_block/pallas_call | solution.py:389
  49.5 1.3 %gamma_block.5.refs_0_ = bf16[272,512]{1,0:T(8,128)(2,1)S(1)} custom-call(bf16[4,256,1024]{2,1,0:T(8,128)(2,1)S(1)} %get-tuple-element.43.refs_5_.metric_high, bf16[4,256,1024]{2,1,0:T(8,128)(2,1)S(1)} %get-tuple-element.44.refs_6_.metric_low, bf16[512,1024]{1,0:T(8,128)(2,1)S(1)} %get-tuple-element.46.high, bf16[512,1024]{1,0:T(8,128)(2,1)S(1)} %get-tuple-element.47.low, ...), custom_call_target="tpu_custom_call" | custom-call | flops 805306368 | tf_op jit(solution)/shard_map/gamma_block/pallas_call | solution.py:389
  50.8 3.6 %collective-permute-start.22 = (bf16[272,512]{1,0:T(8,128)(2,1)S(1)}, bf16[272,512]{1,0:T(8,128)(2,1)S(1)}, u32[]{:S(2)}, u32[]{:S(2)}) collective-permute-start(bf16[272,512]{1,0:T(8,128)(2,1)S(1)} %gamma_block.5.refs_0_), channel_id=1, source_target_pairs={{0,0},{1,4},{2,2},{3,6},{4,1},{5,5},{6,3},{7,7},{8,8},{9,12},{10,1... | collective-permute-start | bytes 835592 | tf_op jit(solution)/shard_map/ppermute | solution.py:148
  55.4 2.4 %collective-permute-done.23.near = bf16[80,512]{1,0:T(8,128)(2,1)S(1)} collective-permute-done((bf16[80,512]{1,0:T(8,128)(2,1)S(1)}, bf16[80,512]{1,0:T(8,128)(2,1)S(1)}, u32[]{:S(2)}, u32[]{:S(2)}) %collective-permute-start.23) | collective-permute-done | bytes 81952 | tf_op jit(solution)/shard_map/ppermute | solution.py:148
  59.2 1.2 %gamma_sum.1 = f32[256,1,512]{2,1,0:T(1,128)} custom-call(f32[256,512]{1,0:T(8,128)S(1)} %gamma_part.1.refs_0_.part, bf16[272,512]{1,0:T(8,128)(2,1)S(1)} %collective-permute-done.21.left, bf16[272,512]{1,0:T(8,128)(2,1)S(1)} %collective-permute-done.22.right, f32[64,512]{1,0:T(8,128)S(1)} %density_block.1.refs_0_.block), custom_call_target="tpu_custom_call" | custom-call | tf_op jit(solution)/shard_map/gamma_sum/pallas_call | solution.py:389
  (50 shorter events, 11.2 us)
Async XLA Ops:
  0.6 12.7 %collective-permute-start = (bf16[512,256]{1,0:T(8,128)(2,1)}, bf16[512,256]{1,0:T(8,128)(2,1)S(1)}, u32[]{:S(2)}, u32[]{:S(2)}) collective-permute-start(bf16[512,256]{1,0:T(8,128)(2,1)} %bitcast.7), channel_id=1, source_target_pairs={{0,2},{1,3},{2,0},{3,1},{4,6},{5,7},{6,4},{7,5},{8,10},{9,11},{10,... | collective-permute-start | bytes 786440 | tf_op jit(solution)/shard_map/gather/ppermute | solution.py:148
  2.7 13.9 %collective-permute-start.1 = (bf16[512,256]{1,0:T(8,128)(2,1)}, bf16[512,256]{1,0:T(8,128)(2,1)S(1)}, u32[]{:S(2)}, u32[]{:S(2)}) collective-permute-start(bf16[512,256]{1,0:T(8,128)(2,1)} %bitcast.8), channel_id=1, source_target_pairs={{0,16},{1,17},{2,18},{3,19},{4,20},{5,21},{6,22},{7,23},{8,24},{9,... | collective-permute-start | bytes 786440 | tf_op jit(solution)/shard_map/gather/ppermute | solution.py:148
  5.0 14.1 %collective-permute-start.4 = (bf16[512,256]{1,0:T(8,128)(2,1)}, bf16[512,256]{1,0:T(8,128)(2,1)S(1)}, u32[]{:S(2)}, u32[]{:S(2)}) collective-permute-start(bf16[512,256]{1,0:T(8,128)(2,1)} %bitcast.9), channel_id=1, source_target_pairs={{0,8},{1,9},{2,2},{3,3},{4,12},{5,13},{6,6},{7,7},{8,0},{9,1},{10,... | collective-permute-start | bytes 786440 | tf_op jit(solution)/shard_map/gather/ppermute | solution.py:148
  8.2 12.9 %collective-permute-start.5 = (bf16[512,256]{1,0:T(8,128)(2,1)}, bf16[512,256]{1,0:T(8,128)(2,1)S(1)}, u32[]{:S(2)}, u32[]{:S(2)}) collective-permute-start(bf16[512,256]{1,0:T(8,128)(2,1)} %bitcast.10), channel_id=1, source_target_pairs={{0,2},{1,3},{2,8},{3,9},{4,6},{5,7},{6,12},{7,13},{8,10},{9,11},{1... | collective-permute-start | bytes 786440 | tf_op jit(solution)/shard_map/gather/ppermute | solution.py:148
  8.3 14.4 %collective-permute-start.6 = (bf16[512,256]{1,0:T(8,128)(2,1)}, bf16[512,256]{1,0:T(8,128)(2,1)S(1)}, u32[]{:S(2)}, u32[]{:S(2)}) collective-permute-start(bf16[512,256]{1,0:T(8,128)(2,1)} %bitcast.11), channel_id=1, source_target_pairs={{0,4},{1,0},{2,6},{3,2},{4,5},{5,1},{6,7},{7,3},{8,12},{9,8},{10,1... | collective-permute-start | bytes 786440 | tf_op jit(solution)/shard_map/gather/ppermute | solution.py:148
  13.4 12.4 %collective-permute-start.7 = (bf16[512,256]{1,0:T(8,128)(2,1)S(1)}, bf16[512,256]{1,0:T(8,128)(2,1)S(1)}, u32[]{:S(2)}, u32[]{:S(2)}) collective-permute-start(bf16[512,256]{1,0:T(8,128)(2,1)S(1)} %bitcast.12), channel_id=1, source_target_pairs={{0,0},{1,4},{2,2},{3,6},{4,1},{5,5},{6,3},{7,7},{8,8},{9,12},{10,1... | collective-permute-start | bytes 786440 | tf_op jit(solution)/shard_map/gather/ppermute | solution.py:148
  16.7 11.0 %collective-permute-start.2 = (bf16[512,256]{1,0:T(8,128)(2,1)S(1)}, bf16[512,256]{1,0:T(8,128)(2,1)S(1)}, u32[]{:S(2)}, u32[]{:S(2)}) collective-permute-start(bf16[512,256]{1,0:T(8,128)(2,1)S(1)} %collective-permute-done.1), channel_id=1, source_target_pairs={{0,10},{1,11},{2,0},{3,1},{4,14},{5,15},{6,4},{7,5},{8,2},{9,3},{1... | collective-permute-start | bytes 786440 | tf_op jit(solution)/shard_map/gather/ppermute | solution.py:148
  19.1 8.6 %collective-permute-start.3 = (bf16[512,256]{1,0:T(8,128)(2,1)S(1)}, bf16[512,256]{1,0:T(8,128)(2,1)S(1)}, u32[]{:S(2)}, u32[]{:S(2)}) collective-permute-start(bf16[512,256]{1,0:T(8,128)(2,1)S(1)} %collective-permute-done.1), channel_id=1, source_target_pairs={{0,0},{1,1},{2,10},{3,11},{4,4},{5,5},{6,14},{7,15},{8,8},{9,9},{1... | collective-permute-start | bytes 786440 | tf_op jit(solution)/shard_map/gather/ppermute | solution.py:148
  21.1 7.6 %collective-permute-start.8 = (bf16[512,256]{1,0:T(8,128)(2,1)S(1)}, bf16[512,256]{1,0:T(8,128)(2,1)S(1)}, u32[]{:S(2)}, u32[]{:S(2)}) collective-permute-start(bf16[512,256]{1,0:T(8,128)(2,1)S(1)} %collective-permute-done.swapped), channel_id=1, source_target_pairs={{0,4},{1,0},{2,6},{3,2},{4,5},{5,1},{6,7},{7,3},{8,12},{9,8},{10,1... | collective-permute-start | bytes 786440 | tf_op jit(solution)/shard_map/gather/ppermute | solution.py:148
  22.7 7.9 %collective-permute-start.9 = (bf16[512,256]{1,0:T(8,128)(2,1)S(1)}, bf16[512,256]{1,0:T(8,128)(2,1)S(1)}, u32[]{:S(2)}, u32[]{:S(2)}) collective-permute-start(bf16[512,256]{1,0:T(8,128)(2,1)S(1)} %collective-permute-done.swapped), channel_id=1, source_target_pairs={{0,0},{1,4},{2,2},{3,6},{4,1},{5,5},{6,3},{7,7},{8,8},{9,12},{10,1... | collective-permute-start | bytes 786440 | tf_op jit(solution)/shard_map/gather/ppermute | solution.py:148
  27.7 2.8 %collective-permute-start.12 = (bf16[512,256]{1,0:T(8,128)(2,1)S(1)}, bf16[512,256]{1,0:T(8,128)(2,1)S(1)}, u32[]{:S(2)}, u32[]{:S(2)}) collective-permute-start(bf16[512,256]{1,0:T(8,128)(2,1)S(1)} %collective-permute-done.4.refs_0_.refs_4_), channel_id=1, source_target_pairs={{0,1},{1,0},{2,3},{3,2},{4,5},{5,4},{6,7},{7,6},{8,9},{9,8},{10,11... | collective-permute-start | bytes 786440 | tf_op jit(solution)/shard_map/gather/ppermute | solution.py:148
  28.2 3.7 %collective-permute-start.10 = (bf16[512,256]{1,0:T(8,128)(2,1)S(1)}, bf16[512,256]{1,0:T(8,128)(2,1)S(1)}, u32[]{:S(2)}, u32[]{:S(2)}) collective-permute-start(bf16[512,256]{1,0:T(8,128)(2,1)S(1)} %collective-permute-done.3.refs_2_.refs_0_), channel_id=1, source_target_pairs={{0,1},{1,0},{2,3},{3,2},{4,5},{5,4},{6,7},{7,6},{8,9},{9,8},{10,11... | collective-permute-start | bytes 786440 | tf_op jit(solution)/shard_map/gather/ppermute | solution.py:148
  28.7 3.2 %collective-permute-start.11 = (bf16[512,256]{1,0:T(8,128)(2,1)S(1)}, bf16[512,256]{1,0:T(8,128)(2,1)S(1)}, u32[]{:S(2)}, u32[]{:S(2)}) collective-permute-start(bf16[512,256]{1,0:T(8,128)(2,1)S(1)} %collective-permute-done.2.refs_3_.refs_1_), channel_id=1, source_target_pairs={{0,1},{1,0},{2,3},{3,2},{4,5},{5,4},{6,7},{7,6},{8,9},{9,8},{10,11... | collective-permute-start | bytes 786440 | tf_op jit(solution)/shard_map/gather/ppermute | solution.py:148
  33.4 4.4 %collective-permute-start.15 = (f32[4,64,512]{2,1,0:T(8,128)S(1)}, f32[4,64,512]{2,1,0:T(8,128)S(1)}, u32[]{:S(2)}, u32[]{:S(2)}) collective-permute-start(f32[4,64,512]{2,1,0:T(8,128)S(1)} %get-tuple-element.51), channel_id=1, source_target_pairs={{0,1},{1,0},{2,3},{3,2},{4,5},{5,4},{6,7},{7,6},{8,9},{9,8},{10,11... | collective-permute-start | bytes 1572872 | tf_op jit(solution)/shard_map/ppermute | solution.py:148
  35.5 9.2 %collective-permute-start.14 = (bf16[272,512]{1,0:T(8,128)(2,1)S(1)}, bf16[272,512]{1,0:T(8,128)(2,1)S(1)}, u32[]{:S(2)}, u32[]{:S(2)}) collective-permute-start(bf16[272,512]{1,0:T(8,128)(2,1)S(1)} %get-tuple-element.45.refs_0_), channel_id=1, source_target_pairs={{0,3},{1,7},{2,1},{3,5},{4,2},{5,6},{6,0},{7,4},{8,11},{9,15},{10,... | collective-permute-start | bytes 835592 | tf_op jit(solution)/shard_map/ppermute | solution.py:148
  38.2 10.0 %collective-permute-start.17 = (bf16[80,512]{1,0:T(8,128)(2,1)S(1)}, bf16[80,512]{1,0:T(8,128)(2,1)S(1)}, u32[]{:S(2)}, u32[]{:S(2)}) collective-permute-start(bf16[80,512]{1,0:T(8,128)(2,1)S(1)} %get-tuple-element.53), channel_id=1, source_target_pairs={{0,28},{1,24},{2,30},{3,26},{4,29},{5,25},{6,31},{7,27},{8,20},{9,... | collective-permute-start | bytes 245768 | tf_op jit(solution)/shard_map/ppermute | solution.py:148
  40.6 8.5 %collective-permute-start.18 = (bf16[80,512]{1,0:T(8,128)(2,1)S(1)}, bf16[80,512]{1,0:T(8,128)(2,1)S(1)}, u32[]{:S(2)}, u32[]{:S(2)}) collective-permute-start(bf16[80,512]{1,0:T(8,128)(2,1)S(1)} %get-tuple-element.54), channel_id=1, source_target_pairs={{0,20},{1,16},{2,22},{3,18},{4,21},{5,17},{6,23},{7,19},{8,28},{9,... | collective-permute-start | bytes 245768 | tf_op jit(solution)/shard_map/ppermute | solution.py:148
  40.6 8.5 %collective-permute-start.19 = (bf16[80,512]{1,0:T(8,128)(2,1)S(1)}, bf16[80,512]{1,0:T(8,128)(2,1)S(1)}, u32[]{:S(2)}, u32[]{:S(2)}) collective-permute-start(bf16[80,512]{1,0:T(8,128)(2,1)S(1)} %get-tuple-element.55), channel_id=1, source_target_pairs={{0,12},{1,8},{2,14},{3,10},{4,13},{5,9},{6,15},{7,11},{8,4},{9,0},... | collective-permute-start | bytes 245768 | tf_op jit(solution)/shard_map/ppermute | solution.py:148
  42.4 6.7 %collective-permute-start.20 = (bf16[80,512]{1,0:T(8,128)(2,1)S(1)}, bf16[80,512]{1,0:T(8,128)(2,1)S(1)}, u32[]{:S(2)}, u32[]{:S(2)}) collective-permute-start(bf16[80,512]{1,0:T(8,128)(2,1)S(1)} %get-tuple-element.52.refs_0_), channel_id=1, source_target_pairs={{0,4},{1,0},{2,6},{3,2},{4,5},{5,1},{6,7},{7,3},{8,12},{9,8},{10,1... | collective-permute-start | bytes 245768 | tf_op jit(solution)/shard_map/ppermute | solution.py:148
  44.7 10.4 %collective-permute-start.16 = (bf16[272,512]{1,0:T(8,128)(2,1)S(1)}, bf16[272,512]{1,0:T(8,128)(2,1)S(1)}, u32[]{:S(2)}, u32[]{:S(2)}) collective-permute-start(bf16[272,512]{1,0:T(8,128)(2,1)S(1)} %gamma_block.3.refs_0_), channel_id=1, source_target_pairs={{0,2},{1,6},{2,0},{3,4},{4,3},{5,7},{6,1},{7,5},{8,10},{9,14},{10,... | collective-permute-start | bytes 835592 | tf_op jit(solution)/shard_map/ppermute | solution.py:148
  48.2 9.8 %collective-permute-start.21 = (bf16[272,512]{1,0:T(8,128)(2,1)S(1)}, bf16[272,512]{1,0:T(8,128)(2,1)S(1)}, u32[]{:S(2)}, u32[]{:S(2)}) collective-permute-start(bf16[272,512]{1,0:T(8,128)(2,1)S(1)} %gamma_block.4.refs_0_), channel_id=1, source_target_pairs={{0,1},{1,5},{2,3},{3,7},{4,0},{5,4},{6,2},{7,6},{8,9},{9,13},{10,1... | collective-permute-start | bytes 835592 | tf_op jit(solution)/shard_map/ppermute | solution.py:148
  50.8 8.3 %collective-permute-start.22 = (bf16[272,512]{1,0:T(8,128)(2,1)S(1)}, bf16[272,512]{1,0:T(8,128)(2,1)S(1)}, u32[]{:S(2)}, u32[]{:S(2)}) collective-permute-start(bf16[272,512]{1,0:T(8,128)(2,1)S(1)} %gamma_block.5.refs_0_), channel_id=1, source_target_pairs={{0,0},{1,4},{2,2},{3,6},{4,1},{5,5},{6,3},{7,7},{8,8},{9,12},{10,1... | collective-permute-start | bytes 835592 | tf_op jit(solution)/shard_map/ppermute | solution.py:148
  54.4 3.4 %collective-permute-start.23 = (bf16[80,512]{1,0:T(8,128)(2,1)S(1)}, bf16[80,512]{1,0:T(8,128)(2,1)S(1)}, u32[]{:S(2)}, u32[]{:S(2)}) collective-permute-start(bf16[80,512]{1,0:T(8,128)(2,1)S(1)} %density_rows.1.refs_0_.refs_1_.far), channel_id=1, source_target_pairs={{0,2},{1,3},{2,0},{3,1},{4,6},{5,7},{6,4},{7,5},{8,10},{9,11},{10,... | collective-permute-start | bytes 245768 | tf_op jit(solution)/shard_map/ppermute | solution.py:148
  57.9 2.5 %collective-permute-start.24 = (f32[64,512]{1,0:T(8,128)S(1)}, f32[64,512]{1,0:T(8,128)S(1)}, u32[]{:S(2)}, u32[]{:S(2)}) collective-permute-start(f32[64,512]{1,0:T(8,128)S(1)} %density_block.1.refs_0_.block), channel_id=1, source_target_pairs={{0,1},{1,0},{2,3},{3,2},{4,5},{5,4},{6,7},{7,6},{8,9},{9,8},{10,11... | collective-permute-start | bytes 393224 | tf_op jit(solution)/shard_map/ppermute | solution.py:148
  (5 other events, 40.3 us)

commit v9 on v8

--- a/solution.py
+++ b/solution.py
@@ -154,9 +154,7 @@
     power = jnp.clip(power, -120.0, 120.0)
     scaled = value * jnp.exp2(power)
     second = scaled * scaled
-    fourth = second * second
-    eighth = fourth * fourth
-    coded = jnp.where(scaled < 0.0, -eighth, eighth).astype(jnp.bfloat16)
+    coded = ((second * second) * (second * scaled)).astype(jnp.bfloat16)
     tail = jnp.broadcast_to(power, (TAIL_ROWS, value.shape[1])).astype(jnp.bfloat16)
     return coded, tail
 
@@ -172,7 +170,7 @@
     rows = ref.shape[0] - TAIL_ROWS
     power = ref[rows:].astype(jnp.float32)[:1]
     coded = ref[:rows].astype(jnp.float32)
-    root = jnp.exp2(jnp.log2(jnp.abs(coded)) * 0.125 - power)
+    root = jnp.exp2(jnp.log2(jnp.abs(coded)) * (1.0 / 7.0) - power)
     return jnp.where(coded < 0.0, -root, root)
 
 

time: 61.3 us -> 61.3 us (level)
  no operation moved by 1% of the time
where the time goes in v9:
time: 61.3 us; the launch traced here: 61 us
  starting transfers between devices  36 us (59%)
  Pallas kernels  13.8 us (23%)
  waiting for transfers between devices  8.11 us (13%)
  local copies, waits for them, and re-layouts  2.2 us (4%)
  between operations  0.89 us (1%)
    ppermute x25, starting transfers between devices, send(): return lax.ppermute(value, AXES, pairs)  36 us
    pallas_call x16, Pallas kernels, call(): pl.pallas_call(kernel, in_specs=[vmem] * len(operands) + [unread] * len(e...  13.8 us
    ppermute x25, waiting for transfers between devices, send(): return lax.ppermute(value, AXES, pairs)  8.11 us
    unnamed x8, local copies, waits for them, and re-layouts  2.2 us
  transfers between devices with their start and end apart: 25, of which 7 were waited for; matrix products, arithmetic and copies ran while one was open for 0% of the time, Pallas kernels for 19%

profile of v9, /device:TPU:1, one launch (start us, length us, event | category | flops | bytes accessed | tf_op | source)
XLA Modules:
  0.0 61.0 jit_solution(12129949642351979238)
XLA Ops:
  0.6 2.1 %collective-permute-start = (bf16[512,256]{1,0:T(8,128)(2,1)}, bf16[512,256]{1,0:T(8,128)(2,1)S(1)}, u32[]{:S(2)}, u32[]{:S(2)}) collective-permute-start(bf16[512,256]{1,0:T(8,128)(2,1)} %bitcast.7), channel_id=1, source_target_pairs={{0,2},{1,3},{2,0},{3,1},{4,6},{5,7},{6,4},{7,5},{8,10},{9,11},{10,... | collective-permute-start | bytes 786440 | tf_op jit(solution)/shard_map/gather/ppermute | solution.py:148
  2.7 2.3 %collective-permute-start.1 = (bf16[512,256]{1,0:T(8,128)(2,1)}, bf16[512,256]{1,0:T(8,128)(2,1)S(1)}, u32[]{:S(2)}, u32[]{:S(2)}) collective-permute-start(bf16[512,256]{1,0:T(8,128)(2,1)} %bitcast.8), channel_id=1, source_target_pairs={{0,16},{1,17},{2,18},{3,19},{4,20},{5,21},{6,22},{7,23},{8,24},{9,... | collective-permute-start | bytes 786440 | tf_op jit(solution)/shard_map/gather/ppermute | solution.py:148
  5.0 3.2 %collective-permute-start.4 = (bf16[512,256]{1,0:T(8,128)(2,1)}, bf16[512,256]{1,0:T(8,128)(2,1)S(1)}, u32[]{:S(2)}, u32[]{:S(2)}) collective-permute-start(bf16[512,256]{1,0:T(8,128)(2,1)} %bitcast.9), channel_id=1, source_target_pairs={{0,8},{1,9},{2,2},{3,3},{4,12},{5,13},{6,6},{7,7},{8,0},{9,1},{10,... | collective-permute-start | bytes 786440 | tf_op jit(solution)/shard_map/gather/ppermute | solution.py:148
  8.3 1.5 %collective-permute-start.6 = (bf16[512,256]{1,0:T(8,128)(2,1)}, bf16[512,256]{1,0:T(8,128)(2,1)S(1)}, u32[]{:S(2)}, u32[]{:S(2)}) collective-permute-start(bf16[512,256]{1,0:T(8,128)(2,1)} %bitcast.11), channel_id=1, source_target_pairs={{0,4},{1,0},{2,6},{3,2},{4,5},{5,1},{6,7},{7,3},{8,12},{9,8},{10,1... | collective-permute-start | bytes 786440 | tf_op jit(solution)/shard_map/gather/ppermute | solution.py:148
  9.8 2.2 %copy-done = f32[1024,1024]{1,0:T(8,128)S(1)} copy-done((f32[1024,1024]{1,0:T(8,128)S(1)}, f32[1024,1024]{1,0:T(8,128)}, u32[]{:S(2)}) %copy-start) | copy-done | bytes 4194328
  12.0 1.3 %metric_turn.1 = (bf16[4,256,1024]{2,1,0:T(8,128)(2,1)S(1)}, bf16[4,256,1024]{2,1,0:T(8,128)(2,1)S(1)}) custom-call(f32[1024,1024]{1,0:T(8,128)S(1)} %copy-done), custom_call_target="tpu_custom_call" | custom-call | flops 1073741824 | tf_op jit(solution)/shard_map/metric_turn/pallas_call | solution.py:387
  13.4 3.0 %collective-permute-start.7 = (bf16[512,256]{1,0:T(8,128)(2,1)S(1)}, bf16[512,256]{1,0:T(8,128)(2,1)S(1)}, u32[]{:S(2)}, u32[]{:S(2)}) collective-permute-start(bf16[512,256]{1,0:T(8,128)(2,1)S(1)} %bitcast.12), channel_id=1, source_target_pairs={{0,0},{1,4},{2,2},{3,6},{4,1},{5,5},{6,3},{7,7},{8,8},{9,12},{10,1... | collective-permute-start | bytes 786440 | tf_op jit(solution)/shard_map/gather/ppermute | solution.py:148
  16.7 2.4 %collective-permute-start.2 = (bf16[512,256]{1,0:T(8,128)(2,1)S(1)}, bf16[512,256]{1,0:T(8,128)(2,1)S(1)}, u32[]{:S(2)}, u32[]{:S(2)}) collective-permute-start(bf16[512,256]{1,0:T(8,128)(2,1)S(1)} %collective-permute-done.1), channel_id=1, source_target_pairs={{0,10},{1,11},{2,0},{3,1},{4,14},{5,15},{6,4},{7,5},{8,2},{9,3},{1... | collective-permute-start | bytes 786440 | tf_op jit(solution)/shard_map/gather/ppermute | solution.py:148
  19.8 1.4 %collective-permute-done.5.refs_1_.refs_5_ = bf16[512,256]{1,0:T(8,128)(2,1)S(1)} collective-permute-done((bf16[512,256]{1,0:T(8,128)(2,1)}, bf16[512,256]{1,0:T(8,128)(2,1)S(1)}, u32[]{:S(2)}, u32[]{:S(2)}) %collective-permute-start.5) | collective-permute-done | bytes 262176 | tf_op jit(solution)/shard_map/gather/ppermute | solution.py:148
  21.1 1.5 %collective-permute-start.8 = (bf16[512,256]{1,0:T(8,128)(2,1)S(1)}, bf16[512,256]{1,0:T(8,128)(2,1)S(1)}, u32[]{:S(2)}, u32[]{:S(2)}) collective-permute-start(bf16[512,256]{1,0:T(8,128)(2,1)S(1)} %collective-permute-done.swapped), channel_id=1, source_target_pairs={{0,4},{1,0},{2,6},{3,2},{4,5},{5,1},{6,7},{7,3},{8,12},{9,8},{10,1... | collective-permute-start | bytes 786440 | tf_op jit(solution)/shard_map/gather/ppermute | solution.py:148
  22.7 3.1 %collective-permute-start.9 = (bf16[512,256]{1,0:T(8,128)(2,1)S(1)}, bf16[512,256]{1,0:T(8,128)(2,1)S(1)}, u32[]{:S(2)}, u32[]{:S(2)}) collective-permute-start(bf16[512,256]{1,0:T(8,128)(2,1)S(1)} %collective-permute-done.swapped), channel_id=1, source_target_pairs={{0,0},{1,4},{2,2},{3,6},{4,1},{5,5},{6,3},{7,7},{8,8},{9,12},{10,1... | collective-permute-start | bytes 786440 | tf_op jit(solution)/shard_map/gather/ppermute | solution.py:148
  25.8 1.9 %collective-permute-done.2.refs_3_.refs_1_ = bf16[512,256]{1,0:T(8,128)(2,1)S(1)} collective-permute-done((bf16[512,256]{1,0:T(8,128)(2,1)S(1)}, bf16[512,256]{1,0:T(8,128)(2,1)S(1)}, u32[]{:S(2)}, u32[]{:S(2)}) %collective-permute-start.2) | collective-permute-done | bytes 262176 | tf_op jit(solution)/shard_map/gather/ppermute | solution.py:148
  30.6 1.3 %first_pair.1 = (f32[512,1024]{1,0:T(8,128)S(1)}, bf16[512,512]{1,0:T(8,128)(2,1)S(1)}, bf16[512,512]{1,0:T(8,128)(2,1)S(1)}) custom-call(f32[1,8]{1,0:T(1,128)S(1)} %bitcast.5, f32[1,512]{1,0:T(1,128)S(1)} %bitcast.3, f32[512,512]{1,0:T(8,128)S(1)} %get-tuple-element.39.half, bf16[512,256]{1,0:T(8,128)(2,1)S(1)} %collective-permute-done.6.near.refs_0_, ...), custom_call_target="tpu_custom_call" | custom-call | tf_op jit(solution)/shard_map/first_pair/pallas_call | solution.py:387
  33.5 2.0 %gradient.1 = (bf16[512,1024]{1,0:T(8,128)(2,1)S(1)}, bf16[512,1024]{1,0:T(8,128)(2,1)S(1)}, bf16[272,512]{1,0:T(8,128)(2,1)S(1)}) custom-call(bf16[512,512]{1,0:T(8,128)(2,1)S(1)} %get-tuple-element.41.mixed.last_mixed, bf16[512,256]{1,0:T(8,128)(2,1)S(1)} %collective-permute-done.3.refs_2_.refs_0_, ...), custom_call_target="tpu_custom_call" | custom-call | flops 1610612736 | tf_op jit(solution)/shard_map/gradient/pallas_call | solution.py:387
  35.5 2.3 %collective-permute-start.14 = (bf16[272,512]{1,0:T(8,128)(2,1)S(1)}, bf16[272,512]{1,0:T(8,128)(2,1)S(1)}, u32[]{:S(2)}, u32[]{:S(2)}) collective-permute-start(bf16[272,512]{1,0:T(8,128)(2,1)S(1)} %get-tuple-element.45.refs_0_), channel_id=1, source_target_pairs={{0,3},{1,7},{2,1},{3,5},{4,2},{5,6},{6,0},{7,4},{8,11},{9,15},{10,... | collective-permute-start | bytes 835592 | tf_op jit(solution)/shard_map/ppermute | solution.py:148
  38.1 2.4 %collective-permute-start.17 = (bf16[80,512]{1,0:T(8,128)(2,1)S(1)}, bf16[80,512]{1,0:T(8,128)(2,1)S(1)}, u32[]{:S(2)}, u32[]{:S(2)}) collective-permute-start(bf16[80,512]{1,0:T(8,128)(2,1)S(1)} %get-tuple-element.53), channel_id=1, source_target_pairs={{0,28},{1,24},{2,30},{3,26},{4,29},{5,25},{6,31},{7,27},{8,20},{9,... | collective-permute-start | bytes 245768 | tf_op jit(solution)/shard_map/ppermute | solution.py:148
  40.6 1.8 %collective-permute-start.19 = (bf16[80,512]{1,0:T(8,128)(2,1)S(1)}, bf16[80,512]{1,0:T(8,128)(2,1)S(1)}, u32[]{:S(2)}, u32[]{:S(2)}) collective-permute-start(bf16[80,512]{1,0:T(8,128)(2,1)S(1)} %get-tuple-element.55), channel_id=1, source_target_pairs={{0,12},{1,8},{2,14},{3,10},{4,13},{5,9},{6,15},{7,11},{8,4},{9,0},... | collective-permute-start | bytes 245768 | tf_op jit(solution)/shard_map/ppermute | solution.py:148
  43.3 1.3 %gamma_block.3.refs_0_ = bf16[272,512]{1,0:T(8,128)(2,1)S(1)} custom-call(bf16[4,256,1024]{2,1,0:T(8,128)(2,1)S(1)} %get-tuple-element.43.refs_5_.metric_high, bf16[4,256,1024]{2,1,0:T(8,128)(2,1)S(1)} %get-tuple-element.44.refs_6_.metric_low, bf16[512,1024]{1,0:T(8,128)(2,1)S(1)} %get-tuple-element.46.high, bf16[512,1024]{1,0:T(8,128)(2,1)S(1)} %get-tuple-element.47.low, ...), custom_call_target="tpu_custom_call" | custom-call | flops 805306368 | tf_op jit(solution)/shard_map/gamma_block/pallas_call | solution.py:387
  44.7 2.0 %collective-permute-start.16 = (bf16[272,512]{1,0:T(8,128)(2,1)S(1)}, bf16[272,512]{1,0:T(8,128)(2,1)S(1)}, u32[]{:S(2)}, u32[]{:S(2)}) collective-permute-start(bf16[272,512]{1,0:T(8,128)(2,1)S(1)} %gamma_block.3.refs_0_), channel_id=1, source_target_pairs={{0,2},{1,6},{2,0},{3,4},{4,3},{5,7},{6,1},{7,5},{8,10},{9,14},{10,... | collective-permute-start | bytes 835592 | tf_op jit(solution)/shard_map/ppermute | solution.py:148
  46.8 1.3 %gamma_block.4.refs_0_ = bf16[272,512]{1,0:T(8,128)(2,1)S(1)} custom-call(bf16[4,256,1024]{2,1,0:T(8,128)(2,1)S(1)} %get-tuple-element.43.refs_5_.metric_high, bf16[4,256,1024]{2,1,0:T(8,128)(2,1)S(1)} %get-tuple-element.44.refs_6_.metric_low, bf16[512,1024]{1,0:T(8,128)(2,1)S(1)} %get-tuple-element.46.high, bf16[512,1024]{1,0:T(8,128)(2,1)S(1)} %get-tuple-element.47.low, ...), custom_call_target="tpu_custom_call" | custom-call | flops 805306368 | tf_op jit(solution)/shard_map/gamma_block/pallas_call | solution.py:387
  49.5 1.3 %gamma_block.5.refs_0_ = bf16[272,512]{1,0:T(8,128)(2,1)S(1)} custom-call(bf16[4,256,1024]{2,1,0:T(8,128)(2,1)S(1)} %get-tuple-element.43.refs_5_.metric_high, bf16[4,256,1024]{2,1,0:T(8,128)(2,1)S(1)} %get-tuple-element.44.refs_6_.metric_low, bf16[512,1024]{1,0:T(8,128)(2,1)S(1)} %get-tuple-element.46.high, bf16[512,1024]{1,0:T(8,128)(2,1)S(1)} %get-tuple-element.47.low, ...), custom_call_target="tpu_custom_call" | custom-call | flops 805306368 | tf_op jit(solution)/shard_map/gamma_block/pallas_call | solution.py:387
  50.8 3.6 %collective-permute-start.22 = (bf16[272,512]{1,0:T(8,128)(2,1)S(1)}, bf16[272,512]{1,0:T(8,128)(2,1)S(1)}, u32[]{:S(2)}, u32[]{:S(2)}) collective-permute-start(bf16[272,512]{1,0:T(8,128)(2,1)S(1)} %gamma_block.5.refs_0_), channel_id=1, source_target_pairs={{0,0},{1,4},{2,2},{3,6},{4,1},{5,5},{6,3},{7,7},{8,8},{9,12},{10,1... | collective-permute-start | bytes 835592 | tf_op jit(solution)/shard_map/ppermute | solution.py:148
  55.3 2.4 %collective-permute-done.23.near = bf16[80,512]{1,0:T(8,128)(2,1)S(1)} collective-permute-done((bf16[80,512]{1,0:T(8,128)(2,1)S(1)}, bf16[80,512]{1,0:T(8,128)(2,1)S(1)}, u32[]{:S(2)}, u32[]{:S(2)}) %collective-permute-start.23) | collective-permute-done | bytes 81952 | tf_op jit(solution)/shard_map/ppermute | solution.py:148
  59.1 1.2 %gamma_sum.1 = f32[256,1,512]{2,1,0:T(1,128)} custom-call(f32[256,512]{1,0:T(8,128)S(1)} %gamma_part.1.refs_0_.part, bf16[272,512]{1,0:T(8,128)(2,1)S(1)} %collective-permute-done.21.left, bf16[272,512]{1,0:T(8,128)(2,1)S(1)} %collective-permute-done.22.right, f32[64,512]{1,0:T(8,128)S(1)} %density_block.1.refs_0_.block), custom_call_target="tpu_custom_call" | custom-call | tf_op jit(solution)/shard_map/gamma_sum/pallas_call | solution.py:387
  (50 shorter events, 11.1 us)
Async XLA Ops:
  0.6 12.7 %collective-permute-start = (bf16[512,256]{1,0:T(8,128)(2,1)}, bf16[512,256]{1,0:T(8,128)(2,1)S(1)}, u32[]{:S(2)}, u32[]{:S(2)}) collective-permute-start(bf16[512,256]{1,0:T(8,128)(2,1)} %bitcast.7), channel_id=1, source_target_pairs={{0,2},{1,3},{2,0},{3,1},{4,6},{5,7},{6,4},{7,5},{8,10},{9,11},{10,... | collective-permute-start | bytes 786440 | tf_op jit(solution)/shard_map/gather/ppermute | solution.py:148
  2.7 13.9 %collective-permute-start.1 = (bf16[512,256]{1,0:T(8,128)(2,1)}, bf16[512,256]{1,0:T(8,128)(2,1)S(1)}, u32[]{:S(2)}, u32[]{:S(2)}) collective-permute-start(bf16[512,256]{1,0:T(8,128)(2,1)} %bitcast.8), channel_id=1, source_target_pairs={{0,16},{1,17},{2,18},{3,19},{4,20},{5,21},{6,22},{7,23},{8,24},{9,... | collective-permute-start | bytes 786440 | tf_op jit(solution)/shard_map/gather/ppermute | solution.py:148
  5.0 14.1 %collective-permute-start.4 = (bf16[512,256]{1,0:T(8,128)(2,1)}, bf16[512,256]{1,0:T(8,128)(2,1)S(1)}, u32[]{:S(2)}, u32[]{:S(2)}) collective-permute-start(bf16[512,256]{1,0:T(8,128)(2,1)} %bitcast.9), channel_id=1, source_target_pairs={{0,8},{1,9},{2,2},{3,3},{4,12},{5,13},{6,6},{7,7},{8,0},{9,1},{10,... | collective-permute-start | bytes 786440 | tf_op jit(solution)/shard_map/gather/ppermute | solution.py:148
  8.2 12.9 %collective-permute-start.5 = (bf16[512,256]{1,0:T(8,128)(2,1)}, bf16[512,256]{1,0:T(8,128)(2,1)S(1)}, u32[]{:S(2)}, u32[]{:S(2)}) collective-permute-start(bf16[512,256]{1,0:T(8,128)(2,1)} %bitcast.10), channel_id=1, source_target_pairs={{0,2},{1,3},{2,8},{3,9},{4,6},{5,7},{6,12},{7,13},{8,10},{9,11},{1... | collective-permute-start | bytes 786440 | tf_op jit(solution)/shard_map/gather/ppermute | solution.py:148
  8.3 14.4 %collective-permute-start.6 = (bf16[512,256]{1,0:T(8,128)(2,1)}, bf16[512,256]{1,0:T(8,128)(2,1)S(1)}, u32[]{:S(2)}, u32[]{:S(2)}) collective-permute-start(bf16[512,256]{1,0:T(8,128)(2,1)} %bitcast.11), channel_id=1, source_target_pairs={{0,4},{1,0},{2,6},{3,2},{4,5},{5,1},{6,7},{7,3},{8,12},{9,8},{10,1... | collective-permute-start | bytes 786440 | tf_op jit(solution)/shard_map/gather/ppermute | solution.py:148
  13.4 12.4 %collective-permute-start.7 = (bf16[512,256]{1,0:T(8,128)(2,1)S(1)}, bf16[512,256]{1,0:T(8,128)(2,1)S(1)}, u32[]{:S(2)}, u32[]{:S(2)}) collective-permute-start(bf16[512,256]{1,0:T(8,128)(2,1)S(1)} %bitcast.12), channel_id=1, source_target_pairs={{0,0},{1,4},{2,2},{3,6},{4,1},{5,5},{6,3},{7,7},{8,8},{9,12},{10,1... | collective-permute-start | bytes 786440 | tf_op jit(solution)/shard_map/gather/ppermute | solution.py:148
  16.7 11.0 %collective-permute-start.2 = (bf16[512,256]{1,0:T(8,128)(2,1)S(1)}, bf16[512,256]{1,0:T(8,128)(2,1)S(1)}, u32[]{:S(2)}, u32[]{:S(2)}) collective-permute-start(bf16[512,256]{1,0:T(8,128)(2,1)S(1)} %collective-permute-done.1), channel_id=1, source_target_pairs={{0,10},{1,11},{2,0},{3,1},{4,14},{5,15},{6,4},{7,5},{8,2},{9,3},{1... | collective-permute-start | bytes 786440 | tf_op jit(solution)/shard_map/gather/ppermute | solution.py:148
  19.1 8.6 %collective-permute-start.3 = (bf16[512,256]{1,0:T(8,128)(2,1)S(1)}, bf16[512,256]{1,0:T(8,128)(2,1)S(1)}, u32[]{:S(2)}, u32[]{:S(2)}) collective-permute-start(bf16[512,256]{1,0:T(8,128)(2,1)S(1)} %collective-permute-done.1), channel_id=1, source_target_pairs={{0,0},{1,1},{2,10},{3,11},{4,4},{5,5},{6,14},{7,15},{8,8},{9,9},{1... | collective-permute-start | bytes 786440 | tf_op jit(solution)/shard_map/gather/ppermute | solution.py:148
  21.1 7.6 %collective-permute-start.8 = (bf16[512,256]{1,0:T(8,128)(2,1)S(1)}, bf16[512,256]{1,0:T(8,128)(2,1)S(1)}, u32[]{:S(2)}, u32[]{:S(2)}) collective-permute-start(bf16[512,256]{1,0:T(8,128)(2,1)S(1)} %collective-permute-done.swapped), channel_id=1, source_target_pairs={{0,4},{1,0},{2,6},{3,2},{4,5},{5,1},{6,7},{7,3},{8,12},{9,8},{10,1... | collective-permute-start | bytes 786440 | tf_op jit(solution)/shard_map/gather/ppermute | solution.py:148
  22.7 7.9 %collective-permute-start.9 = (bf16[512,256]{1,0:T(8,128)(2,1)S(1)}, bf16[512,256]{1,0:T(8,128)(2,1)S(1)}, u32[]{:S(2)}, u32[]{:S(2)}) collective-permute-start(bf16[512,256]{1,0:T(8,128)(2,1)S(1)} %collective-permute-done.swapped), channel_id=1, source_target_pairs={{0,0},{1,4},{2,2},{3,6},{4,1},{5,5},{6,3},{7,7},{8,8},{9,12},{10,1... | collective-permute-start | bytes 786440 | tf_op jit(solution)/shard_map/gather/ppermute | solution.py:148
  27.7 2.8 %collective-permute-start.12 = (bf16[512,256]{1,0:T(8,128)(2,1)S(1)}, bf16[512,256]{1,0:T(8,128)(2,1)S(1)}, u32[]{:S(2)}, u32[]{:S(2)}) collective-permute-start(bf16[512,256]{1,0:T(8,128)(2,1)S(1)} %collective-permute-done.4.refs_0_.refs_4_), channel_id=1, source_target_pairs={{0,1},{1,0},{2,3},{3,2},{4,5},{5,4},{6,7},{7,6},{8,9},{9,8},{10,11... | collective-permute-start | bytes 786440 | tf_op jit(solution)/shard_map/gather/ppermute | solution.py:148
  28.2 3.7 %collective-permute-start.10 = (bf16[512,256]{1,0:T(8,128)(2,1)S(1)}, bf16[512,256]{1,0:T(8,128)(2,1)S(1)}, u32[]{:S(2)}, u32[]{:S(2)}) collective-permute-start(bf16[512,256]{1,0:T(8,128)(2,1)S(1)} %collective-permute-done.3.refs_2_.refs_0_), channel_id=1, source_target_pairs={{0,1},{1,0},{2,3},{3,2},{4,5},{5,4},{6,7},{7,6},{8,9},{9,8},{10,11... | collective-permute-start | bytes 786440 | tf_op jit(solution)/shard_map/gather/ppermute | solution.py:148
  28.7 3.2 %collective-permute-start.11 = (bf16[512,256]{1,0:T(8,128)(2,1)S(1)}, bf16[512,256]{1,0:T(8,128)(2,1)S(1)}, u32[]{:S(2)}, u32[]{:S(2)}) collective-permute-start(bf16[512,256]{1,0:T(8,128)(2,1)S(1)} %collective-permute-done.2.refs_3_.refs_1_), channel_id=1, source_target_pairs={{0,1},{1,0},{2,3},{3,2},{4,5},{5,4},{6,7},{7,6},{8,9},{9,8},{10,11... | collective-permute-start | bytes 786440 | tf_op jit(solution)/shard_map/gather/ppermute | solution.py:148
  33.4 4.4 %collective-permute-start.15 = (f32[4,64,512]{2,1,0:T(8,128)S(1)}, f32[4,64,512]{2,1,0:T(8,128)S(1)}, u32[]{:S(2)}, u32[]{:S(2)}) collective-permute-start(f32[4,64,512]{2,1,0:T(8,128)S(1)} %get-tuple-element.51), channel_id=1, source_target_pairs={{0,1},{1,0},{2,3},{3,2},{4,5},{5,4},{6,7},{7,6},{8,9},{9,8},{10,11... | collective-permute-start | bytes 1572872 | tf_op jit(solution)/shard_map/ppermute | solution.py:148
  35.5 9.2 %collective-permute-start.14 = (bf16[272,512]{1,0:T(8,128)(2,1)S(1)}, bf16[272,512]{1,0:T(8,128)(2,1)S(1)}, u32[]{:S(2)}, u32[]{:S(2)}) collective-permute-start(bf16[272,512]{1,0:T(8,128)(2,1)S(1)} %get-tuple-element.45.refs_0_), channel_id=1, source_target_pairs={{0,3},{1,7},{2,1},{3,5},{4,2},{5,6},{6,0},{7,4},{8,11},{9,15},{10,... | collective-permute-start | bytes 835592 | tf_op jit(solution)/shard_map/ppermute | solution.py:148
  38.1 10.0 %collective-permute-start.17 = (bf16[80,512]{1,0:T(8,128)(2,1)S(1)}, bf16[80,512]{1,0:T(8,128)(2,1)S(1)}, u32[]{:S(2)}, u32[]{:S(2)}) collective-permute-start(bf16[80,512]{1,0:T(8,128)(2,1)S(1)} %get-tuple-element.53), channel_id=1, source_target_pairs={{0,28},{1,24},{2,30},{3,26},{4,29},{5,25},{6,31},{7,27},{8,20},{9,... | collective-permute-start | bytes 245768 | tf_op jit(solution)/shard_map/ppermute | solution.py:148
  40.6 8.5 %collective-permute-start.18 = (bf16[80,512]{1,0:T(8,128)(2,1)S(1)}, bf16[80,512]{1,0:T(8,128)(2,1)S(1)}, u32[]{:S(2)}, u32[]{:S(2)}) collective-permute-start(bf16[80,512]{1,0:T(8,128)(2,1)S(1)} %get-tuple-element.54), channel_id=1, source_target_pairs={{0,20},{1,16},{2,22},{3,18},{4,21},{5,17},{6,23},{7,19},{8,28},{9,... | collective-permute-start | bytes 245768 | tf_op jit(solution)/shard_map/ppermute | solution.py:148
  40.6 8.5 %collective-permute-start.19 = (bf16[80,512]{1,0:T(8,128)(2,1)S(1)}, bf16[80,512]{1,0:T(8,128)(2,1)S(1)}, u32[]{:S(2)}, u32[]{:S(2)}) collective-permute-start(bf16[80,512]{1,0:T(8,128)(2,1)S(1)} %get-tuple-element.55), channel_id=1, source_target_pairs={{0,12},{1,8},{2,14},{3,10},{4,13},{5,9},{6,15},{7,11},{8,4},{9,0},... | collective-permute-start | bytes 245768 | tf_op jit(solution)/shard_map/ppermute | solution.py:148
  42.4 6.7 %collective-permute-start.20 = (bf16[80,512]{1,0:T(8,128)(2,1)S(1)}, bf16[80,512]{1,0:T(8,128)(2,1)S(1)}, u32[]{:S(2)}, u32[]{:S(2)}) collective-permute-start(bf16[80,512]{1,0:T(8,128)(2,1)S(1)} %get-tuple-element.52.refs_0_), channel_id=1, source_target_pairs={{0,4},{1,0},{2,6},{3,2},{4,5},{5,1},{6,7},{7,3},{8,12},{9,8},{10,1... | collective-permute-start | bytes 245768 | tf_op jit(solution)/shard_map/ppermute | solution.py:148
  44.7 10.5 %collective-permute-start.16 = (bf16[272,512]{1,0:T(8,128)(2,1)S(1)}, bf16[272,512]{1,0:T(8,128)(2,1)S(1)}, u32[]{:S(2)}, u32[]{:S(2)}) collective-permute-start(bf16[272,512]{1,0:T(8,128)(2,1)S(1)} %gamma_block.3.refs_0_), channel_id=1, source_target_pairs={{0,2},{1,6},{2,0},{3,4},{4,3},{5,7},{6,1},{7,5},{8,10},{9,14},{10,... | collective-permute-start | bytes 835592 | tf_op jit(solution)/shard_map/ppermute | solution.py:148
  48.2 9.8 %collective-permute-start.21 = (bf16[272,512]{1,0:T(8,128)(2,1)S(1)}, bf16[272,512]{1,0:T(8,128)(2,1)S(1)}, u32[]{:S(2)}, u32[]{:S(2)}) collective-permute-start(bf16[272,512]{1,0:T(8,128)(2,1)S(1)} %gamma_block.4.refs_0_), channel_id=1, source_target_pairs={{0,1},{1,5},{2,3},{3,7},{4,0},{5,4},{6,2},{7,6},{8,9},{9,13},{10,1... | collective-permute-start | bytes 835592 | tf_op jit(solution)/shard_map/ppermute | solution.py:148
  50.8 8.3 %collective-permute-start.22 = (bf16[272,512]{1,0:T(8,128)(2,1)S(1)}, bf16[272,512]{1,0:T(8,128)(2,1)S(1)}, u32[]{:S(2)}, u32[]{:S(2)}) collective-permute-start(bf16[272,512]{1,0:T(8,128)(2,1)S(1)} %gamma_block.5.refs_0_), channel_id=1, source_target_pairs={{0,0},{1,4},{2,2},{3,6},{4,1},{5,5},{6,3},{7,7},{8,8},{9,12},{10,1... | collective-permute-start | bytes 835592 | tf_op jit(solution)/shard_map/ppermute | solution.py:148
  54.4 3.4 %collective-permute-start.23 = (bf16[80,512]{1,0:T(8,128)(2,1)S(1)}, bf16[80,512]{1,0:T(8,128)(2,1)S(1)}, u32[]{:S(2)}, u32[]{:S(2)}) collective-permute-start(bf16[80,512]{1,0:T(8,128)(2,1)S(1)} %density_rows.1.refs_0_.refs_1_.far), channel_id=1, source_target_pairs={{0,2},{1,3},{2,0},{3,1},{4,6},{5,7},{6,4},{7,5},{8,10},{9,11},{10,... | collective-permute-start | bytes 245768 | tf_op jit(solution)/shard_map/ppermute | solution.py:148
  57.9 2.5 %collective-permute-start.24 = (f32[64,512]{1,0:T(8,128)S(1)}, f32[64,512]{1,0:T(8,128)S(1)}, u32[]{:S(2)}, u32[]{:S(2)}) collective-permute-start(f32[64,512]{1,0:T(8,128)S(1)} %density_block.1.refs_0_.block), channel_id=1, source_target_pairs={{0,1},{1,0},{2,3},{3,2},{4,5},{5,4},{6,7},{7,6},{8,9},{9,8},{10,11... | collective-permute-start | bytes 393224 | tf_op jit(solution)/shard_map/ppermute | solution.py:148
  (5 other events, 40.3 us)
